TPU v7x, 128 devices: a whole 4x4x4 slice. The times are simulated.
128 devices in a mesh: seq: 8 (over z, core), ch: 16 (over y, x).
Axes of the slice: x: 4, y: 4, z: 4, core: 2. Of those that a mesh axis runs over, the one named last changes fastest.
Arguments:
- key_branch: bfloat16 [4096, 4096], P('seq', 'ch'), may hold values from -6 to 6
- value_branch: bfloat16 [4096, 4096], P('seq', 'ch'), may hold values from -6 to 6
- gate_branch: bfloat16 [4096, 4096], P('seq', 'ch'), may hold values from -6 to 6
- conv_filter: bfloat16 [4096, 4096], P('seq', 'ch'), may hold values from -0.5 to 0.5, as said below
- skip_gain: float32 [4096], P('ch'), may hold values from -4 to 4
Outputs:
- output: bfloat16 [4096, 4096], P('seq', 'ch')
Inputs may be any that keep to these rules, and one draw needn't show every extreme that they name: `conv_filter`: one filter value per position and channel.
All inputs are finite; a program needn't handle non-finite values.
Results may differ from a plain program's by a relative error of at most 0.0049.
Values may be sent and summed in bfloat16 or wider, within the bound.
No kernel may reach another device: no remote copies, remote signals or barrier semaphores. Data moves between devices by JAX's collectives and lax.ppermute only.
A program may use at most 128 MiB of HBM per device.

v0:
```python
import jax
import jax.numpy as jnp
from jax import lax
from jax.experimental import pallas as pl
from jax.experimental.pallas import tpu as pltpu
from jax.sharding import PartitionSpec as P

F32 = jnp.float32
BF16 = jnp.bfloat16
PARTS = 8
CH = 32
VMEM = 48 * 1024 * 1024


def product_of(k, v):
    return (k.astype(F32) * v.astype(F32)).astype(BF16)


def pack_kernel(k_ref, v_ref, f_ref, o_ref):
    p = product_of(k_ref[...], v_ref[...]).astype(F32)
    p = p.reshape(2, 16, 16, 256).transpose(1, 0, 2, 3).reshape(512, 256)
    f = f_ref[...].astype(F32)
    for half in range(2):
        for q in range(4):
            for at, x in ((0, p), (4, f)):
                block = x[128 * q : 128 * q + 128, 128 * half : 128 * half + 128]
                block = block.T.astype(BF16).reshape(4, CH, 128)
                o_ref[4 * half : 4 * half + 4, at + q] = block


def conv_kernel(r_ref, y_ref, g_s, v_s, vv_s, gl_s, a_s, b_s, o_s, y_s):
    lane = lax.broadcasted_iota(jnp.int32, (16, 128), 1)
    row16 = lax.broadcasted_iota(jnp.int32, (16, 128), 0)
    g_s[0:CH] = jnp.zeros((CH, 128), F32)
    for s in range(PARTS):
        for q in range(4):
            g = 4 * s + q + 1
            g_s[CH * g : CH * g + CH] = r_ref[s, 4 + q].astype(F32)
    lane32 = lax.broadcasted_iota(jnp.int32, (CH, 128), 1)
    for x0h in range(4):
        pieces = [r_ref[s, x0h].astype(F32) for s in range(PARTS)]
        for x0l in range(4):
            x0 = 4 * x0h + x0l
            for tile in range(2):
                out = None
                for i in range(4):
                    piece = pieces[4 * tile + i]
                    shift = (32 * i - 32 * x0l) % 128
                    if shift:
                        piece = pltpu.roll(piece, shift, 1)
                    out = piece if out is None else jnp.where(lane32 >= 32 * i, piece, out)
                v_s[tile, CH * x0 : CH * x0 + CH] = out

    def gather(c, carry):
        for tile in range(2):
            vv_s[pl.ds(pl.multiple_of(16 * c, 16), 16), 128 * tile : 128 * tile + 128] = v_s[
                tile, pl.ds(c, 16, stride=CH), :
            ].astype(BF16)
        rows = [g_s[pl.ds(CH * j + c, 16, stride=2 * CH), :].astype(BF16) for j in range(3)]
        for half in range(2):
            at = pl.multiple_of(32 * c + 16 * half, 16)
            gl_s[pl.ds(at, 16), 0:128] = rows[half]
            gl_s[pl.ds(at, 16), 128:256] = rows[half + 1]
        return carry

    lax.fori_loop(0, CH, gather, 0)

    wide_row = lax.broadcasted_iota(jnp.int32, (256, 256), 0)
    wide_col = lax.broadcasted_iota(jnp.int32, (256, 256), 1)

    def expand_a(x1, carry):
        hit = (wide_row % 16 == wide_col // 16) & (wide_row // 16 + wide_col % 16 == x1)
        table = jnp.where(hit, 1.0, 0.0).astype(BF16)
        out = jnp.dot(vv_s[...], table, preferred_element_type=F32).astype(BF16)
        a_s[:, pl.ds(pl.multiple_of(16 * x1, 16), 16), :] = out.reshape(CH, 16, 256)
        return carry

    lax.fori_loop(0, 16, expand_a, 0)

    def expand_b(i, carry):
        hit = wide_row == 128 + wide_col % 128 - (2 * i + wide_col // 128)
        table = jnp.where(hit, 1.0, 0.0).astype(BF16)
        out = jnp.dot(gl_s[...], table, preferred_element_type=F32).astype(BF16)
        out = out.reshape(CH, 2, 16, 256)
        for j in range(2):
            at = pl.multiple_of(32 * i + 16 * j, 16)
            for half in range(2):
                b_s[:, pl.ds(at, 16), 128 * half : 128 * half + 128] = out[
                    :, half, :, 128 * j : 128 * j + 128
                ]
        return carry

    lax.fori_loop(0, 8, expand_b, 0)

    def convolve(c, carry):
        out = jnp.dot(a_s[c], b_s[c], preferred_element_type=F32)
        o_s[0] = out[:, :128]
        o_s[1] = out[:, 128:]
        acc = [jnp.zeros((16, 128), F32) for _ in range(4)]
        for x0 in range(16):
            r0 = o_s[0, pl.ds(x0, 16, stride=16), :]
            r1 = o_s[1, pl.ds(x0, 16, stride=16), :]
            shift, t = 16 * (x0 % 8), x0 // 8
            if shift:
                r0 = pltpu.roll(r0, shift, 1)
                r1 = pltpu.roll(r1, shift, 1)
                low = lane < shift
                acc[t] = acc[t] + jnp.where(low, 0.0, r0)
                acc[t + 1] = acc[t + 1] + jnp.where(low, r0, r1)
                acc[t + 2] = acc[t + 2] + jnp.where(low, r1, 0.0)
            else:
                acc[t] = acc[t] + r0
                acc[t + 1] = acc[t + 1] + r1
        for half in range(2):
            late = jnp.where(row16 == 0, 0.0, pltpu.roll(acc[2 + half], 1, 0))
            y_s[pl.ds(CH * half + c, 16, stride=2 * CH), :] = acc[half] + late
        return carry

    lax.fori_loop(0, CH, convolve, 0)
    for s in range(PARTS):
        for q in range(4):
            g = 4 * s + q
            y_ref[s, q] = y_s[CH * g : CH * g + CH].astype(BF16)


def gate_kernel(y_ref, k_ref, v_ref, g_ref, s_ref, o_ref):
    for half in range(2):
        ch = slice(128 * half, 128 * half + 128)
        for q in range(4):
            pos = slice(128 * q, 128 * q + 128)
            y = y_ref[4 * half : 4 * half + 4, q].reshape(128, 128).astype(F32).T
            p = product_of(k_ref[pos, ch], v_ref[pos, ch]).astype(F32)
            out = g_ref[pos, ch].astype(F32) * (y + s_ref[:, ch] * p)
            o_ref[pos, ch] = out.astype(BF16)


def call(kernel, shape, scratch=(), flops=0):
    return pl.pallas_call(
        kernel,
        out_shape=jax.ShapeDtypeStruct(shape, BF16),
        scratch_shapes=scratch,
        compiler_params=pltpu.CompilerParams(vmem_limit_bytes=VMEM),
    )


def exchange(x):
    return lax.all_to_all(x, "seq", split_axis=0, concat_axis=0, tiled=True)


def on_device(key_branch, value_branch, gate_branch, conv_filter, skip_gain):
    sent = call(pack_kernel, (PARTS, 8, CH, 128))(key_branch, value_branch, conv_filter)
    got = exchange(sent)
    mixed = call(
        conv_kernel,
        (PARTS, 4, CH, 128),
        [
            pltpu.VMEM((33 * CH, 128), F32),
            pltpu.VMEM((2, 16 * CH, 128), F32),
            pltpu.VMEM((16 * CH, 256), BF16),
            pltpu.VMEM((32 * CH, 256), BF16),
            pltpu.VMEM((CH, 256, 256), BF16),
            pltpu.VMEM((CH, 256, 256), BF16),
            pltpu.VMEM((2, 256, 128), F32),
            pltpu.VMEM((32 * CH, 128), F32),
        ],
    )(got)
    back = exchange(mixed)
    return call(gate_kernel, (512, 256))(
        back, key_branch, value_branch, gate_branch, skip_gain.reshape(1, 256)
    )


def solution(mesh):
    in_specs = (P("seq", "ch"), P("seq", "ch"), P("seq", "ch"), P("seq", "ch"), P("ch"))
    return jax.shard_map(
        on_device, mesh=mesh, in_specs=in_specs, out_specs=P("seq", "ch"), check_vma=False
    )
```

profile of v0, /device:TPU:0, one launch (start us, length us, event | category | flops | bytes accessed | tf_op | source)
XLA Modules:
  0.0 49.6 jit_solution(3496753826600861600)
XLA Ops:
  0.0 0.0 copy-start
  0.0 0.9 %copy-done = bf16[512,256]{1,0:T(8,128)(2,1)S(1)} copy-done((bf16[512,256]{1,0:T(8,128)(2,1)S(1)}, bf16[512,256]{1,0:T(8,128)(2,1)}, u32[]{:S(2)}) %copy-start) | copy-done | bytes 262168
  1.0 0.0 copy-start.2
  1.0 0.9 %copy-done.2 = bf16[512,256]{1,0:T(8,128)(2,1)S(1)} copy-done((bf16[512,256]{1,0:T(8,128)(2,1)S(1)}, bf16[512,256]{1,0:T(8,128)(2,1)}, u32[]{:S(2)}) %copy-start.2) | copy-done | bytes 262168
  1.9 0.0 copy-start.4
  1.9 0.9 %copy-done.4 = bf16[512,256]{1,0:T(8,128)(2,1)S(1)} copy-done((bf16[512,256]{1,0:T(8,128)(2,1)S(1)}, bf16[512,256]{1,0:T(8,128)(2,1)}, u32[]{:S(2)}) %copy-start.4) | copy-done | bytes 262168
  2.9 0.2 shard_map.55
  3.1 15.6 %all_to_all.10.r_ref = bf16[8,8,32,128]{3,2,1,0:T(8,128)(2,1)S(1)} all-to-all(bf16[8,8,32,128]{3,2,1,0:T(8,128)(2,1)S(1)} %shard_map.55), channel_id=1, replica_groups=mesh['seq'=8,'ch'=16] {'seq'}, dimensions={0} | all-to-all | bytes 1048576 | tf_op jit(solution)/shard_map/all_to_all | solution.py:147
  18.7 0.0 copy-start.5
  18.7 19.3 %shard_map.56 = bf16[8,4,32,128]{3,2,1,0:T(8,128)(2,1)S(1)} custom-call(bf16[8,8,32,128]{3,2,1,0:T(8,128)(2,1)S(1)} %all_to_all.10.r_ref), custom_call_target="tpu_custom_call" | custom-call | tf_op jit(solution)/shard_map/pallas_call | solution.py:153
  37.9 0.0 copy-start.1
  38.0 0.0 copy-start.3
  38.0 10.1 %all_to_all.11.y_ref = bf16[8,4,32,128]{3,2,1,0:T(8,128)(2,1)S(1)} all-to-all(bf16[8,4,32,128]{3,2,1,0:T(8,128)(2,1)S(1)} %shard_map.56), channel_id=1, replica_groups=mesh['seq'=8,'ch'=16] {'seq'}, dimensions={0} | all-to-all | bytes 524288 | tf_op jit(solution)/shard_map/all_to_all | solution.py:147
  48.0 0.0 copy-start.6
  48.1 0.0 copy-done.5
  48.1 0.0 copy-done.1
  48.1 0.0 copy-done.3
  48.1 0.7 %copy-done.6 = f32[256]{0:T(256)S(1)} copy-done((f32[256]{0:T(256)S(1)}, f32[256]{0:T(256)}, u32[]{:S(2)}) %copy-start.6) | copy-done | bytes 1048
  48.7 0.9 %shard_map.57 = bf16[512,256]{1,0:T(8,128)(2,1)} custom-call(bf16[8,4,32,128]{3,2,1,0:T(8,128)(2,1)S(1)} %all_to_all.11.y_ref, bf16[512,256]{1,0:T(8,128)(2,1)S(1)} %copy-done.1, bf16[512,256]{1,0:T(8,128)(2,1)S(1)} %copy-done.3, bf16[512,256]{1,0:T(8,128)(2,1)S(1)} %copy-done.5, f32[1,256]{1,0:T(1,128)S(1)} %bitcast.1), custom_call_target="tpu_custom_call" | custom-call | tf_op jit(solution)/shard_map/pallas_call | solution.py:168
Async XLA Ops:
  0.0 0.9 %copy-start = (bf16[512,256]{1,0:T(8,128)(2,1)S(1)}, bf16[512,256]{1,0:T(8,128)(2,1)}, u32[]{:S(2)}) copy-start(bf16[512,256]{1,0:T(8,128)(2,1)} %k_ref.3) | copy-start | bytes 786436
  1.0 0.9 %copy-start.2 = (bf16[512,256]{1,0:T(8,128)(2,1)S(1)}, bf16[512,256]{1,0:T(8,128)(2,1)}, u32[]{:S(2)}) copy-start(bf16[512,256]{1,0:T(8,128)(2,1)} %v_ref.3) | copy-start | bytes 786436
  1.9 0.9 %copy-start.4 = (bf16[512,256]{1,0:T(8,128)(2,1)S(1)}, bf16[512,256]{1,0:T(8,128)(2,1)}, u32[]{:S(2)}) copy-start(bf16[512,256]{1,0:T(8,128)(2,1)} %f_ref.1) | copy-start | bytes 786436
  18.7 29.4 %copy-start.5 = (bf16[512,256]{1,0:T(8,128)(2,1)S(1)}, bf16[512,256]{1,0:T(8,128)(2,1)}, u32[]{:S(2)}) copy-start(bf16[512,256]{1,0:T(8,128)(2,1)} %g_ref.1) | copy-start | bytes 786436
  37.9 10.1 %copy-start.1 = (bf16[512,256]{1,0:T(8,128)(2,1)S(1)}, bf16[512,256]{1,0:T(8,128)(2,1)}, u32[]{:S(2)}) copy-start(bf16[512,256]{1,0:T(8,128)(2,1)} %k_ref.3) | copy-start | bytes 786436
  38.0 10.1 %copy-start.3 = (bf16[512,256]{1,0:T(8,128)(2,1)S(1)}, bf16[512,256]{1,0:T(8,128)(2,1)}, u32[]{:S(2)}) copy-start(bf16[512,256]{1,0:T(8,128)(2,1)} %v_ref.3) | copy-start | bytes 786436
  48.0 0.7 %copy-start.6 = (f32[256]{0:T(256)S(1)}, f32[256]{0:T(256)}, u32[]{:S(2)}) copy-start(f32[256]{0:T(256)} %param.9) | copy-start | bytes 3076
where the time goes:
time: 50.3 us; the launch traced here: 49.6 us
  blocking collectives  25.7 us (51%)
  Pallas kernels  20.4 us (41%)
  local copies, waits for them, and re-layouts  3.53 us (7%)
    all_to_all x2, blocking collectives, exchange(): return lax.all_to_all(x, 'seq', split_axis=0, concat_axis=0, tiled=True)  25.7 us
    pallas_call x1, Pallas kernels, on_device(): call(conv_kernel, (PARTS, 4, CH, 128), [pltpu.VMEM((33 * CH, 128), F32),...  19.3 us
    unnamed x14, local copies, waits for them, and re-layouts  3.53 us

commit v1 on v0

v1 whole, which is shorter than its diff:
```python
import jax
import jax.numpy as jnp
from jax import lax
from jax.experimental import pallas as pl
from jax.experimental.pallas import tpu as pltpu
from jax.sharding import PartitionSpec as P

F32 = jnp.float32
BF16 = jnp.bfloat16
PARTS = 8
CH = 32
AT_ONCE = 4
VMEM = 48 * 1024 * 1024


def product_of(k, v):
    return (k.astype(F32) * v.astype(F32)).astype(BF16)


def pack_kernel(p_ref, f_ref, o_ref):
    p = p_ref[...].astype(F32)
    p = p.reshape(4, 8, 16, 256)
    p = jnp.stack([p[3 - a] for a in range(4)], 1).reshape(512, 256)
    f = f_ref[...].astype(F32)
    for half in range(2):
        for q in range(4):
            for at, x in ((0, p), (4, f)):
                block = x[128 * q : 128 * q + 128, 128 * half : 128 * half + 128]
                block = block.T.astype(BF16).reshape(4, CH, 128)
                o_ref[4 * half : 4 * half + 4, at + q] = block


def conv_kernel(r_ref, s_ref, y_ref, so_ref, g_s, v_s, a_s, b_s, o_s, y_s):
    so_ref[...] = s_ref[...]
    lane = lax.broadcasted_iota(jnp.int32, (32, 128), 1)
    row = lax.broadcasted_iota(jnp.int32, (32, 128), 0)
    for s in range(PARTS):
        for q in range(4):
            g = 4 * s + q
            g_s[CH * g : CH * g + CH] = r_ref[s, 4 + q].astype(F32)
    for q in range(4):
        for j in range(4):
            first, second = [r_ref[s, q].astype(F32) for s in (2 * j + 1, 2 * j)]
            at = 2 * CH * q
            v_s[j, at : at + CH] = jnp.where(lane < 64, first, pltpu.roll(second, 64, 1))
            v_s[j, at + CH : at + 2 * CH] = jnp.where(lane < 64, pltpu.roll(first, 64, 1), second)
    stay_a = lane[:8] < 16 + 16 * row[:8]
    stay_b = lane[:16] >= row[:16]
    zero = jnp.zeros((8, 128), F32)

    def pair(a, b):
        return jnp.concatenate([a, b], 0).astype(BF16)

    def build(c, u):
        prev = jnp.zeros((16, 128), F32)
        for g in range(32):
            taps = jnp.broadcast_to(g_s[pl.ds(CH * g + c, 1), :], (16, 128))
            rot = pltpu.roll(taps, 0, 1, stride=1, stride_axis=0)
            at, half = 16 * (g % 16), 128 * (g // 16)
            b_s[u, at : at + 16, half : half + 128] = jnp.where(stay_b, rot, prev).astype(BF16)
            prev = rot
        for b in range(8):
            prev, w = zero, []
            for j in range(4):
                vals = jnp.broadcast_to(v_s[j, pl.ds(CH * b + c, 1), :], (8, 128))
                rot = pltpu.roll(vals, 16, 1, stride=16, stride_axis=0)
                w.append(jnp.where(stay_a, rot, prev))
                prev = rot
            lo, hi = slice(16 * b, 16 * b + 16), slice(128 + 16 * b, 144 + 16 * b)
            a_s[u, lo, :128] = pair(w[0], w[1])
            a_s[u, lo, 128:] = pair(zero, w[0])
            a_s[u, hi, :128] = pair(w[2], w[3])
            a_s[u, hi, 128:] = pair(w[1], w[2])

    def multiply(u):
        o_s[u] = jnp.dot(a_s[u], b_s[u], preferred_element_type=F32)

    def collect(c, u):
        here = jnp.zeros((32, 128), F32)
        late = jnp.zeros((32, 128), F32)
        for b in range(8):
            lo, hi = slice(16 * b, 16 * b + 16), slice(128 + 16 * b, 144 + 16 * b)
            r = jnp.concatenate([o_s[u, lo, :128], o_s[u, hi, :128] + o_s[u, lo, 128:]], 0)
            if b:
                r = pltpu.roll(r, 16 * b, 1)
                over = lane < 16 * b
                late = late + jnp.where(over, r, 0.0)
                r = jnp.where(over, 0.0, r)
            here = here + r
        late = jnp.where(row == 0, 0.0, pltpu.roll(late, 1, 0))
        y_s[pl.ds(c, 32, stride=CH), :] = here + late

    for u in range(AT_ONCE):
        build(u, u)
    for u in range(AT_ONCE):
        multiply(u)
    for u in range(AT_ONCE):
        build(AT_ONCE + u, u)

    def step(i, carry):
        for u in range(AT_ONCE):
            collect((i - 1) * AT_ONCE + u, u)
            multiply(u)
            build(jnp.minimum((i + 1) * AT_ONCE, CH - AT_ONCE) + u, u)
        return carry

    lax.fori_loop(1, CH // AT_ONCE, step, 0)
    for u in range(AT_ONCE):
        collect(CH - AT_ONCE + u, u)
    for s in range(PARTS):
        for q in range(4):
            g = 4 * s + q
            y_ref[s, q] = y_s[CH * g : CH * g + CH].astype(BF16)


def gate_kernel(y_ref, k_ref, v_ref, g_ref, s_ref, o_ref):
    for half in range(2):
        ch = slice(128 * half, 128 * half + 128)
        for q in range(4):
            pos = slice(128 * q, 128 * q + 128)
            y = y_ref[4 * half : 4 * half + 4, q].reshape(128, 128).astype(F32).T
            p = product_of(k_ref[pos, ch], v_ref[pos, ch]).astype(F32)
            out = g_ref[pos, ch].astype(F32) * (y + s_ref[:, ch] * p)
            o_ref[pos, ch] = out.astype(BF16)


def call(kernel, out, scratch=(), limit=VMEM, **more):
    return pl.pallas_call(
        kernel,
        out_shape=out,
        scratch_shapes=scratch,
        compiler_params=pltpu.CompilerParams(vmem_limit_bytes=limit),
        **more,
    )


def exchange(x):
    return lax.all_to_all(x, "seq", split_axis=0, concat_axis=0, tiled=True)


def on_device(key_branch, value_branch, gate_branch, conv_filter, skip_gain):
    skip_gain = skip_gain.reshape(1, 256)
    sent = call(pack_kernel, jax.ShapeDtypeStruct((PARTS, 8, CH, 128), BF16))(
        product_of(key_branch, value_branch), conv_filter
    )
    got = exchange(sent)
    mixed, skip_gain = call(
        conv_kernel,
        [jax.ShapeDtypeStruct((PARTS, 4, CH, 128), BF16), jax.ShapeDtypeStruct((1, 256), F32)],
        [
            pltpu.VMEM((32 * CH, 128), F32),
            pltpu.VMEM((4, 8 * CH, 128), F32),
            pltpu.VMEM((AT_ONCE, 256, 256), BF16),
            pltpu.VMEM((AT_ONCE, 256, 256), BF16),
            pltpu.VMEM((AT_ONCE, 256, 256), F32),
            pltpu.VMEM((32 * CH, 128), F32),
        ],
    )(got, skip_gain)
    back = exchange(mixed)
    return call(gate_kernel, jax.ShapeDtypeStruct((512, 256), BF16))(
        back, key_branch, value_branch, gate_branch, skip_gain
    )


def solution(mesh):
    in_specs = (P("seq", "ch"), P("seq", "ch"), P("seq", "ch"), P("seq", "ch"), P("ch"))
    return jax.shard_map(
        on_device, mesh=mesh, in_specs=in_specs, out_specs=P("seq", "ch"), check_vma=False
    )
```

time: 50.3 us -> 33.5 us (0.67)
  Pallas kernels: 20.4 us -> 5.35 us
  local copies, waits for them, and re-layouts: 3.53 us -> 0.7 us
  other arithmetic: 0 us -> 1.14 us
    pallas_call x3, Pallas kernels: 20.4 us -> 5.35 us  [the longest x1 4.23 us: on_device(): call(conv_kernel, [jax.ShapeDtypeStruct((PARTS, 4, CH, 128), BF16), jax.S...]
    unnamed x14 -> x10, local copies, waits for them, and re-layouts: 3.53 us -> 0.7 us
    convert_element_type x0 -> x1, other arithmetic: none -> 1.14 us  [product_of(): return (k.astype(F32) * v.astype(F32)).astype(BF16)]
where the time goes in v1:
time: 33.5 us; the launch traced here: 32.9 us
  blocking collectives  25.7 us (77%)
  Pallas kernels  5.35 us (16%)
  other arithmetic  1.14 us (3%)
  local copies, waits for them, and re-layouts  0.7 us (2%)
    all_to_all x2, blocking collectives, exchange(): return lax.all_to_all(x, 'seq', split_axis=0, concat_axis=0, tiled=True)  25.7 us
    pallas_call x1, Pallas kernels, on_device(): call(conv_kernel, [jax.ShapeDtypeStruct((PARTS, 4, CH, 128), BF16), jax.S...  4.23 us
    convert_element_type x1, other arithmetic, product_of(): return (k.astype(F32) * v.astype(F32)).astype(BF16)  1.14 us
    pallas_call x1, Pallas kernels, on_device(): call(gate_kernel, jax.ShapeDtypeStruct((512, 256), BF16))  0.9 us
    unnamed x10, local copies, waits for them, and re-layouts  0.7 us

profile of v1, /device:TPU:0, one launch (start us, length us, event | category | flops | bytes accessed | tf_op | source)
XLA Modules:
  0.0 32.9 jit_solution(12811515468380352899)
XLA Ops:
  0.0 0.0 copy-start.2
  0.0 1.1 %multiply_convert_fusion.p_ref = bf16[512,256]{1,0:T(8,128)(2,1)S(1)} fusion(bf16[512,256]{1,0:T(8,128)(2,1)} %v_ref.1, bf16[512,256]{1,0:T(8,128)(2,1)} %k_ref.1), kind=kLoop, calls=%fused_computation | loop fusion | flops 524288 | bytes 786432 | tf_op jit(solution)/shard_map/convert_element_type | solution.py:17
  1.1 0.0 copy-done.2
  1.1 0.2 shard_map.55
  1.4 15.6 %all_to_all.10.r_ref = bf16[8,8,32,128]{3,2,1,0:T(8,128)(2,1)S(1)} all-to-all(bf16[8,8,32,128]{3,2,1,0:T(8,128)(2,1)S(1)} %shard_map.55), channel_id=1, replica_groups=mesh['seq'=8,'ch'=16] {'seq'}, dimensions={0} | all-to-all | bytes 1048576 | tf_op jit(solution)/shard_map/all_to_all | solution.py:138
  17.0 0.0 copy-start.4
  17.0 0.7 %copy-done.4 = f32[256]{0:T(256)S(1)} copy-done((f32[256]{0:T(256)S(1)}, f32[256]{0:T(256)}, u32[]{:S(2)}) %copy-start.4) | copy-done | bytes 1048
  17.6 0.0 copy-start.3
  17.6 4.2 %shard_map.56 = (bf16[8,4,32,128]{3,2,1,0:T(8,128)(2,1)S(1)}, f32[1,256]{1,0:T(1,128)S(1)}) custom-call(bf16[8,8,32,128]{3,2,1,0:T(8,128)(2,1)S(1)} %all_to_all.10.r_ref, f32[1,256]{1,0:T(1,128)S(1)} %bitcast.1), custom_call_target="tpu_custom_call" | custom-call | tf_op jit(solution)/shard_map/pallas_call | solution.py:147
  21.9 0.0 copy-start
  21.9 0.0 copy-start.1
  21.9 10.1 %all_to_all.11.y_ref = bf16[8,4,32,128]{3,2,1,0:T(8,128)(2,1)S(1)} all-to-all(bf16[8,4,32,128]{3,2,1,0:T(8,128)(2,1)S(1)} %get-tuple-element.7), channel_id=1, replica_groups=mesh['seq'=8,'ch'=16] {'seq'}, dimensions={0} | all-to-all | bytes 524288 | tf_op jit(solution)/shard_map/all_to_all | solution.py:138
  32.0 0.0 copy-done.3
  32.0 0.0 copy-done
  32.0 0.0 copy-done.1
  32.0 0.9 %shard_map.57 = bf16[512,256]{1,0:T(8,128)(2,1)} custom-call(bf16[8,4,32,128]{3,2,1,0:T(8,128)(2,1)S(1)} %all_to_all.11.y_ref, bf16[512,256]{1,0:T(8,128)(2,1)S(1)} %copy-done.1, bf16[512,256]{1,0:T(8,128)(2,1)S(1)} %copy-done, bf16[512,256]{1,0:T(8,128)(2,1)S(1)} %copy-done.3, f32[1,256]{1,0:T(1,128)S(1)} %get-tuple-element.8.s_ref), custom_call_target="tpu_custom_call" | custom-call | tf_op jit(solution)/shard_map/pallas_call | solution.py:160
Async XLA Ops:
  0.0 1.1 %copy-start.2 = (bf16[512,256]{1,0:T(8,128)(2,1)S(1)}, bf16[512,256]{1,0:T(8,128)(2,1)}, u32[]{:S(2)}) copy-start(bf16[512,256]{1,0:T(8,128)(2,1)} %f_ref.1) | copy-start | bytes 786436
  17.0 0.7 %copy-start.4 = (f32[256]{0:T(256)S(1)}, f32[256]{0:T(256)}, u32[]{:S(2)}) copy-start(f32[256]{0:T(256)} %param.9) | copy-start | bytes 3076
  17.6 14.3 %copy-start.3 = (bf16[512,256]{1,0:T(8,128)(2,1)S(1)}, bf16[512,256]{1,0:T(8,128)(2,1)}, u32[]{:S(2)}) copy-start(bf16[512,256]{1,0:T(8,128)(2,1)} %g_ref.1) | copy-start | bytes 786436
  21.9 10.1 %copy-start = (bf16[512,256]{1,0:T(8,128)(2,1)S(1)}, bf16[512,256]{1,0:T(8,128)(2,1)}, u32[]{:S(2)}) copy-start(bf16[512,256]{1,0:T(8,128)(2,1)} %v_ref.1) | copy-start | bytes 786436
  21.9 10.1 %copy-start.1 = (bf16[512,256]{1,0:T(8,128)(2,1)S(1)}, bf16[512,256]{1,0:T(8,128)(2,1)}, u32[]{:S(2)}) copy-start(bf16[512,256]{1,0:T(8,128)(2,1)} %k_ref.1) | copy-start | bytes 786436

commit v2 on v1

--- a/solution.py
+++ b/solution.py
@@ -9,7 +9,8 @@
 BF16 = jnp.bfloat16
 PARTS = 8
 CH = 32
-AT_ONCE = 4
+AT_ONCE = 8
+PITCH = 40
 VMEM = 48 * 1024 * 1024
 
 
@@ -30,8 +31,7 @@
                 o_ref[4 * half : 4 * half + 4, at + q] = block
 
 
-def conv_kernel(r_ref, s_ref, y_ref, so_ref, g_s, v_s, a_s, b_s, o_s, y_s):
-    so_ref[...] = s_ref[...]
+def conv_kernel(r_ref, y_ref, g_s, v_s, a_s, b_s, o_s, y_s):
     lane = lax.broadcasted_iota(jnp.int32, (32, 128), 1)
     row = lax.broadcasted_iota(jnp.int32, (32, 128), 0)
     for s in range(PARTS):
@@ -41,9 +41,10 @@
     for q in range(4):
         for j in range(4):
             first, second = [r_ref[s, q].astype(F32) for s in (2 * j + 1, 2 * j)]
+            swapped = pltpu.roll(jnp.where(lane < 64, second, first), 64, 1)
             at = 2 * CH * q
-            v_s[j, at : at + CH] = jnp.where(lane < 64, first, pltpu.roll(second, 64, 1))
-            v_s[j, at + CH : at + 2 * CH] = jnp.where(lane < 64, pltpu.roll(first, 64, 1), second)
+            v_s[j, at : at + CH] = jnp.where(lane < 64, first, swapped)
+            v_s[j, at + CH : at + 2 * CH] = jnp.where(lane < 64, swapped, second)
     stay_a = lane[:8] < 16 + 16 * row[:8]
     stay_b = lane[:16] >= row[:16]
     zero = jnp.zeros((8, 128), F32)
@@ -88,7 +89,7 @@
                 r = jnp.where(over, 0.0, r)
             here = here + r
         late = jnp.where(row == 0, 0.0, pltpu.roll(late, 1, 0))
-        y_s[pl.ds(c, 32, stride=CH), :] = here + late
+        y_s[pl.ds(c, 32, stride=PITCH), :] = here + late
 
     for u in range(AT_ONCE):
         build(u, u)
@@ -101,27 +102,34 @@
         for u in range(AT_ONCE):
             collect((i - 1) * AT_ONCE + u, u)
             multiply(u)
-            build(jnp.minimum((i + 1) * AT_ONCE, CH - AT_ONCE) + u, u)
+            build((i + 1) * AT_ONCE + u, u)
         return carry
 
-    lax.fori_loop(1, CH // AT_ONCE, step, 0)
+    lax.fori_loop(1, CH // AT_ONCE - 1, step, 0)
+    for u in range(AT_ONCE):
+        collect(CH - 2 * AT_ONCE + u, u)
+        multiply(u)
     for u in range(AT_ONCE):
         collect(CH - AT_ONCE + u, u)
     for s in range(PARTS):
         for q in range(4):
-            g = 4 * s + q
-            y_ref[s, q] = y_s[CH * g : CH * g + CH].astype(BF16)
+            at = PITCH * (4 * s + q)
+            y_ref[s, q] = y_s[at : at + CH].astype(BF16)
 
 
-def gate_kernel(y_ref, k_ref, v_ref, g_ref, s_ref, o_ref):
-    for half in range(2):
-        ch = slice(128 * half, 128 * half + 128)
-        for q in range(4):
-            pos = slice(128 * q, 128 * q + 128)
+def gate_kernel(y_ref, d_ref, g_ref, o_ref, o_s, sem):
+    copies = []
+    for q in range(4):
+        pos = slice(128 * q, 128 * q + 128)
+        for half in range(2):
+            ch = slice(128 * half, 128 * half + 128)
             y = y_ref[4 * half : 4 * half + 4, q].reshape(128, 128).astype(F32).T
-            p = product_of(k_ref[pos, ch], v_ref[pos, ch]).astype(F32)
-            out = g_ref[pos, ch].astype(F32) * (y + s_ref[:, ch] * p)
-            o_ref[pos, ch] = out.astype(BF16)
+            out = g_ref[pos, ch].astype(F32) * (y + d_ref[pos, ch])
+            o_s[pos, ch] = out.astype(BF16)
+        copies.append(pltpu.make_async_copy(o_s.at[pos], o_ref.at[pos], sem.at[q]))
+        copies[-1].start()
+    for copy in copies:
+        copy.wait()
 
 
 def call(kernel, out, scratch=(), limit=VMEM, **more):
@@ -139,27 +147,31 @@
 
 
 def on_device(key_branch, value_branch, gate_branch, conv_filter, skip_gain):
-    skip_gain = skip_gain.reshape(1, 256)
+    product = product_of(key_branch, value_branch)
+    direct = skip_gain[None, :] * product.astype(F32)
     sent = call(pack_kernel, jax.ShapeDtypeStruct((PARTS, 8, CH, 128), BF16))(
-        product_of(key_branch, value_branch), conv_filter
+        product, conv_filter
     )
     got = exchange(sent)
-    mixed, skip_gain = call(
+    mixed = call(
         conv_kernel,
-        [jax.ShapeDtypeStruct((PARTS, 4, CH, 128), BF16), jax.ShapeDtypeStruct((1, 256), F32)],
+        jax.ShapeDtypeStruct((PARTS, 4, CH, 128), BF16),
         [
             pltpu.VMEM((32 * CH, 128), F32),
             pltpu.VMEM((4, 8 * CH, 128), F32),
             pltpu.VMEM((AT_ONCE, 256, 256), BF16),
             pltpu.VMEM((AT_ONCE, 256, 256), BF16),
             pltpu.VMEM((AT_ONCE, 256, 256), F32),
-            pltpu.VMEM((32 * CH, 128), F32),
+            pltpu.VMEM((32 * PITCH, 128), F32),
         ],
-    )(got, skip_gain)
+    )(got)
     back = exchange(mixed)
-    return call(gate_kernel, jax.ShapeDtypeStruct((512, 256), BF16))(
-        back, key_branch, value_branch, gate_branch, skip_gain
-    )
+    return call(
+        gate_kernel,
+        jax.ShapeDtypeStruct((512, 256), BF16),
+        [pltpu.VMEM((512, 256), BF16), pltpu.SemaphoreType.DMA((4,))],
+        out_specs=pl.BlockSpec(memory_space=pl.ANY),
+    )(back, direct, gate_branch)
 
 
 def solution(mesh):

time: 33.5 us -> 31.8 us (0.949)
  Pallas kernels: 5.35 us -> 4.39 us
  local copies, waits for them, and re-layouts: 0.7 us -> 0.01 us
    mul x0 -> x1, other arithmetic: none -> 1.17 us  [on_device(): direct = skip_gain[None, :] * product.astype(F32)]
    convert_element_type x1 -> x0, other arithmetic: 1.14 us -> none  [product_of(): return (k.astype(F32) * v.astype(F32)).astype(BF16)]
    pallas_call x2, Pallas kernels: 5.13 us -> 4.17 us  [the longest x1 3.34 us: on_device(): call(conv_kernel, jax.ShapeDtypeStruct((PARTS, 4, CH, 128), BF16), [pltpu...]
    unnamed x10 -> x4, local copies, waits for them, and re-layouts: 0.7 us -> 0.01 us
where the time goes in v2:
time: 31.8 us; the launch traced here: 31.3 us
  blocking collectives  25.7 us (81%)
  Pallas kernels  4.39 us (14%)
  other arithmetic  1.17 us (4%)
    all_to_all x2, blocking collectives, exchange(): return lax.all_to_all(x, 'seq', split_axis=0, concat_axis=0, tiled=True)  25.7 us
    pallas_call x1, Pallas kernels, on_device(): call(conv_kernel, jax.ShapeDtypeStruct((PARTS, 4, CH, 128), BF16), [pltpu...  3.34 us
    mul x1, other arithmetic, on_device(): direct = skip_gain[None, :] * product.astype(F32)  1.17 us
    pallas_call x1, Pallas kernels, on_device(): call(gate_kernel, jax.ShapeDtypeStruct((512, 256), BF16), [pltpu.VMEM((51...  0.83 us

profile of v2, /device:TPU:0, one launch (start us, length us, event | category | flops | bytes accessed | tf_op | source)
XLA Modules:
  0.0 31.3 jit_solution(15991284944066636801)
XLA Ops:
  0.0 0.0 copy-start.1
  0.0 1.2 %convert_multiply_fusion = (f32[512,256]{1,0:T(8,128)S(1)}, bf16[512,256]{1,0:T(8,128)(2,1)S(1)}) fusion(f32[256]{0:T(256)} %param.9, bf16[512,256]{1,0:T(8,128)(2,1)} %param.6, bf16[512,256]{1,0:T(8,128)(2,1)} %param.5), kind=kLoop, calls=%fused_computation | loop fusion | flops 786432 | bytes 1311744 | tf_op jit(solution)/shard_map/mul | solution.py:151
  1.2 0.0 copy-done.1
  1.2 0.2 shard_map.55
  1.4 15.6 %all_to_all.10.r_ref = bf16[8,8,32,128]{3,2,1,0:T(8,128)(2,1)S(1)} all-to-all(bf16[8,8,32,128]{3,2,1,0:T(8,128)(2,1)S(1)} %shard_map.55), channel_id=1, replica_groups=mesh['seq'=8,'ch'=16] {'seq'}, dimensions={0} | all-to-all | bytes 1048576 | tf_op jit(solution)/shard_map/all_to_all | solution.py:146
  17.0 3.3 %shard_map.56 = bf16[8,4,32,128]{3,2,1,0:T(8,128)(2,1)S(1)} custom-call(bf16[8,8,32,128]{3,2,1,0:T(8,128)(2,1)S(1)} %all_to_all.10.r_ref), custom_call_target="tpu_custom_call" | custom-call | tf_op jit(solution)/shard_map/pallas_call | solution.py:156
  20.3 0.0 copy-start
  20.3 10.1 %all_to_all.11.y_ref = bf16[8,4,32,128]{3,2,1,0:T(8,128)(2,1)S(1)} all-to-all(bf16[8,4,32,128]{3,2,1,0:T(8,128)(2,1)S(1)} %shard_map.56), channel_id=1, replica_groups=mesh['seq'=8,'ch'=16] {'seq'}, dimensions={0} | all-to-all | bytes 524288 | tf_op jit(solution)/shard_map/all_to_all | solution.py:146
  30.4 0.0 copy-done
  30.4 0.8 %shard_map.57 = bf16[512,256]{1,0:T(8,128)(2,1)} custom-call(bf16[8,4,32,128]{3,2,1,0:T(8,128)(2,1)S(1)} %all_to_all.11.y_ref, f32[512,256]{1,0:T(8,128)S(1)} %get-tuple-element.5.d_ref, bf16[512,256]{1,0:T(8,128)(2,1)S(1)} %copy-done), custom_call_target="tpu_custom_call" | custom-call | tf_op jit(solution)/shard_map/pallas_call | solution.py:169
Async XLA Ops:
  0.0 1.2 %copy-start.1 = (bf16[512,256]{1,0:T(8,128)(2,1)S(1)}, bf16[512,256]{1,0:T(8,128)(2,1)}, u32[]{:S(2)}) copy-start(bf16[512,256]{1,0:T(8,128)(2,1)} %f_ref.1) | copy-start | bytes 786436
  20.3 10.1 %copy-start = (bf16[512,256]{1,0:T(8,128)(2,1)S(1)}, bf16[512,256]{1,0:T(8,128)(2,1)}, u32[]{:S(2)}) copy-start(bf16[512,256]{1,0:T(8,128)(2,1)} %g_ref.1) | copy-start | bytes 786436

commit v3 on v2

--- a/solution.py
+++ b/solution.py
@@ -9,16 +9,21 @@
 BF16 = jnp.bfloat16
 PARTS = 8
 CH = 32
+ORDER = (0, 3, 1, 2)
 AT_ONCE = 8
 PITCH = 40
 VMEM = 48 * 1024 * 1024
 
 
-def product_of(k, v):
-    return (k.astype(F32) * v.astype(F32)).astype(BF16)
-
-
-def pack_kernel(p_ref, f_ref, o_ref):
+def pieces_of(refs):
+    def piece(j, low, high):
+        return refs[ORDER.index(j // 2)][j % 2, low:high]
+
+    return piece
+
+
+def pack_kernel(p_ref, f_ref, o_s):
+    me = lax.axis_index("seq")
     p = p_ref[...].astype(F32)
     p = p.reshape(4, 8, 16, 256)
     p = jnp.stack([p[3 - a] for a in range(4)], 1).reshape(512, 256)
@@ -28,19 +33,26 @@
             for at, x in ((0, p), (4, f)):
                 block = x[128 * q : 128 * q + 128, 128 * half : 128 * half + 128]
                 block = block.T.astype(BF16).reshape(4, CH, 128)
-                o_ref[4 * half : 4 * half + 4, at + q] = block
-
-
-def conv_kernel(r_ref, y_ref, g_s, v_s, a_s, b_s, o_s, y_s):
+                for t in range(4):
+                    o_s[lax.bitwise_xor(me, 4 * half + t), at + q] = block[t]
+
+
+def conv_kernel(*refs):
+    r_refs, (y_ref, g_s, v_s, a_s, b_s, o_s, y_s) = refs[:-7], refs[-7:]
+    piece = pieces_of(r_refs)
+    me = lax.axis_index("seq")
+    odd = lax.rem(me, 2) == 1
     lane = lax.broadcasted_iota(jnp.int32, (32, 128), 1)
     row = lax.broadcasted_iota(jnp.int32, (32, 128), 0)
     for s in range(PARTS):
+        at = pl.multiple_of(4 * CH * lax.bitwise_xor(me, s), 4 * CH)
+        g_s[pl.ds(at, 4 * CH)] = piece(s, 4, 8).astype(F32).reshape(4 * CH, 128)
+    for i in range(4):
+        j = lax.div(lax.bitwise_xor(me, 2 * i), 2)
+        mine, other = piece(2 * i, 0, 4).astype(F32), piece(2 * i + 1, 0, 4).astype(F32)
+        firsts, seconds = jnp.where(odd, mine, other), jnp.where(odd, other, mine)
         for q in range(4):
-            g = 4 * s + q
-            g_s[CH * g : CH * g + CH] = r_ref[s, 4 + q].astype(F32)
-    for q in range(4):
-        for j in range(4):
-            first, second = [r_ref[s, q].astype(F32) for s in (2 * j + 1, 2 * j)]
+            first, second = firsts[q], seconds[q]
             swapped = pltpu.roll(jnp.where(lane < 64, second, first), 64, 1)
             at = 2 * CH * q
             v_s[j, at : at + CH] = jnp.where(lane < 64, first, swapped)
@@ -114,16 +126,21 @@
     for s in range(PARTS):
         for q in range(4):
             at = PITCH * (4 * s + q)
-            y_ref[s, q] = y_s[at : at + CH].astype(BF16)
-
-
-def gate_kernel(y_ref, d_ref, g_ref, o_ref, o_s, sem):
+            y_ref[lax.bitwise_xor(me, s), q] = y_s[at : at + CH].astype(BF16)
+
+
+def gate_kernel(*refs):
+    y_refs, (d_ref, g_ref, o_ref, y_s, o_s, sem) = refs[:-6], refs[-6:]
+    piece = pieces_of(y_refs)
+    me = lax.axis_index("seq")
+    for s in range(PARTS):
+        y_s[lax.bitwise_xor(me, s)] = piece(s, 0, 4)
     copies = []
     for q in range(4):
         pos = slice(128 * q, 128 * q + 128)
         for half in range(2):
             ch = slice(128 * half, 128 * half + 128)
-            y = y_ref[4 * half : 4 * half + 4, q].reshape(128, 128).astype(F32).T
+            y = y_s[4 * half : 4 * half + 4, q].reshape(128, 128).astype(F32).T
             out = g_ref[pos, ch].astype(F32) * (y + d_ref[pos, ch])
             o_s[pos, ch] = out.astype(BF16)
         copies.append(pltpu.make_async_copy(o_s.at[pos], o_ref.at[pos], sem.at[q]))
@@ -142,13 +159,22 @@
     )
 
 
+def swap(x, j):
+    return lax.ppermute(x, "seq", [(i, i ^ j) for i in range(PARTS)])
+
+
 def exchange(x):
-    return lax.all_to_all(x, "seq", split_axis=0, concat_axis=0, tiled=True)
+    x = x.reshape(4, 2, *x.shape[1:])
+    other = swap(x[:, 1], 1)
+    pairs = jnp.stack([x[:, 0], other], 1)
+    return [swap(pairs[i], 2 * i) if i else pairs[i] for i in ORDER]
 
 
 def on_device(key_branch, value_branch, gate_branch, conv_filter, skip_gain):
-    product = product_of(key_branch, value_branch)
-    direct = skip_gain[None, :] * product.astype(F32)
+    product = key_branch.astype(F32) * value_branch.astype(F32)
+    product = lax.reduce_precision(product, 8, 7)
+    direct = skip_gain[None, :] * product
+    product = product.astype(BF16)
     sent = call(pack_kernel, jax.ShapeDtypeStruct((PARTS, 8, CH, 128), BF16))(
         product, conv_filter
     )
@@ -164,14 +190,18 @@
             pltpu.VMEM((AT_ONCE, 256, 256), F32),
             pltpu.VMEM((32 * PITCH, 128), F32),
         ],
-    )(got)
+    )(*got)
     back = exchange(mixed)
     return call(
         gate_kernel,
         jax.ShapeDtypeStruct((512, 256), BF16),
-        [pltpu.VMEM((512, 256), BF16), pltpu.SemaphoreType.DMA((4,))],
+        [
+            pltpu.VMEM((PARTS, 4, CH, 128), BF16),
+            pltpu.VMEM((512, 256), BF16),
+            pltpu.SemaphoreType.DMA((4,)),
+        ],
         out_specs=pl.BlockSpec(memory_space=pl.ANY),
-    )(back, direct, gate_branch)
+    )(*back, direct, gate_branch)
 
 
 def solution(mesh):

time: 31.8 us -> 28.4 us (0.89); the launches traced: 31.3 us -> 28.3 us
  blocking collectives: 25.7 us -> 0 us
  waiting for transfers between devices: 0 us -> 13.5 us
  starting transfers between devices: 0 us -> 9 us
    all_to_all x2 -> x0, blocking collectives: 25.7 us -> none  [exchange(): return lax.all_to_all(x, 'seq', split_axis=0, concat_axis=0, tiled=True)]
    ppermute x0 -> x8, waiting for transfers between devices: none -> 13.5 us  [swap(): return lax.ppermute(x, 'seq', [(i, i ^ j) for i in range(PARTS)])]
    ppermute x0 -> x8, starting transfers between devices: none -> 9 us  [swap(): return lax.ppermute(x, 'seq', [(i, i ^ j) for i in range(PARTS)])]
  transfers between devices with their start and end apart: 0 -> 8, of which waited for: 0 -> 8; matrix products, arithmetic and copies ran while one was open for 0% -> 0% of each run, Pallas kernels for 0% -> 0%
where the time goes in v3:
time: 28.4 us; the launch traced here: 28.3 us
  waiting for transfers between devices  13.5 us (48%)
  starting transfers between devices  9 us (32%)
  Pallas kernels  4.45 us (16%)
  other arithmetic  1.24 us (4%)
    ppermute x8, waiting for transfers between devices, swap(): return lax.ppermute(x, 'seq', [(i, i ^ j) for i in range(PARTS)])  13.5 us
    ppermute x8, starting transfers between devices, swap(): return lax.ppermute(x, 'seq', [(i, i ^ j) for i in range(PARTS)])  9 us
    pallas_call x1, Pallas kernels, on_device(): call(conv_kernel, jax.ShapeDtypeStruct((PARTS, 4, CH, 128), BF16), [pltpu...  3.37 us
    mul x1, other arithmetic, on_device(): direct = skip_gain[None, :] * product  1.17 us
    pallas_call x1, Pallas kernels, on_device(): call(gate_kernel, jax.ShapeDtypeStruct((512, 256), BF16), [pltpu.VMEM((PA...  0.86 us
  transfers between devices with their start and end apart: 8, of which 8 were waited for; matrix products, arithmetic and copies ran while one was open for 0% of the time, Pallas kernels for 0%

profile of v3, /device:TPU:0, one launch (start us, length us, event | category | flops | bytes accessed | tf_op | source)
XLA Modules:
  0.0 28.3 jit_solution(1758324757958690018)
XLA Ops:
  0.0 0.0 copy-start.1
  0.0 1.2 %fusion = (f32[512,256]{1,0:T(8,128)S(1)}, bf16[512,256]{1,0:T(8,128)(2,1)S(1)}) fusion(bf16[512,256]{1,0:T(8,128)(2,1)} %param.6, bf16[512,256]{1,0:T(8,128)(2,1)} %param.5, f32[256]{0:T(256)} %param.9), kind=kLoop, calls=%fused_computation.7 | loop fusion | flops 786432 | bytes 1311744 | tf_op jit(solution)/shard_map/mul | solution.py:176
  1.2 0.0 copy-done.1
  1.2 0.2 shard_map.55
  1.5 0.1 collective-permute-start
  1.6 1.5 %collective-permute-done = bf16[4,8,32,128]{3,2,1,0:T(8,128)(2,1)S(1)} collective-permute-done((bf16[4,8,32,128]{3,2,1,0:T(8,128)(2,1)S(1)}, bf16[4,8,32,128]{3,2,1,0:T(8,128)(2,1)S(1)}, u32[]{:S(2)}, u32[]{:S(2)}) %collective-permute-start) | collective-permute-done | bytes 262176 | tf_op jit(solution)/shard_map/ppermute | solution.py:163
  3.1 4.0 %collective-permute-start.3 = (bf16[2,8,32,128]{3,2,1,0:T(8,128)(2,1)S(1)}, bf16[2,8,32,128]{3,2,1,0:T(8,128)(2,1)S(1)}, u32[]{:S(2)}, u32[]{:S(2)}) collective-permute-start(bf16[2,8,32,128]{3,2,1,0:T(8,128)(2,1)S(1)} %get-tuple-element.7), channel_id=1, source_target_pairs={{0,64},{16,80},{32,96},{48,112},{64,0},{80,16},{96,32},{112,48},{1... | collective-permute-start | bytes 393224 | tf_op jit(solution)/shard_map/ppermute | solution.py:163
  7.2 0.7 %collective-permute-start.1 = (bf16[2,8,32,128]{3,2,1,0:T(8,128)(2,1)S(1)}, bf16[2,8,32,128]{3,2,1,0:T(8,128)(2,1)S(1)}, u32[]{:S(2)}, u32[]{:S(2)}) collective-permute-start(bf16[2,8,32,128]{3,2,1,0:T(8,128)(2,1)S(1)} %get-tuple-element.9), channel_id=1, source_target_pairs={{0,96},{16,112},{32,64},{48,80},{64,32},{80,48},{96,0},{112,16},{1... | collective-permute-start | bytes 393224 | tf_op jit(solution)/shard_map/ppermute | solution.py:163
  7.9 0.3 %collective-permute-start.2 = (bf16[2,8,32,128]{3,2,1,0:T(8,128)(2,1)S(1)}, bf16[2,8,32,128]{3,2,1,0:T(8,128)(2,1)S(1)}, u32[]{:S(2)}, u32[]{:S(2)}) collective-permute-start(bf16[2,8,32,128]{3,2,1,0:T(8,128)(2,1)S(1)} %get-tuple-element.10), channel_id=1, source_target_pairs={{0,32},{16,48},{32,0},{48,16},{64,96},{80,112},{96,64},{112,80},{1... | collective-permute-start | bytes 393224 | tf_op jit(solution)/shard_map/ppermute | solution.py:163
  8.2 2.9 %collective-permute-done.3.refs_3_ = bf16[2,8,32,128]{3,2,1,0:T(8,128)(2,1)S(1)} collective-permute-done((bf16[2,8,32,128]{3,2,1,0:T(8,128)(2,1)S(1)}, bf16[2,8,32,128]{3,2,1,0:T(8,128)(2,1)S(1)}, u32[]{:S(2)}, u32[]{:S(2)}) %collective-permute-start.3) | collective-permute-done | bytes 131104 | tf_op jit(solution)/shard_map/ppermute | solution.py:163
  11.1 2.7 %collective-permute-done.1.refs_1_ = bf16[2,8,32,128]{3,2,1,0:T(8,128)(2,1)S(1)} collective-permute-done((bf16[2,8,32,128]{3,2,1,0:T(8,128)(2,1)S(1)}, bf16[2,8,32,128]{3,2,1,0:T(8,128)(2,1)S(1)}, u32[]{:S(2)}, u32[]{:S(2)}) %collective-permute-start.1) | collective-permute-done | bytes 131104 | tf_op jit(solution)/shard_map/ppermute | solution.py:163
  13.8 0.8 %collective-permute-done.2.refs_2_ = bf16[2,8,32,128]{3,2,1,0:T(8,128)(2,1)S(1)} collective-permute-done((bf16[2,8,32,128]{3,2,1,0:T(8,128)(2,1)S(1)}, bf16[2,8,32,128]{3,2,1,0:T(8,128)(2,1)S(1)}, u32[]{:S(2)}, u32[]{:S(2)}) %collective-permute-start.2) | collective-permute-done | bytes 131104 | tf_op jit(solution)/shard_map/ppermute | solution.py:163
  14.5 3.4 %shard_map.56 = bf16[8,4,32,128]{3,2,1,0:T(8,128)(2,1)S(1)} custom-call(bf16[2,8,32,128]{3,2,1,0:T(8,128)(2,1)S(1)} %get-tuple-element.8.refs_0_, bf16[2,8,32,128]{3,2,1,0:T(8,128)(2,1)S(1)} %collective-permute-done.1.refs_1_, bf16[2,8,32,128]{3,2,1,0:T(8,128)(2,1)S(1)} %collective-permute-done.2.refs_2_, ...), custom_call_target="tpu_custom_call" | custom-call | tf_op jit(solution)/shard_map/pallas_call | solution.py:182
  18.0 0.1 collective-permute-start.4
  18.0 1.3 %collective-permute-done.4 = bf16[4,4,32,128]{3,2,1,0:T(8,128)(2,1)S(1)} collective-permute-done((bf16[4,4,32,128]{3,2,1,0:T(8,128)(2,1)S(1)}, bf16[4,4,32,128]{3,2,1,0:T(8,128)(2,1)S(1)}, u32[]{:S(2)}, u32[]{:S(2)}) %collective-permute-start.4) | collective-permute-done | bytes 131104 | tf_op jit(solution)/shard_map/ppermute | solution.py:163
  19.4 0.0 copy-start
  19.4 2.1 %collective-permute-start.7 = (bf16[2,4,32,128]{3,2,1,0:T(8,128)(2,1)S(1)}, bf16[2,4,32,128]{3,2,1,0:T(8,128)(2,1)S(1)}, u32[]{:S(2)}, u32[]{:S(2)}) collective-permute-start(bf16[2,4,32,128]{3,2,1,0:T(8,128)(2,1)S(1)} %get-tuple-element.13), channel_id=1, source_target_pairs={{0,64},{16,80},{32,96},{48,112},{64,0},{80,16},{96,32},{112,48},{1... | collective-permute-start | bytes 196616 | tf_op jit(solution)/shard_map/ppermute | solution.py:163
  21.5 1.7 %collective-permute-start.5 = (bf16[2,4,32,128]{3,2,1,0:T(8,128)(2,1)S(1)}, bf16[2,4,32,128]{3,2,1,0:T(8,128)(2,1)S(1)}, u32[]{:S(2)}, u32[]{:S(2)}) collective-permute-start(bf16[2,4,32,128]{3,2,1,0:T(8,128)(2,1)S(1)} %get-tuple-element.15), channel_id=1, source_target_pairs={{0,96},{16,112},{32,64},{48,80},{64,32},{80,48},{96,0},{112,16},{1... | collective-permute-start | bytes 196616 | tf_op jit(solution)/shard_map/ppermute | solution.py:163
  23.2 0.0 collective-permute-start.6
  23.2 2.1 %collective-permute-done.7.refs_3_ = bf16[2,4,32,128]{3,2,1,0:T(8,128)(2,1)S(1)} collective-permute-done((bf16[2,4,32,128]{3,2,1,0:T(8,128)(2,1)S(1)}, bf16[2,4,32,128]{3,2,1,0:T(8,128)(2,1)S(1)}, u32[]{:S(2)}, u32[]{:S(2)}) %collective-permute-start.7) | collective-permute-done | bytes 65568 | tf_op jit(solution)/shard_map/ppermute | solution.py:163
  25.3 1.7 %collective-permute-done.5.refs_1_ = bf16[2,4,32,128]{3,2,1,0:T(8,128)(2,1)S(1)} collective-permute-done((bf16[2,4,32,128]{3,2,1,0:T(8,128)(2,1)S(1)}, bf16[2,4,32,128]{3,2,1,0:T(8,128)(2,1)S(1)}, u32[]{:S(2)}, u32[]{:S(2)}) %collective-permute-start.5) | collective-permute-done | bytes 65568 | tf_op jit(solution)/shard_map/ppermute | solution.py:163
  27.0 0.4 %collective-permute-done.6.refs_2_ = bf16[2,4,32,128]{3,2,1,0:T(8,128)(2,1)S(1)} collective-permute-done((bf16[2,4,32,128]{3,2,1,0:T(8,128)(2,1)S(1)}, bf16[2,4,32,128]{3,2,1,0:T(8,128)(2,1)S(1)}, u32[]{:S(2)}, u32[]{:S(2)}) %collective-permute-start.6) | collective-permute-done | bytes 65568 | tf_op jit(solution)/shard_map/ppermute | solution.py:163
  27.4 0.0 copy-done
  27.4 0.9 %shard_map.57 = bf16[512,256]{1,0:T(8,128)(2,1)} custom-call(bf16[2,4,32,128]{3,2,1,0:T(8,128)(2,1)S(1)} %get-tuple-element.14.refs_0_, bf16[2,4,32,128]{3,2,1,0:T(8,128)(2,1)S(1)} %collective-permute-done.5.refs_1_, bf16[2,4,32,128]{3,2,1,0:T(8,128)(2,1)S(1)} %collective-permute-done.6.refs_2_, bf16[2,4,32,128]{3,2,1,0:T(8,128)(2,1)S(1)} %collective-permute-done.7.refs_3_, ...), custom_call_target="tpu_custom_call" | custom-call | tf_op jit(solution)/shard_map/pallas_call | solution.py:195
  (4 shorter events, 0.1 us)
Async XLA Ops:
  0.0 1.2 %copy-start.1 = (bf16[512,256]{1,0:T(8,128)(2,1)S(1)}, bf16[512,256]{1,0:T(8,128)(2,1)}, u32[]{:S(2)}) copy-start(bf16[512,256]{1,0:T(8,128)(2,1)} %f_ref.1) | copy-start | bytes 786436
  1.5 1.6 %collective-permute-start = (bf16[4,8,32,128]{3,2,1,0:T(8,128)(2,1)S(1)}, bf16[4,8,32,128]{3,2,1,0:T(8,128)(2,1)S(1)}, u32[]{:S(2)}, u32[]{:S(2)}) collective-permute-start(bf16[4,8,32,128]{3,2,1,0:T(8,128)(2,1)S(1)} %get-tuple-element.11), channel_id=1, source_target_pairs={{0,16},{16,0},{32,48},{48,32},{64,80},{80,64},{96,112},{112,96},{1... | collective-permute-start | bytes 786440 | tf_op jit(solution)/shard_map/ppermute | solution.py:163
  3.1 7.9 %collective-permute-start.3 = (bf16[2,8,32,128]{3,2,1,0:T(8,128)(2,1)S(1)}, bf16[2,8,32,128]{3,2,1,0:T(8,128)(2,1)S(1)}, u32[]{:S(2)}, u32[]{:S(2)}) collective-permute-start(bf16[2,8,32,128]{3,2,1,0:T(8,128)(2,1)S(1)} %get-tuple-element.7), channel_id=1, source_target_pairs={{0,64},{16,80},{32,96},{48,112},{64,0},{80,16},{96,32},{112,48},{1... | collective-permute-start | bytes 393224 | tf_op jit(solution)/shard_map/ppermute | solution.py:163
  7.2 6.6 %collective-permute-start.1 = (bf16[2,8,32,128]{3,2,1,0:T(8,128)(2,1)S(1)}, bf16[2,8,32,128]{3,2,1,0:T(8,128)(2,1)S(1)}, u32[]{:S(2)}, u32[]{:S(2)}) collective-permute-start(bf16[2,8,32,128]{3,2,1,0:T(8,128)(2,1)S(1)} %get-tuple-element.9), channel_id=1, source_target_pairs={{0,96},{16,112},{32,64},{48,80},{64,32},{80,48},{96,0},{112,16},{1... | collective-permute-start | bytes 393224 | tf_op jit(solution)/shard_map/ppermute | solution.py:163
  7.9 6.7 %collective-permute-start.2 = (bf16[2,8,32,128]{3,2,1,0:T(8,128)(2,1)S(1)}, bf16[2,8,32,128]{3,2,1,0:T(8,128)(2,1)S(1)}, u32[]{:S(2)}, u32[]{:S(2)}) collective-permute-start(bf16[2,8,32,128]{3,2,1,0:T(8,128)(2,1)S(1)} %get-tuple-element.10), channel_id=1, source_target_pairs={{0,32},{16,48},{32,0},{48,16},{64,96},{80,112},{96,64},{112,80},{1... | collective-permute-start | bytes 393224 | tf_op jit(solution)/shard_map/ppermute | solution.py:163
  18.0 1.4 %collective-permute-start.4 = (bf16[4,4,32,128]{3,2,1,0:T(8,128)(2,1)S(1)}, bf16[4,4,32,128]{3,2,1,0:T(8,128)(2,1)S(1)}, u32[]{:S(2)}, u32[]{:S(2)}) collective-permute-start(bf16[4,4,32,128]{3,2,1,0:T(8,128)(2,1)S(1)} %get-tuple-element.17), channel_id=1, source_target_pairs={{0,16},{16,0},{32,48},{48,32},{64,80},{80,64},{96,112},{112,96},{1... | collective-permute-start | bytes 393224 | tf_op jit(solution)/shard_map/ppermute | solution.py:163
  19.4 8.1 %copy-start = (bf16[512,256]{1,0:T(8,128)(2,1)S(1)}, bf16[512,256]{1,0:T(8,128)(2,1)}, u32[]{:S(2)}) copy-start(bf16[512,256]{1,0:T(8,128)(2,1)} %refs_5_.1) | copy-start | bytes 786436
  19.4 5.9 %collective-permute-start.7 = (bf16[2,4,32,128]{3,2,1,0:T(8,128)(2,1)S(1)}, bf16[2,4,32,128]{3,2,1,0:T(8,128)(2,1)S(1)}, u32[]{:S(2)}, u32[]{:S(2)}) collective-permute-start(bf16[2,4,32,128]{3,2,1,0:T(8,128)(2,1)S(1)} %get-tuple-element.13), channel_id=1, source_target_pairs={{0,64},{16,80},{32,96},{48,112},{64,0},{80,16},{96,32},{112,48},{1... | collective-permute-start | bytes 196616 | tf_op jit(solution)/shard_map/ppermute | solution.py:163
  21.5 5.5 %collective-permute-start.5 = (bf16[2,4,32,128]{3,2,1,0:T(8,128)(2,1)S(1)}, bf16[2,4,32,128]{3,2,1,0:T(8,128)(2,1)S(1)}, u32[]{:S(2)}, u32[]{:S(2)}) collective-permute-start(bf16[2,4,32,128]{3,2,1,0:T(8,128)(2,1)S(1)} %get-tuple-element.15), channel_id=1, source_target_pairs={{0,96},{16,112},{32,64},{48,80},{64,32},{80,48},{96,0},{112,16},{1... | collective-permute-start | bytes 196616 | tf_op jit(solution)/shard_map/ppermute | solution.py:163
  23.2 4.3 %collective-permute-start.6 = (bf16[2,4,32,128]{3,2,1,0:T(8,128)(2,1)S(1)}, bf16[2,4,32,128]{3,2,1,0:T(8,128)(2,1)S(1)}, u32[]{:S(2)}, u32[]{:S(2)}) collective-permute-start(bf16[2,4,32,128]{3,2,1,0:T(8,128)(2,1)S(1)} %get-tuple-element.16), channel_id=1, source_target_pairs={{0,32},{16,48},{32,0},{48,16},{64,96},{80,112},{96,64},{112,80},{1... | collective-permute-start | bytes 196616 | tf_op jit(solution)/shard_map/ppermute | solution.py:163

commit v4 on v3

--- a/solution.py
+++ b/solution.py
@@ -17,6 +17,8 @@
 
 def pieces_of(refs):
     def piece(j, low, high):
+        if len(refs) == 8:
+            return refs[2 * (0, 3, 1, 2).index(j // 2) + j % 2][low:high]
         return refs[ORDER.index(j // 2)][j % 2, low:high]
 
     return piece
@@ -170,6 +172,15 @@
     return [swap(pairs[i], 2 * i) if i else pairs[i] for i in ORDER]
 
 
+def z_first(x):
+    x = x.reshape(4, 2, *x.shape[1:])
+    out = []
+    for i in (0, 3, 1, 2):
+        pair = swap(x[i], 2 * i) if i else x[0]
+        out += [pair[0], swap(pair[1], 1)]
+    return out
+
+
 def on_device(key_branch, value_branch, gate_branch, conv_filter, skip_gain):
     product = key_branch.astype(F32) * value_branch.astype(F32)
     product = lax.reduce_precision(product, 8, 7)
@@ -178,7 +189,7 @@
     sent = call(pack_kernel, jax.ShapeDtypeStruct((PARTS, 8, CH, 128), BF16))(
         product, conv_filter
     )
-    got = exchange(sent)
+    got = z_first(sent)
     mixed = call(
         conv_kernel,
         jax.ShapeDtypeStruct((PARTS, 4, CH, 128), BF16),

time: 28.4 us -> 28.3 us (level); the launches traced: 28.3 us -> 27.9 us
  waiting for transfers between devices: 13.5 us -> 12.7 us
  starting transfers between devices: 9 us -> 9.29 us
    ppermute x8 -> x11, waiting for transfers between devices: 13.5 us -> 12.7 us  [swap(): return lax.ppermute(x, 'seq', [(i, i ^ j) for i in range(PARTS)])]
    ppermute x8 -> x11, starting transfers between devices: 9 us -> 9.29 us  [swap(): return lax.ppermute(x, 'seq', [(i, i ^ j) for i in range(PARTS)])]
  transfers between devices with their start and end apart: 8 -> 11, of which waited for: 8 -> 9; matrix products, arithmetic and copies ran while one was open for 0% -> 0% of each run, Pallas kernels for 0% -> 0%
where the time goes in v4:
time: 28.3 us; the launch traced here: 27.9 us
  waiting for transfers between devices  12.7 us (45%)
  starting transfers between devices  9.29 us (33%)
  Pallas kernels  4.45 us (16%)
  other arithmetic  1.19 us (4%)
    ppermute x11, waiting for transfers between devices, swap(): return lax.ppermute(x, 'seq', [(i, i ^ j) for i in range(PARTS)])  12.7 us
    ppermute x11, starting transfers between devices, swap(): return lax.ppermute(x, 'seq', [(i, i ^ j) for i in range(PARTS)])  9.29 us
    pallas_call x1, Pallas kernels, on_device(): call(conv_kernel, jax.ShapeDtypeStruct((PARTS, 4, CH, 128), BF16), [pltpu...  3.37 us
    mul x1, other arithmetic, on_device(): direct = skip_gain[None, :] * product  1.17 us
    pallas_call x1, Pallas kernels, on_device(): call(gate_kernel, jax.ShapeDtypeStruct((512, 256), BF16), [pltpu.VMEM((PA...  0.86 us
  transfers between devices with their start and end apart: 11, of which 9 were waited for; matrix products, arithmetic and copies ran while one was open for 0% of the time, Pallas kernels for 0%

profile of v4, /device:TPU:0, one launch (start us, length us, event | category | flops | bytes accessed | tf_op | source)
XLA Modules:
  0.0 27.9 jit_solution(18421085363979838177)
XLA Ops:
  0.0 0.0 copy-start.1
  0.0 1.2 %fusion = (f32[512,256]{1,0:T(8,128)S(1)}, bf16[512,256]{1,0:T(8,128)(2,1)S(1)}) fusion(bf16[512,256]{1,0:T(8,128)(2,1)} %param.6, bf16[512,256]{1,0:T(8,128)(2,1)} %param.5, f32[256]{0:T(256)} %param.9), kind=kLoop, calls=%fused_computation.1 | loop fusion | flops 786432 | bytes 1311744 | tf_op jit(solution)/shard_map/mul | solution.py:187
  1.2 0.0 copy-done.1
  1.2 0.2 shard_map.55
  1.4 4.0 %collective-permute-start.5 = (bf16[2,8,32,128]{3,2,1,0:T(8,128)(2,1)S(1)}, bf16[2,8,32,128]{3,2,1,0:T(8,128)(2,1)S(1)}, u32[]{:S(2)}, u32[]{:S(2)}) collective-permute-start(bf16[2,8,32,128]{3,2,1,0:T(8,128)(2,1)S(1)} %get-tuple-element.7), channel_id=1, source_target_pairs={{0,64},{16,80},{32,96},{48,112},{64,0},{80,16},{96,32},{112,48},{1... | collective-permute-start | bytes 393224 | tf_op jit(solution)/shard_map/ppermute | solution.py:165
  5.5 0.1 collective-permute-start
  5.6 1.1 %collective-permute-start.3 = (bf16[2,8,32,128]{3,2,1,0:T(8,128)(2,1)S(1)}, bf16[2,8,32,128]{3,2,1,0:T(8,128)(2,1)S(1)}, u32[]{:S(2)}, u32[]{:S(2)}) collective-permute-start(bf16[2,8,32,128]{3,2,1,0:T(8,128)(2,1)S(1)} %get-tuple-element.8), channel_id=1, source_target_pairs={{0,32},{16,48},{32,0},{48,16},{64,96},{80,112},{96,64},{112,80},{1... | collective-permute-start | bytes 393224 | tf_op jit(solution)/shard_map/ppermute | solution.py:165
  6.7 0.0 collective-permute-start.1
  6.7 2.6 %collective-permute-done.5 = bf16[2,8,32,128]{3,2,1,0:T(8,128)(2,1)S(1)} collective-permute-done((bf16[2,8,32,128]{3,2,1,0:T(8,128)(2,1)S(1)}, bf16[2,8,32,128]{3,2,1,0:T(8,128)(2,1)S(1)}, u32[]{:S(2)}, u32[]{:S(2)}) %collective-permute-start.5) | collective-permute-done | bytes 131104 | tf_op jit(solution)/shard_map/ppermute | solution.py:165
  9.3 0.1 collective-permute-start.6
  9.4 3.1 %collective-permute-done.3 = bf16[2,8,32,128]{3,2,1,0:T(8,128)(2,1)S(1)} collective-permute-done((bf16[2,8,32,128]{3,2,1,0:T(8,128)(2,1)S(1)}, bf16[2,8,32,128]{3,2,1,0:T(8,128)(2,1)S(1)}, u32[]{:S(2)}, u32[]{:S(2)}) %collective-permute-start.3) | collective-permute-done | bytes 131104 | tf_op jit(solution)/shard_map/ppermute | solution.py:165
  12.5 0.1 collective-permute-start.4
  12.6 0.8 %collective-permute-done.1 = bf16[2,8,32,128]{3,2,1,0:T(8,128)(2,1)S(1)} collective-permute-done((bf16[2,8,32,128]{3,2,1,0:T(8,128)(2,1)S(1)}, bf16[2,8,32,128]{3,2,1,0:T(8,128)(2,1)S(1)}, u32[]{:S(2)}, u32[]{:S(2)}) %collective-permute-start.1) | collective-permute-done | bytes 131104 | tf_op jit(solution)/shard_map/ppermute | solution.py:165
  13.5 0.1 collective-permute-start.2
  13.6 0.0 collective-permute-done.refs_1_
  13.6 0.0 collective-permute-done.6.refs_7_
  13.6 0.3 %collective-permute-done.4.refs_5_ = bf16[8,32,128]{2,1,0:T(8,128)(2,1)S(1)} collective-permute-done((bf16[8,32,128]{2,1,0:T(8,128)(2,1)S(1)}, bf16[8,32,128]{2,1,0:T(8,128)(2,1)S(1)}, u32[]{:S(2)}, u32[]{:S(2)}) %collective-permute-start.4) | collective-permute-done | bytes 65568 | tf_op jit(solution)/shard_map/ppermute | solution.py:165
  13.9 0.9 %collective-permute-done.2.refs_3_ = bf16[8,32,128]{2,1,0:T(8,128)(2,1)S(1)} collective-permute-done((bf16[8,32,128]{2,1,0:T(8,128)(2,1)S(1)}, bf16[8,32,128]{2,1,0:T(8,128)(2,1)S(1)}, u32[]{:S(2)}, u32[]{:S(2)}) %collective-permute-start.2) | collective-permute-done | bytes 65568 | tf_op jit(solution)/shard_map/ppermute | solution.py:165
  14.8 3.4 %shard_map.56 = bf16[8,4,32,128]{3,2,1,0:T(8,128)(2,1)S(1)} custom-call(bf16[8,32,128]{2,1,0:T(8,128)(2,1)S(1)} %get-tuple-element.11.refs_0_, bf16[8,32,128]{2,1,0:T(8,128)(2,1)S(1)} %collective-permute-done.refs_1_, bf16[8,32,128]{2,1,0:T(8,128)(2,1)S(1)} %get-tuple-element.23.refs_2_, bf16[8,32,128]{2,1,0:T(8,128)(2,1)S(1)} %collective-permute-done.2.refs_3_, ...), custom_call_target="tpu_custom_call" | custom-call | tf_op jit(solution)/shard_map/pallas_call | solution.py:193
  18.2 0.2 collective-permute-start.7
  18.4 1.2 %collective-permute-done.7 = bf16[4,4,32,128]{3,2,1,0:T(8,128)(2,1)S(1)} collective-permute-done((bf16[4,4,32,128]{3,2,1,0:T(8,128)(2,1)S(1)}, bf16[4,4,32,128]{3,2,1,0:T(8,128)(2,1)S(1)}, u32[]{:S(2)}, u32[]{:S(2)}) %collective-permute-start.7) | collective-permute-done | bytes 131104 | tf_op jit(solution)/shard_map/ppermute | solution.py:165
  19.6 0.0 copy-start
  19.7 1.7 %collective-permute-start.10 = (bf16[2,4,32,128]{3,2,1,0:T(8,128)(2,1)S(1)}, bf16[2,4,32,128]{3,2,1,0:T(8,128)(2,1)S(1)}, u32[]{:S(2)}, u32[]{:S(2)}) collective-permute-start(bf16[2,4,32,128]{3,2,1,0:T(8,128)(2,1)S(1)} %get-tuple-element.12), channel_id=1, source_target_pairs={{0,64},{16,80},{32,96},{48,112},{64,0},{80,16},{96,32},{112,48},{1... | collective-permute-start | bytes 196616 | tf_op jit(solution)/shard_map/ppermute | solution.py:165
  21.3 1.4 %collective-permute-start.8 = (bf16[2,4,32,128]{3,2,1,0:T(8,128)(2,1)S(1)}, bf16[2,4,32,128]{3,2,1,0:T(8,128)(2,1)S(1)}, u32[]{:S(2)}, u32[]{:S(2)}) collective-permute-start(bf16[2,4,32,128]{3,2,1,0:T(8,128)(2,1)S(1)} %get-tuple-element.14), channel_id=1, source_target_pairs={{0,96},{16,112},{32,64},{48,80},{64,32},{80,48},{96,0},{112,16},{1... | collective-permute-start | bytes 196616 | tf_op jit(solution)/shard_map/ppermute | solution.py:165
  22.8 0.5 %collective-permute-start.9 = (bf16[2,4,32,128]{3,2,1,0:T(8,128)(2,1)S(1)}, bf16[2,4,32,128]{3,2,1,0:T(8,128)(2,1)S(1)}, u32[]{:S(2)}, u32[]{:S(2)}) collective-permute-start(bf16[2,4,32,128]{3,2,1,0:T(8,128)(2,1)S(1)} %get-tuple-element.15), channel_id=1, source_target_pairs={{0,32},{16,48},{32,0},{48,16},{64,96},{80,112},{96,64},{112,80},{1... | collective-permute-start | bytes 196616 | tf_op jit(solution)/shard_map/ppermute | solution.py:165
  23.2 2.3 %collective-permute-done.10.refs_3_ = bf16[2,4,32,128]{3,2,1,0:T(8,128)(2,1)S(1)} collective-permute-done((bf16[2,4,32,128]{3,2,1,0:T(8,128)(2,1)S(1)}, bf16[2,4,32,128]{3,2,1,0:T(8,128)(2,1)S(1)}, u32[]{:S(2)}, u32[]{:S(2)}) %collective-permute-start.10) | collective-permute-done | bytes 65568 | tf_op jit(solution)/shard_map/ppermute | solution.py:165
  25.6 1.3 %collective-permute-done.8.refs_1_ = bf16[2,4,32,128]{3,2,1,0:T(8,128)(2,1)S(1)} collective-permute-done((bf16[2,4,32,128]{3,2,1,0:T(8,128)(2,1)S(1)}, bf16[2,4,32,128]{3,2,1,0:T(8,128)(2,1)S(1)}, u32[]{:S(2)}, u32[]{:S(2)}) %collective-permute-start.8) | collective-permute-done | bytes 65568 | tf_op jit(solution)/shard_map/ppermute | solution.py:165
  26.9 0.1 collective-permute-done.9.refs_2_
  27.0 0.0 copy-done
  27.0 0.9 %shard_map.57 = bf16[512,256]{1,0:T(8,128)(2,1)} custom-call(bf16[2,4,32,128]{3,2,1,0:T(8,128)(2,1)S(1)} %get-tuple-element.13.refs_0_, bf16[2,4,32,128]{3,2,1,0:T(8,128)(2,1)S(1)} %collective-permute-done.8.refs_1_, bf16[2,4,32,128]{3,2,1,0:T(8,128)(2,1)S(1)} %collective-permute-done.9.refs_2_, bf16[2,4,32,128]{3,2,1,0:T(8,128)(2,1)S(1)} %collective-permute-done.10.refs_3_, ...), custom_call_target="tpu_custom_call" | custom-call | tf_op jit(solution)/shard_map/pallas_call | solution.py:206
  (7 shorter events, 0.1 us)
Async XLA Ops:
  0.0 1.2 %copy-start.1 = (bf16[512,256]{1,0:T(8,128)(2,1)S(1)}, bf16[512,256]{1,0:T(8,128)(2,1)}, u32[]{:S(2)}) copy-start(bf16[512,256]{1,0:T(8,128)(2,1)} %f_ref.1) | copy-start | bytes 786436
  1.4 7.8 %collective-permute-start.5 = (bf16[2,8,32,128]{3,2,1,0:T(8,128)(2,1)S(1)}, bf16[2,8,32,128]{3,2,1,0:T(8,128)(2,1)S(1)}, u32[]{:S(2)}, u32[]{:S(2)}) collective-permute-start(bf16[2,8,32,128]{3,2,1,0:T(8,128)(2,1)S(1)} %get-tuple-element.7), channel_id=1, source_target_pairs={{0,64},{16,80},{32,96},{48,112},{64,0},{80,16},{96,32},{112,48},{1... | collective-permute-start | bytes 393224 | tf_op jit(solution)/shard_map/ppermute | solution.py:165
  5.5 8.1 %collective-permute-start = (bf16[8,32,128]{2,1,0:T(8,128)(2,1)S(1)}, bf16[8,32,128]{2,1,0:T(8,128)(2,1)S(1)}, u32[]{:S(2)}, u32[]{:S(2)}) collective-permute-start(bf16[8,32,128]{2,1,0:T(8,128)(2,1)S(1)} %get-tuple-element.10), channel_id=1, source_target_pairs={{0,16},{16,0},{32,48},{48,32},{64,80},{80,64},{96,112},{112,96},{1... | collective-permute-start | bytes 196616 | tf_op jit(solution)/shard_map/ppermute | solution.py:165
  5.6 6.9 %collective-permute-start.3 = (bf16[2,8,32,128]{3,2,1,0:T(8,128)(2,1)S(1)}, bf16[2,8,32,128]{3,2,1,0:T(8,128)(2,1)S(1)}, u32[]{:S(2)}, u32[]{:S(2)}) collective-permute-start(bf16[2,8,32,128]{3,2,1,0:T(8,128)(2,1)S(1)} %get-tuple-element.8), channel_id=1, source_target_pairs={{0,32},{16,48},{32,0},{48,16},{64,96},{80,112},{96,64},{112,80},{1... | collective-permute-start | bytes 393224 | tf_op jit(solution)/shard_map/ppermute | solution.py:165
  6.7 6.8 %collective-permute-start.1 = (bf16[2,8,32,128]{3,2,1,0:T(8,128)(2,1)S(1)}, bf16[2,8,32,128]{3,2,1,0:T(8,128)(2,1)S(1)}, u32[]{:S(2)}, u32[]{:S(2)}) collective-permute-start(bf16[2,8,32,128]{3,2,1,0:T(8,128)(2,1)S(1)} %get-tuple-element.9), channel_id=1, source_target_pairs={{0,96},{16,112},{32,64},{48,80},{64,32},{80,48},{96,0},{112,16},{1... | collective-permute-start | bytes 393224 | tf_op jit(solution)/shard_map/ppermute | solution.py:165
  9.3 4.3 %collective-permute-start.6 = (bf16[8,32,128]{2,1,0:T(8,128)(2,1)S(1)}, bf16[8,32,128]{2,1,0:T(8,128)(2,1)S(1)}, u32[]{:S(2)}, u32[]{:S(2)}) collective-permute-start(bf16[8,32,128]{2,1,0:T(8,128)(2,1)S(1)} %get-tuple-element.18), channel_id=1, source_target_pairs={{0,16},{16,0},{32,48},{48,32},{64,80},{80,64},{96,112},{112,96},{1... | collective-permute-start | bytes 196616 | tf_op jit(solution)/shard_map/ppermute | solution.py:165
  12.5 1.3 %collective-permute-start.4 = (bf16[8,32,128]{2,1,0:T(8,128)(2,1)S(1)}, bf16[8,32,128]{2,1,0:T(8,128)(2,1)S(1)}, u32[]{:S(2)}, u32[]{:S(2)}) collective-permute-start(bf16[8,32,128]{2,1,0:T(8,128)(2,1)S(1)} %get-tuple-element.20), channel_id=1, source_target_pairs={{0,16},{16,0},{32,48},{48,32},{64,80},{80,64},{96,112},{112,96},{1... | collective-permute-start | bytes 196616 | tf_op jit(solution)/shard_map/ppermute | solution.py:165
  13.5 1.3 %collective-permute-start.2 = (bf16[8,32,128]{2,1,0:T(8,128)(2,1)S(1)}, bf16[8,32,128]{2,1,0:T(8,128)(2,1)S(1)}, u32[]{:S(2)}, u32[]{:S(2)}) collective-permute-start(bf16[8,32,128]{2,1,0:T(8,128)(2,1)S(1)} %get-tuple-element.22), channel_id=1, source_target_pairs={{0,16},{16,0},{32,48},{48,32},{64,80},{80,64},{96,112},{112,96},{1... | collective-permute-start | bytes 196616 | tf_op jit(solution)/shard_map/ppermute | solution.py:165
  18.2 1.4 %collective-permute-start.7 = (bf16[4,4,32,128]{3,2,1,0:T(8,128)(2,1)S(1)}, bf16[4,4,32,128]{3,2,1,0:T(8,128)(2,1)S(1)}, u32[]{:S(2)}, u32[]{:S(2)}) collective-permute-start(bf16[4,4,32,128]{3,2,1,0:T(8,128)(2,1)S(1)} %get-tuple-element.16), channel_id=1, source_target_pairs={{0,16},{16,0},{32,48},{48,32},{64,80},{80,64},{96,112},{112,96},{1... | collective-permute-start | bytes 393224 | tf_op jit(solution)/shard_map/ppermute | solution.py:165
  19.6 7.4 %copy-start = (bf16[512,256]{1,0:T(8,128)(2,1)S(1)}, bf16[512,256]{1,0:T(8,128)(2,1)}, u32[]{:S(2)}) copy-start(bf16[512,256]{1,0:T(8,128)(2,1)} %refs_5_.1) | copy-start | bytes 786436
  19.7 5.9 %collective-permute-start.10 = (bf16[2,4,32,128]{3,2,1,0:T(8,128)(2,1)S(1)}, bf16[2,4,32,128]{3,2,1,0:T(8,128)(2,1)S(1)}, u32[]{:S(2)}, u32[]{:S(2)}) collective-permute-start(bf16[2,4,32,128]{3,2,1,0:T(8,128)(2,1)S(1)} %get-tuple-element.12), channel_id=1, source_target_pairs={{0,64},{16,80},{32,96},{48,112},{64,0},{80,16},{96,32},{112,48},{1... | collective-permute-start | bytes 196616 | tf_op jit(solution)/shard_map/ppermute | solution.py:165
  21.3 5.6 %collective-permute-start.8 = (bf16[2,4,32,128]{3,2,1,0:T(8,128)(2,1)S(1)}, bf16[2,4,32,128]{3,2,1,0:T(8,128)(2,1)S(1)}, u32[]{:S(2)}, u32[]{:S(2)}) collective-permute-start(bf16[2,4,32,128]{3,2,1,0:T(8,128)(2,1)S(1)} %get-tuple-element.14), channel_id=1, source_target_pairs={{0,96},{16,112},{32,64},{48,80},{64,32},{80,48},{96,0},{112,16},{1... | collective-permute-start | bytes 196616 | tf_op jit(solution)/shard_map/ppermute | solution.py:165
  22.8 4.3 %collective-permute-start.9 = (bf16[2,4,32,128]{3,2,1,0:T(8,128)(2,1)S(1)}, bf16[2,4,32,128]{3,2,1,0:T(8,128)(2,1)S(1)}, u32[]{:S(2)}, u32[]{:S(2)}) collective-permute-start(bf16[2,4,32,128]{3,2,1,0:T(8,128)(2,1)S(1)} %get-tuple-element.15), channel_id=1, source_target_pairs={{0,32},{16,48},{32,0},{48,16},{64,96},{80,112},{96,64},{112,80},{1... | collective-permute-start | bytes 196616 | tf_op jit(solution)/shard_map/ppermute | solution.py:165

commit v5 on v3

v5 whole, which is shorter than its diff:
```python
import jax
import jax.numpy as jnp
from jax import lax
from jax.experimental import pallas as pl
from jax.experimental.pallas import tpu as pltpu
from jax.sharding import PartitionSpec as P

F32 = jnp.float32
BF16 = jnp.bfloat16
PARTS = 8
CH = 32
ORDER = (0, 3, 1, 2)
AT_ONCE = 8
SPREAD_AT_ONCE = 32
PITCH = 40
VMEM = 24 * 1024 * 1024


def pieces_of(refs):
    def piece(j, low, high):
        return refs[ORDER.index(j // 2)][j % 2, low:high]

    return piece


def pack_kernel(p_ref, f_ref, o_s):
    me = lax.axis_index("seq")
    p = p_ref[...].astype(F32)
    p = p.reshape(4, 8, 16, 256)
    p = jnp.stack([p[3 - a] for a in range(4)], 1).reshape(512, 256)
    f = f_ref[...].astype(F32)
    for half in range(2):
        for q in range(4):
            for at, x in ((0, p), (4, f)):
                block = x[128 * q : 128 * q + 128, 128 * half : 128 * half + 128]
                block = block.T.astype(BF16).reshape(4, CH, 128)
                for t in range(4):
                    o_s[lax.bitwise_xor(me, 4 * half + t), at + q] = block[t]


def spread_kernel(pair_ref, t_ref, w_ref, g_s, v_s):
    odd = lax.rem(lax.axis_index("seq"), 2)
    lane = lax.broadcasted_iota(jnp.int32, (32, 128), 1)
    row = lax.broadcasted_iota(jnp.int32, (32, 128), 0)
    for j, at in ((0, odd), (1, 1 - odd)):
        at = pl.multiple_of(4 * CH * at, 4 * CH)
        g_s[pl.ds(at, 4 * CH)] = pair_ref[j, 4:8].astype(F32).reshape(4 * CH, 128)
    mine, other = pair_ref[0, 0:4].astype(F32), pair_ref[1, 0:4].astype(F32)
    firsts, seconds = jnp.where(odd == 1, mine, other), jnp.where(odd == 1, other, mine)
    for q in range(4):
        first, second = firsts[q], seconds[q]
        swapped = pltpu.roll(jnp.where(lane < 64, second, first), 64, 1)
        at = 2 * CH * q
        v_s[at : at + CH] = jnp.where(lane < 64, first, swapped)
        v_s[at + CH : at + 2 * CH] = jnp.where(lane < 64, swapped, second)
    stay_a = lane[:16] < 16 + 16 * (row[:16] % 8)
    stay_b = lane[:16] >= row[:16]

    def spread(c):
        prev = jnp.zeros((16, 128), F32)
        for g in range(8):
            taps = jnp.broadcast_to(g_s[pl.ds(CH * g + c, 1), :], (16, 128))
            rot = pltpu.roll(taps, 0, 1, stride=1, stride_axis=0)
            t_ref[c, 16 * g : 16 * g + 16] = jnp.where(stay_b, rot, prev).astype(BF16)
            prev = rot
        t_ref[c, 128:144] = jnp.where(stay_b, 0.0, prev).astype(BF16)
        for b in range(0, 8, 2):
            rots = []
            for j in range(2):
                vals = jnp.broadcast_to(v_s[pl.ds(CH * (b + j) + c, 1), :], (8, 128))
                rots.append(pltpu.roll(vals, 16, 1, stride=16, stride_axis=0))
            rot = jnp.concatenate(rots, 0)
            w_ref[c, 8 * b : 8 * b + 16] = jnp.where(stay_a, rot, 0.0).astype(BF16)
            w_ref[c, 64 + 8 * b : 80 + 8 * b] = jnp.where(stay_a, 0.0, rot).astype(BF16)

    def step(i, carry):
        for u in range(SPREAD_AT_ONCE):
            spread(i * SPREAD_AT_ONCE + u)
        return carry

    lax.fori_loop(0, CH // SPREAD_AT_ONCE, step, 0)


def conv_kernel(*refs):
    ts, ws, (y_ref, o_s, y_s) = refs[:4], refs[4:8], refs[8:]
    me = lax.axis_index("seq")
    z = lax.div(me, 2)
    for at in range(4):
        order = [at ^ chip for chip in range(4)]

        @pl.when(z == at)
        def _(order=order):
            convolve([ts[i] for i in order], [ws[i] for i in order], o_s, y_s)

    for s in range(PARTS):
        for q in range(4):
            at = PITCH * (4 * s + q)
            y_ref[lax.bitwise_xor(me, s), q] = y_s[at : at + CH].astype(BF16)


def convolve(ts, ws, o_s, y_s):
    lane = lax.broadcasted_iota(jnp.int32, (32, 128), 1)
    row = lax.broadcasted_iota(jnp.int32, (32, 128), 0)

    def multiply(c, u):
        right = [ts[0][c, 0:128]]
        for j in range(1, 4):
            first = ts[j][c, 0:16] + ts[j - 1][c, 128:144]
            right.append(jnp.concatenate([first, ts[j][c, 16:128]], 0))
        right = jnp.concatenate(
            [jnp.concatenate(right[0:2], 0), jnp.concatenate(right[2:4], 0)], 1
        )
        w = [ws[0][c, 0:64]] + [ws[j][c, 0:64] + ws[j - 1][c, 64:128] for j in range(1, 4)]
        zero = jnp.zeros((64, 128), BF16)
        left = jnp.concatenate(
            [jnp.concatenate([w[j], w[j - 1] if j else zero], 1) for j in range(4)], 0
        )
        o_s[u] = jnp.dot(left, right, preferred_element_type=F32)

    def collect(c, u):
        here = jnp.zeros((32, 128), F32)
        late = jnp.zeros((32, 128), F32)
        for b in range(8):
            r = []
            for j in range(4):
                part = o_s[u, 64 * j + 8 * b : 64 * j + 8 * b + 8, :128]
                if j >= 2:
                    at = 64 * (j - 2) + 8 * b
                    part = part + o_s[u, at : at + 8, 128:]
                r.append(part)
            r = jnp.concatenate(r, 0)
            if b:
                r = pltpu.roll(r, 16 * b, 1)
                over = lane < 16 * b
                late = late + jnp.where(over, r, 0.0)
                r = jnp.where(over, 0.0, r)
            here = here + r
        late = jnp.where(row == 0, 0.0, pltpu.roll(late, 1, 0))
        y_s[pl.ds(c, 32, stride=PITCH), :] = here + late

    for u in range(AT_ONCE):
        multiply(u, u)

    def step(i, carry):
        for u in range(AT_ONCE):
            collect((i - 1) * AT_ONCE + u, u)
            multiply(i * AT_ONCE + u, u)
        return carry

    lax.fori_loop(1, CH // AT_ONCE, step, 0)
    for u in range(AT_ONCE):
        collect(CH - AT_ONCE + u, u)


def gate_kernel(*refs):
    y_refs, (d_ref, g_ref, o_ref, y_s, o_s, sem) = refs[:-6], refs[-6:]
    piece = pieces_of(y_refs)
    me = lax.axis_index("seq")
    for s in range(PARTS):
        y_s[lax.bitwise_xor(me, s)] = piece(s, 0, 4)
    copies = []
    for q in range(4):
        pos = slice(128 * q, 128 * q + 128)
        for half in range(2):
            ch = slice(128 * half, 128 * half + 128)
            y = y_s[4 * half : 4 * half + 4, q].reshape(128, 128).astype(F32).T
            out = g_ref[pos, ch].astype(F32) * (y + d_ref[pos, ch])
            o_s[pos, ch] = out.astype(BF16)
        copies.append(pltpu.make_async_copy(o_s.at[pos], o_ref.at[pos], sem.at[q]))
        copies[-1].start()
    for copy in copies:
        copy.wait()


def call(kernel, out, scratch=(), limit=VMEM, **more):
    return pl.pallas_call(
        kernel,
        out_shape=out,
        scratch_shapes=scratch,
        compiler_params=pltpu.CompilerParams(vmem_limit_bytes=limit),
        **more,
    )


def swap(x, j):
    return lax.ppermute(x, "seq", [(i, i ^ j) for i in range(PARTS)])


def exchange(x):
    x = x.reshape(4, 2, *x.shape[1:])
    other = swap(x[:, 1], 1)
    pairs = jnp.stack([x[:, 0], other], 1)
    return [swap(pairs[i], 2 * i) if i else pairs[i] for i in ORDER]


def on_device(key_branch, value_branch, gate_branch, conv_filter, skip_gain):
    product = key_branch.astype(F32) * value_branch.astype(F32)
    product = lax.reduce_precision(product, 8, 7)
    direct = skip_gain[None, :] * product
    product = product.astype(BF16)
    sent = call(pack_kernel, jax.ShapeDtypeStruct((PARTS, 8, CH, 128), BF16))(
        product, conv_filter
    )
    pairs = dict(zip(ORDER, exchange(sent)))
    tiles = [None] * 4
    for last, i in ((None, 0), (0, 2), (2, 3), (3, 1)):
        pair = pairs[i]
        if last is not None:
            pair, tiles[last] = lax.optimization_barrier((pair, tiles[last]))
        tiles[i] = call(
            spread_kernel,
            [
                jax.ShapeDtypeStruct((CH, 144, 128), BF16),
                jax.ShapeDtypeStruct((CH, 128, 128), BF16),
            ],
            [pltpu.VMEM((8 * CH, 128), F32)] * 2,
            cost_estimate=pl.CostEstimate(flops=10**9, bytes_accessed=10**7, transcendentals=0),
        )(pair)
    mixed = call(
        conv_kernel,
        jax.ShapeDtypeStruct((PARTS, 4, CH, 128), BF16),
        [
            pltpu.VMEM((AT_ONCE, 256, 256), F32),
            pltpu.VMEM((32 * PITCH, 128), F32),
        ],
    )(*[t for t, _ in tiles], *[w for _, w in tiles])
    back = exchange(mixed)
    return call(
        gate_kernel,
        jax.ShapeDtypeStruct((512, 256), BF16),
        [
            pltpu.VMEM((PARTS, 4, CH, 128), BF16),
            pltpu.VMEM((512, 256), BF16),
            pltpu.SemaphoreType.DMA((4,)),
        ],
        out_specs=pl.BlockSpec(memory_space=pl.ANY),
    )(*back, direct, gate_branch)


def solution(mesh):
    in_specs = (P("seq", "ch"), P("seq", "ch"), P("seq", "ch"), P("seq", "ch"), P("ch"))
    return jax.shard_map(
        on_device, mesh=mesh, in_specs=in_specs, out_specs=P("seq", "ch"), check_vma=False
    )
```

time: 28.4 us -> 27.8 us (0.979)
  waiting for transfers between devices: 13.5 us -> 11.7 us
  Pallas kernels: 4.45 us -> 5.3 us
  starting transfers between devices: 9 us -> 9.31 us
    pallas_call x0 -> x4, Pallas kernels: none -> 2.05 us  [on_device(): call(spread_kernel, [jax.ShapeDtypeStruct((CH, 144, 128), BF16), jax.Shap...]
    ppermute x8, waiting for transfers between devices: 13.5 us -> 11.7 us  [swap(): return lax.ppermute(x, 'seq', [(i, i ^ j) for i in range(PARTS)])]
    pallas_call x1, Pallas kernels: 3.37 us -> 2.17 us  [on_device(): call(conv_kernel, jax.ShapeDtypeStruct((PARTS, 4, CH, 128), BF16), [pltpu...]
    ppermute x8, starting transfers between devices: 9 us -> 9.31 us  [swap(): return lax.ppermute(x, 'seq', [(i, i ^ j) for i in range(PARTS)])]
  transfers between devices with their start and end apart: 8 -> 8, of which waited for: 8 -> 7; matrix products, arithmetic and copies ran while one was open for 0% -> 0% of each run, Pallas kernels for 0% -> 6%
where the time goes in v5:
time: 27.8 us; the launch traced here: 27.7 us
  waiting for transfers between devices  11.7 us (42%)
  starting transfers between devices  9.31 us (33%)
  Pallas kernels  5.3 us (19%)
  other arithmetic  1.24 us (4%)
    ppermute x8, waiting for transfers between devices, swap(): return lax.ppermute(x, 'seq', [(i, i ^ j) for i in range(PARTS)])  11.7 us
    ppermute x8, starting transfers between devices, swap(): return lax.ppermute(x, 'seq', [(i, i ^ j) for i in range(PARTS)])  9.31 us
    pallas_call x1, Pallas kernels, on_device(): call(conv_kernel, jax.ShapeDtypeStruct((PARTS, 4, CH, 128), BF16), [pltpu...  2.17 us
    pallas_call x4, Pallas kernels, on_device(): call(spread_kernel, [jax.ShapeDtypeStruct((CH, 144, 128), BF16), jax.Shap...  2.05 us
    mul x1, other arithmetic, on_device(): direct = skip_gain[None, :] * product  1.17 us
    pallas_call x1, Pallas kernels, on_device(): call(gate_kernel, jax.ShapeDtypeStruct((512, 256), BF16), [pltpu.VMEM((PA...  0.86 us
  transfers between devices with their start and end apart: 8, of which 7 were waited for; matrix products, arithmetic and copies ran while one was open for 0% of the time, Pallas kernels for 6%

profile of v5, /device:TPU:0, one launch (start us, length us, event | category | flops | bytes accessed | tf_op | source)
XLA Modules:
  0.0 27.7 jit_solution(17868329490050016276)
XLA Ops:
  0.0 0.0 copy-start.1
  0.0 1.2 %fusion = (f32[512,256]{1,0:T(8,128)S(1)}, bf16[512,256]{1,0:T(8,128)(2,1)S(1)}) fusion(bf16[512,256]{1,0:T(8,128)(2,1)} %param.6, bf16[512,256]{1,0:T(8,128)(2,1)} %param.5, f32[256]{0:T(256)} %param.9), kind=kLoop, calls=%fused_computation.7 | loop fusion | flops 786432 | bytes 1311744 | tf_op jit(solution)/shard_map/mul | solution.py:199
  1.2 0.0 copy-done.1
  1.2 0.2 shard_map.55
  1.5 0.1 collective-permute-start
  1.6 1.5 %collective-permute-done = bf16[4,8,32,128]{3,2,1,0:T(8,128)(2,1)S(1)} collective-permute-done((bf16[4,8,32,128]{3,2,1,0:T(8,128)(2,1)S(1)}, bf16[4,8,32,128]{3,2,1,0:T(8,128)(2,1)S(1)}, u32[]{:S(2)}, u32[]{:S(2)}) %collective-permute-start) | collective-permute-done | bytes 262176 | tf_op jit(solution)/shard_map/ppermute | solution.py:186
  3.1 4.0 %collective-permute-start.1 = (bf16[2,8,32,128]{3,2,1,0:T(8,128)(2,1)S(1)}, bf16[2,8,32,128]{3,2,1,0:T(8,128)(2,1)S(1)}, u32[]{:S(2)}, u32[]{:S(2)}) collective-permute-start(bf16[2,8,32,128]{3,2,1,0:T(8,128)(2,1)S(1)} %get-tuple-element.42), channel_id=1, source_target_pairs={{0,64},{16,80},{32,96},{48,112},{64,0},{80,16},{96,32},{112,48},{1... | collective-permute-start | bytes 393224 | tf_op jit(solution)/shard_map/ppermute | solution.py:186
  7.2 0.7 %collective-permute-start.3 = (bf16[2,8,32,128]{3,2,1,0:T(8,128)(2,1)S(1)}, bf16[2,8,32,128]{3,2,1,0:T(8,128)(2,1)S(1)}, u32[]{:S(2)}, u32[]{:S(2)}) collective-permute-start(bf16[2,8,32,128]{3,2,1,0:T(8,128)(2,1)S(1)} %get-tuple-element.41), channel_id=1, source_target_pairs={{0,96},{16,112},{32,64},{48,80},{64,32},{80,48},{96,0},{112,16},{1... | collective-permute-start | bytes 393224 | tf_op jit(solution)/shard_map/ppermute | solution.py:186
  7.9 0.3 %collective-permute-start.2 = (bf16[2,8,32,128]{3,2,1,0:T(8,128)(2,1)S(1)}, bf16[2,8,32,128]{3,2,1,0:T(8,128)(2,1)S(1)}, u32[]{:S(2)}, u32[]{:S(2)}) collective-permute-start(bf16[2,8,32,128]{3,2,1,0:T(8,128)(2,1)S(1)} %get-tuple-element.44), channel_id=1, source_target_pairs={{0,32},{16,48},{32,0},{48,16},{64,96},{80,112},{96,64},{112,80},{1... | collective-permute-start | bytes 393224 | tf_op jit(solution)/shard_map/ppermute | solution.py:186
  8.2 0.5 %shard_map.56 = (bf16[32,144,128]{2,1,0:T(8,128)(2,1)S(1)}, bf16[32,128,128]{2,1,0:T(8,128)(2,1)S(1)}) custom-call(bf16[2,8,32,128]{3,2,1,0:T(8,128)(2,1)S(1)} %get-tuple-element.43.pair_ref), custom_call_target="tpu_custom_call" | custom-call | flops 1000000000 | bytes 10000000 | tf_op jit(solution)/shard_map/pallas_call | solution.py:210
  8.7 2.4 %collective-permute-done.1.pair_ref = bf16[2,8,32,128]{3,2,1,0:T(8,128)(2,1)S(1)} collective-permute-done((bf16[2,8,32,128]{3,2,1,0:T(8,128)(2,1)S(1)}, bf16[2,8,32,128]{3,2,1,0:T(8,128)(2,1)S(1)}, u32[]{:S(2)}, u32[]{:S(2)}) %collective-permute-start.1) | collective-permute-done | bytes 131104 | tf_op jit(solution)/shard_map/ppermute | solution.py:186
  11.1 0.5 %shard_map.57 = (bf16[32,144,128]{2,1,0:T(8,128)(2,1)S(1)}, bf16[32,128,128]{2,1,0:T(8,128)(2,1)S(1)}) custom-call(bf16[2,8,32,128]{3,2,1,0:T(8,128)(2,1)S(1)} %collective-permute-done.1.pair_ref), custom_call_target="tpu_custom_call" | custom-call | flops 1000000000 | bytes 10000000 | tf_op jit(solution)/shard_map/pallas_call | solution.py:210
  11.6 2.2 %collective-permute-done.3.pair_ref = bf16[2,8,32,128]{3,2,1,0:T(8,128)(2,1)S(1)} collective-permute-done((bf16[2,8,32,128]{3,2,1,0:T(8,128)(2,1)S(1)}, bf16[2,8,32,128]{3,2,1,0:T(8,128)(2,1)S(1)}, u32[]{:S(2)}, u32[]{:S(2)}) %collective-permute-start.3) | collective-permute-done | bytes 131104 | tf_op jit(solution)/shard_map/ppermute | solution.py:186
  13.8 0.5 %shard_map.58 = (bf16[32,144,128]{2,1,0:T(8,128)(2,1)S(1)}, bf16[32,128,128]{2,1,0:T(8,128)(2,1)S(1)}) custom-call(bf16[2,8,32,128]{3,2,1,0:T(8,128)(2,1)S(1)} %collective-permute-done.3.pair_ref), custom_call_target="tpu_custom_call" | custom-call | flops 1000000000 | bytes 10000000 | tf_op jit(solution)/shard_map/pallas_call | solution.py:210
  14.3 0.3 collective-permute-done.2.pair_ref
  14.5 0.5 %shard_map.59 = (bf16[32,144,128]{2,1,0:T(8,128)(2,1)S(1)}, bf16[32,128,128]{2,1,0:T(8,128)(2,1)S(1)}) custom-call(bf16[2,8,32,128]{3,2,1,0:T(8,128)(2,1)S(1)} %collective-permute-done.2.pair_ref), custom_call_target="tpu_custom_call" | custom-call | flops 1000000000 | bytes 10000000 | tf_op jit(solution)/shard_map/pallas_call | solution.py:210
  15.1 2.2 %shard_map.60 = bf16[8,4,32,128]{3,2,1,0:T(8,128)(2,1)S(1)} custom-call(bf16[32,144,128]{2,1,0:T(8,128)(2,1)S(1)} %get-tuple-element.24.refs_0_, bf16[32,144,128]{2,1,0:T(8,128)(2,1)S(1)} %get-tuple-element.32.refs_1_, bf16[32,144,128]{2,1,0:T(8,128)(2,1)S(1)} %get-tuple-element.33.refs_2_, bf16[32,144,128]{2,1,0:T(8,128)(2,1)S(1)} %get-tuple-element.34.refs_3_, ...), custom_call_target="tpu_custom_call" | custom-call | tf_op jit(solution)/shard_map/pallas_call | solution.py:219
  17.2 0.0 copy-start
  17.3 0.1 collective-permute-start.4
  17.4 1.3 %collective-permute-done.4 = bf16[4,4,32,128]{3,2,1,0:T(8,128)(2,1)S(1)} collective-permute-done((bf16[4,4,32,128]{3,2,1,0:T(8,128)(2,1)S(1)}, bf16[4,4,32,128]{3,2,1,0:T(8,128)(2,1)S(1)}, u32[]{:S(2)}, u32[]{:S(2)}) %collective-permute-start.4) | collective-permute-done | bytes 131104 | tf_op jit(solution)/shard_map/ppermute | solution.py:186
  18.7 2.6 %collective-permute-start.7 = (bf16[2,4,32,128]{3,2,1,0:T(8,128)(2,1)S(1)}, bf16[2,4,32,128]{3,2,1,0:T(8,128)(2,1)S(1)}, u32[]{:S(2)}, u32[]{:S(2)}) collective-permute-start(bf16[2,4,32,128]{3,2,1,0:T(8,128)(2,1)S(1)} %get-tuple-element.47), channel_id=1, source_target_pairs={{0,64},{16,80},{32,96},{48,112},{64,0},{80,16},{96,32},{112,48},{1... | collective-permute-start | bytes 196616 | tf_op jit(solution)/shard_map/ppermute | solution.py:186
  21.4 1.2 %collective-permute-start.5 = (bf16[2,4,32,128]{3,2,1,0:T(8,128)(2,1)S(1)}, bf16[2,4,32,128]{3,2,1,0:T(8,128)(2,1)S(1)}, u32[]{:S(2)}, u32[]{:S(2)}) collective-permute-start(bf16[2,4,32,128]{3,2,1,0:T(8,128)(2,1)S(1)} %get-tuple-element.49), channel_id=1, source_target_pairs={{0,96},{16,112},{32,64},{48,80},{64,32},{80,48},{96,0},{112,16},{1... | collective-permute-start | bytes 196616 | tf_op jit(solution)/shard_map/ppermute | solution.py:186
  22.5 0.3 %collective-permute-start.6 = (bf16[2,4,32,128]{3,2,1,0:T(8,128)(2,1)S(1)}, bf16[2,4,32,128]{3,2,1,0:T(8,128)(2,1)S(1)}, u32[]{:S(2)}, u32[]{:S(2)}) collective-permute-start(bf16[2,4,32,128]{3,2,1,0:T(8,128)(2,1)S(1)} %get-tuple-element.50), channel_id=1, source_target_pairs={{0,32},{16,48},{32,0},{48,16},{64,96},{80,112},{96,64},{112,80},{1... | collective-permute-start | bytes 196616 | tf_op jit(solution)/shard_map/ppermute | solution.py:186
  22.8 1.8 %collective-permute-done.7.refs_3_ = bf16[2,4,32,128]{3,2,1,0:T(8,128)(2,1)S(1)} collective-permute-done((bf16[2,4,32,128]{3,2,1,0:T(8,128)(2,1)S(1)}, bf16[2,4,32,128]{3,2,1,0:T(8,128)(2,1)S(1)}, u32[]{:S(2)}, u32[]{:S(2)}) %collective-permute-start.7) | collective-permute-done | bytes 65568 | tf_op jit(solution)/shard_map/ppermute | solution.py:186
  24.6 2.3 %collective-permute-done.5.refs_1_ = bf16[2,4,32,128]{3,2,1,0:T(8,128)(2,1)S(1)} collective-permute-done((bf16[2,4,32,128]{3,2,1,0:T(8,128)(2,1)S(1)}, bf16[2,4,32,128]{3,2,1,0:T(8,128)(2,1)S(1)}, u32[]{:S(2)}, u32[]{:S(2)}) %collective-permute-start.5) | collective-permute-done | bytes 65568 | tf_op jit(solution)/shard_map/ppermute | solution.py:186
  26.9 0.0 collective-permute-done.6.refs_2_
  26.9 0.0 copy-done
  26.9 0.9 %shard_map.61 = bf16[512,256]{1,0:T(8,128)(2,1)} custom-call(bf16[2,4,32,128]{3,2,1,0:T(8,128)(2,1)S(1)} %get-tuple-element.48.refs_0_, bf16[2,4,32,128]{3,2,1,0:T(8,128)(2,1)S(1)} %collective-permute-done.5.refs_1_, bf16[2,4,32,128]{3,2,1,0:T(8,128)(2,1)S(1)} %collective-permute-done.6.refs_2_, bf16[2,4,32,128]{3,2,1,0:T(8,128)(2,1)S(1)} %collective-permute-done.7.refs_3_, ...), custom_call_target="tpu_custom_call" | custom-call | tf_op jit(solution)/shard_map/pallas_call | solution.py:228
  (4 shorter events, 0.1 us)
Async XLA Ops:
  0.0 1.2 %copy-start.1 = (bf16[512,256]{1,0:T(8,128)(2,1)S(1)}, bf16[512,256]{1,0:T(8,128)(2,1)}, u32[]{:S(2)}) copy-start(bf16[512,256]{1,0:T(8,128)(2,1)} %f_ref.1) | copy-start | bytes 786436
  1.5 1.6 %collective-permute-start = (bf16[4,8,32,128]{3,2,1,0:T(8,128)(2,1)S(1)}, bf16[4,8,32,128]{3,2,1,0:T(8,128)(2,1)S(1)}, u32[]{:S(2)}, u32[]{:S(2)}) collective-permute-start(bf16[4,8,32,128]{3,2,1,0:T(8,128)(2,1)S(1)} %get-tuple-element.45), channel_id=1, source_target_pairs={{0,16},{16,0},{32,48},{48,32},{64,80},{80,64},{96,112},{112,96},{1... | collective-permute-start | bytes 786440 | tf_op jit(solution)/shard_map/ppermute | solution.py:186
  3.1 7.9 %collective-permute-start.1 = (bf16[2,8,32,128]{3,2,1,0:T(8,128)(2,1)S(1)}, bf16[2,8,32,128]{3,2,1,0:T(8,128)(2,1)S(1)}, u32[]{:S(2)}, u32[]{:S(2)}) collective-permute-start(bf16[2,8,32,128]{3,2,1,0:T(8,128)(2,1)S(1)} %get-tuple-element.42), channel_id=1, source_target_pairs={{0,64},{16,80},{32,96},{48,112},{64,0},{80,16},{96,32},{112,48},{1... | collective-permute-start | bytes 393224 | tf_op jit(solution)/shard_map/ppermute | solution.py:186
  7.2 6.6 %collective-permute-start.3 = (bf16[2,8,32,128]{3,2,1,0:T(8,128)(2,1)S(1)}, bf16[2,8,32,128]{3,2,1,0:T(8,128)(2,1)S(1)}, u32[]{:S(2)}, u32[]{:S(2)}) collective-permute-start(bf16[2,8,32,128]{3,2,1,0:T(8,128)(2,1)S(1)} %get-tuple-element.41), channel_id=1, source_target_pairs={{0,96},{16,112},{32,64},{48,80},{64,32},{80,48},{96,0},{112,16},{1... | collective-permute-start | bytes 393224 | tf_op jit(solution)/shard_map/ppermute | solution.py:186
  7.9 6.7 %collective-permute-start.2 = (bf16[2,8,32,128]{3,2,1,0:T(8,128)(2,1)S(1)}, bf16[2,8,32,128]{3,2,1,0:T(8,128)(2,1)S(1)}, u32[]{:S(2)}, u32[]{:S(2)}) collective-permute-start(bf16[2,8,32,128]{3,2,1,0:T(8,128)(2,1)S(1)} %get-tuple-element.44), channel_id=1, source_target_pairs={{0,32},{16,48},{32,0},{48,16},{64,96},{80,112},{96,64},{112,80},{1... | collective-permute-start | bytes 393224 | tf_op jit(solution)/shard_map/ppermute | solution.py:186
  17.2 9.6 %copy-start = (bf16[512,256]{1,0:T(8,128)(2,1)S(1)}, bf16[512,256]{1,0:T(8,128)(2,1)}, u32[]{:S(2)}) copy-start(bf16[512,256]{1,0:T(8,128)(2,1)} %refs_5_.1) | copy-start | bytes 786436
  17.3 1.4 %collective-permute-start.4 = (bf16[4,4,32,128]{3,2,1,0:T(8,128)(2,1)S(1)}, bf16[4,4,32,128]{3,2,1,0:T(8,128)(2,1)S(1)}, u32[]{:S(2)}, u32[]{:S(2)}) collective-permute-start(bf16[4,4,32,128]{3,2,1,0:T(8,128)(2,1)S(1)} %get-tuple-element.51), channel_id=1, source_target_pairs={{0,16},{16,0},{32,48},{48,32},{64,80},{80,64},{96,112},{112,96},{1... | collective-permute-start | bytes 393224 | tf_op jit(solution)/shard_map/ppermute | solution.py:186
  18.7 5.8 %collective-permute-start.7 = (bf16[2,4,32,128]{3,2,1,0:T(8,128)(2,1)S(1)}, bf16[2,4,32,128]{3,2,1,0:T(8,128)(2,1)S(1)}, u32[]{:S(2)}, u32[]{:S(2)}) collective-permute-start(bf16[2,4,32,128]{3,2,1,0:T(8,128)(2,1)S(1)} %get-tuple-element.47), channel_id=1, source_target_pairs={{0,64},{16,80},{32,96},{48,112},{64,0},{80,16},{96,32},{112,48},{1... | collective-permute-start | bytes 196616 | tf_op jit(solution)/shard_map/ppermute | solution.py:186
  21.4 5.5 %collective-permute-start.5 = (bf16[2,4,32,128]{3,2,1,0:T(8,128)(2,1)S(1)}, bf16[2,4,32,128]{3,2,1,0:T(8,128)(2,1)S(1)}, u32[]{:S(2)}, u32[]{:S(2)}) collective-permute-start(bf16[2,4,32,128]{3,2,1,0:T(8,128)(2,1)S(1)} %get-tuple-element.49), channel_id=1, source_target_pairs={{0,96},{16,112},{32,64},{48,80},{64,32},{80,48},{96,0},{112,16},{1... | collective-permute-start | bytes 196616 | tf_op jit(solution)/shard_map/ppermute | solution.py:186
  22.5 4.3 %collective-permute-start.6 = (bf16[2,4,32,128]{3,2,1,0:T(8,128)(2,1)S(1)}, bf16[2,4,32,128]{3,2,1,0:T(8,128)(2,1)S(1)}, u32[]{:S(2)}, u32[]{:S(2)}) collective-permute-start(bf16[2,4,32,128]{3,2,1,0:T(8,128)(2,1)S(1)} %get-tuple-element.50), channel_id=1, source_target_pairs={{0,32},{16,48},{32,0},{48,16},{64,96},{80,112},{96,64},{112,80},{1... | collective-permute-start | bytes 196616 | tf_op jit(solution)/shard_map/ppermute | solution.py:186

commit v6 on v5

--- a/solution.py
+++ b/solution.py
@@ -11,6 +11,7 @@
 CH = 32
 ORDER = (0, 3, 1, 2)
 AT_ONCE = 8
+BEHIND = 4
 SPREAD_AT_ONCE = 32
 PITCH = 40
 VMEM = 24 * 1024 * 1024
@@ -138,18 +139,12 @@
         late = jnp.where(row == 0, 0.0, pltpu.roll(late, 1, 0))
         y_s[pl.ds(c, 32, stride=PITCH), :] = here + late
 
-    for u in range(AT_ONCE):
-        multiply(u, u)
-
-    def step(i, carry):
-        for u in range(AT_ONCE):
-            collect((i - 1) * AT_ONCE + u, u)
-            multiply(i * AT_ONCE + u, u)
-        return carry
-
-    lax.fori_loop(1, CH // AT_ONCE, step, 0)
-    for u in range(AT_ONCE):
-        collect(CH - AT_ONCE + u, u)
+    for c in range(CH):
+        multiply(c, c % AT_ONCE)
+        if c >= BEHIND:
+            collect(c - BEHIND, (c - BEHIND) % AT_ONCE)
+    for c in range(CH - BEHIND, CH):
+        collect(c, c % AT_ONCE)
 
 
 def gate_kernel(*refs):

time: 27.8 us -> 27.1 us (0.975)
  Pallas kernels: 5.3 us -> 4.6 us
    pallas_call x1, Pallas kernels: 2.17 us -> 1.47 us  [on_device(): call(conv_kernel, jax.ShapeDtypeStruct((PARTS, 4, CH, 128), BF16), [pltpu...]
where the time goes in v6:
time: 27.1 us; the launch traced here: 27 us
  waiting for transfers between devices  11.7 us (43%)
  starting transfers between devices  9.31 us (34%)
  Pallas kernels  4.6 us (17%)
  other arithmetic  1.24 us (5%)
    ppermute x8, waiting for transfers between devices, swap(): return lax.ppermute(x, 'seq', [(i, i ^ j) for i in range(PARTS)])  11.7 us
    ppermute x8, starting transfers between devices, swap(): return lax.ppermute(x, 'seq', [(i, i ^ j) for i in range(PARTS)])  9.31 us
    pallas_call x4, Pallas kernels, on_device(): call(spread_kernel, [jax.ShapeDtypeStruct((CH, 144, 128), BF16), jax.Shap...  2.05 us
    pallas_call x1, Pallas kernels, on_device(): call(conv_kernel, jax.ShapeDtypeStruct((PARTS, 4, CH, 128), BF16), [pltpu...  1.47 us
    mul x1, other arithmetic, on_device(): direct = skip_gain[None, :] * product  1.17 us
    pallas_call x1, Pallas kernels, on_device(): call(gate_kernel, jax.ShapeDtypeStruct((512, 256), BF16), [pltpu.VMEM((PA...  0.86 us
  transfers between devices with their start and end apart: 8, of which 7 were waited for; matrix products, arithmetic and copies ran while one was open for 0% of the time, Pallas kernels for 6%

profile of v6, /device:TPU:0, one launch (start us, length us, event | category | flops | bytes accessed | tf_op | source)
XLA Modules:
  0.0 27.0 jit_solution(15468013577938031943)
XLA Ops:
  0.0 0.0 copy-start.1
  0.0 1.2 %fusion = (f32[512,256]{1,0:T(8,128)S(1)}, bf16[512,256]{1,0:T(8,128)(2,1)S(1)}) fusion(bf16[512,256]{1,0:T(8,128)(2,1)} %param.6, bf16[512,256]{1,0:T(8,128)(2,1)} %param.5, f32[256]{0:T(256)} %param.9), kind=kLoop, calls=%fused_computation.7 | loop fusion | flops 786432 | bytes 1311744 | tf_op jit(solution)/shard_map/mul | solution.py:194
  1.2 0.0 copy-done.1
  1.2 0.2 shard_map.55
  1.5 0.1 collective-permute-start
  1.6 1.5 %collective-permute-done = bf16[4,8,32,128]{3,2,1,0:T(8,128)(2,1)S(1)} collective-permute-done((bf16[4,8,32,128]{3,2,1,0:T(8,128)(2,1)S(1)}, bf16[4,8,32,128]{3,2,1,0:T(8,128)(2,1)S(1)}, u32[]{:S(2)}, u32[]{:S(2)}) %collective-permute-start) | collective-permute-done | bytes 262176 | tf_op jit(solution)/shard_map/ppermute | solution.py:181
  3.1 4.0 %collective-permute-start.1 = (bf16[2,8,32,128]{3,2,1,0:T(8,128)(2,1)S(1)}, bf16[2,8,32,128]{3,2,1,0:T(8,128)(2,1)S(1)}, u32[]{:S(2)}, u32[]{:S(2)}) collective-permute-start(bf16[2,8,32,128]{3,2,1,0:T(8,128)(2,1)S(1)} %get-tuple-element.42), channel_id=1, source_target_pairs={{0,64},{16,80},{32,96},{48,112},{64,0},{80,16},{96,32},{112,48},{1... | collective-permute-start | bytes 393224 | tf_op jit(solution)/shard_map/ppermute | solution.py:181
  7.2 0.7 %collective-permute-start.3 = (bf16[2,8,32,128]{3,2,1,0:T(8,128)(2,1)S(1)}, bf16[2,8,32,128]{3,2,1,0:T(8,128)(2,1)S(1)}, u32[]{:S(2)}, u32[]{:S(2)}) collective-permute-start(bf16[2,8,32,128]{3,2,1,0:T(8,128)(2,1)S(1)} %get-tuple-element.41), channel_id=1, source_target_pairs={{0,96},{16,112},{32,64},{48,80},{64,32},{80,48},{96,0},{112,16},{1... | collective-permute-start | bytes 393224 | tf_op jit(solution)/shard_map/ppermute | solution.py:181
  7.9 0.3 %collective-permute-start.2 = (bf16[2,8,32,128]{3,2,1,0:T(8,128)(2,1)S(1)}, bf16[2,8,32,128]{3,2,1,0:T(8,128)(2,1)S(1)}, u32[]{:S(2)}, u32[]{:S(2)}) collective-permute-start(bf16[2,8,32,128]{3,2,1,0:T(8,128)(2,1)S(1)} %get-tuple-element.44), channel_id=1, source_target_pairs={{0,32},{16,48},{32,0},{48,16},{64,96},{80,112},{96,64},{112,80},{1... | collective-permute-start | bytes 393224 | tf_op jit(solution)/shard_map/ppermute | solution.py:181
  8.2 0.5 %shard_map.56 = (bf16[32,144,128]{2,1,0:T(8,128)(2,1)S(1)}, bf16[32,128,128]{2,1,0:T(8,128)(2,1)S(1)}) custom-call(bf16[2,8,32,128]{3,2,1,0:T(8,128)(2,1)S(1)} %get-tuple-element.43.pair_ref), custom_call_target="tpu_custom_call" | custom-call | flops 1000000000 | bytes 10000000 | tf_op jit(solution)/shard_map/pallas_call | solution.py:205
  8.7 2.4 %collective-permute-done.1.pair_ref = bf16[2,8,32,128]{3,2,1,0:T(8,128)(2,1)S(1)} collective-permute-done((bf16[2,8,32,128]{3,2,1,0:T(8,128)(2,1)S(1)}, bf16[2,8,32,128]{3,2,1,0:T(8,128)(2,1)S(1)}, u32[]{:S(2)}, u32[]{:S(2)}) %collective-permute-start.1) | collective-permute-done | bytes 131104 | tf_op jit(solution)/shard_map/ppermute | solution.py:181
  11.1 0.5 %shard_map.57 = (bf16[32,144,128]{2,1,0:T(8,128)(2,1)S(1)}, bf16[32,128,128]{2,1,0:T(8,128)(2,1)S(1)}) custom-call(bf16[2,8,32,128]{3,2,1,0:T(8,128)(2,1)S(1)} %collective-permute-done.1.pair_ref), custom_call_target="tpu_custom_call" | custom-call | flops 1000000000 | bytes 10000000 | tf_op jit(solution)/shard_map/pallas_call | solution.py:205
  11.6 2.2 %collective-permute-done.3.pair_ref = bf16[2,8,32,128]{3,2,1,0:T(8,128)(2,1)S(1)} collective-permute-done((bf16[2,8,32,128]{3,2,1,0:T(8,128)(2,1)S(1)}, bf16[2,8,32,128]{3,2,1,0:T(8,128)(2,1)S(1)}, u32[]{:S(2)}, u32[]{:S(2)}) %collective-permute-start.3) | collective-permute-done | bytes 131104 | tf_op jit(solution)/shard_map/ppermute | solution.py:181
  13.8 0.5 %shard_map.58 = (bf16[32,144,128]{2,1,0:T(8,128)(2,1)S(1)}, bf16[32,128,128]{2,1,0:T(8,128)(2,1)S(1)}) custom-call(bf16[2,8,32,128]{3,2,1,0:T(8,128)(2,1)S(1)} %collective-permute-done.3.pair_ref), custom_call_target="tpu_custom_call" | custom-call | flops 1000000000 | bytes 10000000 | tf_op jit(solution)/shard_map/pallas_call | solution.py:205
  14.3 0.3 collective-permute-done.2.pair_ref
  14.5 0.5 %shard_map.59 = (bf16[32,144,128]{2,1,0:T(8,128)(2,1)S(1)}, bf16[32,128,128]{2,1,0:T(8,128)(2,1)S(1)}) custom-call(bf16[2,8,32,128]{3,2,1,0:T(8,128)(2,1)S(1)} %collective-permute-done.2.pair_ref), custom_call_target="tpu_custom_call" | custom-call | flops 1000000000 | bytes 10000000 | tf_op jit(solution)/shard_map/pallas_call | solution.py:205
  15.1 1.5 %shard_map.60 = bf16[8,4,32,128]{3,2,1,0:T(8,128)(2,1)S(1)} custom-call(bf16[32,144,128]{2,1,0:T(8,128)(2,1)S(1)} %get-tuple-element.24.refs_0_, bf16[32,144,128]{2,1,0:T(8,128)(2,1)S(1)} %get-tuple-element.32.refs_1_, bf16[32,144,128]{2,1,0:T(8,128)(2,1)S(1)} %get-tuple-element.33.refs_2_, bf16[32,144,128]{2,1,0:T(8,128)(2,1)S(1)} %get-tuple-element.34.refs_3_, ...), custom_call_target="tpu_custom_call" | custom-call | tf_op jit(solution)/shard_map/pallas_call | solution.py:214
  16.5 0.0 copy-start
  16.6 0.1 collective-permute-start.4
  16.7 1.3 %collective-permute-done.4 = bf16[4,4,32,128]{3,2,1,0:T(8,128)(2,1)S(1)} collective-permute-done((bf16[4,4,32,128]{3,2,1,0:T(8,128)(2,1)S(1)}, bf16[4,4,32,128]{3,2,1,0:T(8,128)(2,1)S(1)}, u32[]{:S(2)}, u32[]{:S(2)}) %collective-permute-start.4) | collective-permute-done | bytes 131104 | tf_op jit(solution)/shard_map/ppermute | solution.py:181
  18.0 2.6 %collective-permute-start.7 = (bf16[2,4,32,128]{3,2,1,0:T(8,128)(2,1)S(1)}, bf16[2,4,32,128]{3,2,1,0:T(8,128)(2,1)S(1)}, u32[]{:S(2)}, u32[]{:S(2)}) collective-permute-start(bf16[2,4,32,128]{3,2,1,0:T(8,128)(2,1)S(1)} %get-tuple-element.47), channel_id=1, source_target_pairs={{0,64},{16,80},{32,96},{48,112},{64,0},{80,16},{96,32},{112,48},{1... | collective-permute-start | bytes 196616 | tf_op jit(solution)/shard_map/ppermute | solution.py:181
  20.7 1.2 %collective-permute-start.5 = (bf16[2,4,32,128]{3,2,1,0:T(8,128)(2,1)S(1)}, bf16[2,4,32,128]{3,2,1,0:T(8,128)(2,1)S(1)}, u32[]{:S(2)}, u32[]{:S(2)}) collective-permute-start(bf16[2,4,32,128]{3,2,1,0:T(8,128)(2,1)S(1)} %get-tuple-element.49), channel_id=1, source_target_pairs={{0,96},{16,112},{32,64},{48,80},{64,32},{80,48},{96,0},{112,16},{1... | collective-permute-start | bytes 196616 | tf_op jit(solution)/shard_map/ppermute | solution.py:181
  21.8 0.3 %collective-permute-start.6 = (bf16[2,4,32,128]{3,2,1,0:T(8,128)(2,1)S(1)}, bf16[2,4,32,128]{3,2,1,0:T(8,128)(2,1)S(1)}, u32[]{:S(2)}, u32[]{:S(2)}) collective-permute-start(bf16[2,4,32,128]{3,2,1,0:T(8,128)(2,1)S(1)} %get-tuple-element.50), channel_id=1, source_target_pairs={{0,32},{16,48},{32,0},{48,16},{64,96},{80,112},{96,64},{112,80},{1... | collective-permute-start | bytes 196616 | tf_op jit(solution)/shard_map/ppermute | solution.py:181
  22.1 1.8 %collective-permute-done.7.refs_3_ = bf16[2,4,32,128]{3,2,1,0:T(8,128)(2,1)S(1)} collective-permute-done((bf16[2,4,32,128]{3,2,1,0:T(8,128)(2,1)S(1)}, bf16[2,4,32,128]{3,2,1,0:T(8,128)(2,1)S(1)}, u32[]{:S(2)}, u32[]{:S(2)}) %collective-permute-start.7) | collective-permute-done | bytes 65568 | tf_op jit(solution)/shard_map/ppermute | solution.py:181
  23.9 2.3 %collective-permute-done.5.refs_1_ = bf16[2,4,32,128]{3,2,1,0:T(8,128)(2,1)S(1)} collective-permute-done((bf16[2,4,32,128]{3,2,1,0:T(8,128)(2,1)S(1)}, bf16[2,4,32,128]{3,2,1,0:T(8,128)(2,1)S(1)}, u32[]{:S(2)}, u32[]{:S(2)}) %collective-permute-start.5) | collective-permute-done | bytes 65568 | tf_op jit(solution)/shard_map/ppermute | solution.py:181
  26.1 0.0 collective-permute-done.6.refs_2_
  26.2 0.0 copy-done
  26.2 0.9 %shard_map.61 = bf16[512,256]{1,0:T(8,128)(2,1)} custom-call(bf16[2,4,32,128]{3,2,1,0:T(8,128)(2,1)S(1)} %get-tuple-element.48.refs_0_, bf16[2,4,32,128]{3,2,1,0:T(8,128)(2,1)S(1)} %collective-permute-done.5.refs_1_, bf16[2,4,32,128]{3,2,1,0:T(8,128)(2,1)S(1)} %collective-permute-done.6.refs_2_, bf16[2,4,32,128]{3,2,1,0:T(8,128)(2,1)S(1)} %collective-permute-done.7.refs_3_, ...), custom_call_target="tpu_custom_call" | custom-call | tf_op jit(solution)/shard_map/pallas_call | solution.py:223
  (4 shorter events, 0.1 us)
Async XLA Ops:
  0.0 1.2 %copy-start.1 = (bf16[512,256]{1,0:T(8,128)(2,1)S(1)}, bf16[512,256]{1,0:T(8,128)(2,1)}, u32[]{:S(2)}) copy-start(bf16[512,256]{1,0:T(8,128)(2,1)} %f_ref.1) | copy-start | bytes 786436
  1.5 1.6 %collective-permute-start = (bf16[4,8,32,128]{3,2,1,0:T(8,128)(2,1)S(1)}, bf16[4,8,32,128]{3,2,1,0:T(8,128)(2,1)S(1)}, u32[]{:S(2)}, u32[]{:S(2)}) collective-permute-start(bf16[4,8,32,128]{3,2,1,0:T(8,128)(2,1)S(1)} %get-tuple-element.45), channel_id=1, source_target_pairs={{0,16},{16,0},{32,48},{48,32},{64,80},{80,64},{96,112},{112,96},{1... | collective-permute-start | bytes 786440 | tf_op jit(solution)/shard_map/ppermute | solution.py:181
  3.1 7.9 %collective-permute-start.1 = (bf16[2,8,32,128]{3,2,1,0:T(8,128)(2,1)S(1)}, bf16[2,8,32,128]{3,2,1,0:T(8,128)(2,1)S(1)}, u32[]{:S(2)}, u32[]{:S(2)}) collective-permute-start(bf16[2,8,32,128]{3,2,1,0:T(8,128)(2,1)S(1)} %get-tuple-element.42), channel_id=1, source_target_pairs={{0,64},{16,80},{32,96},{48,112},{64,0},{80,16},{96,32},{112,48},{1... | collective-permute-start | bytes 393224 | tf_op jit(solution)/shard_map/ppermute | solution.py:181
  7.2 6.6 %collective-permute-start.3 = (bf16[2,8,32,128]{3,2,1,0:T(8,128)(2,1)S(1)}, bf16[2,8,32,128]{3,2,1,0:T(8,128)(2,1)S(1)}, u32[]{:S(2)}, u32[]{:S(2)}) collective-permute-start(bf16[2,8,32,128]{3,2,1,0:T(8,128)(2,1)S(1)} %get-tuple-element.41), channel_id=1, source_target_pairs={{0,96},{16,112},{32,64},{48,80},{64,32},{80,48},{96,0},{112,16},{1... | collective-permute-start | bytes 393224 | tf_op jit(solution)/shard_map/ppermute | solution.py:181
  7.9 6.7 %collective-permute-start.2 = (bf16[2,8,32,128]{3,2,1,0:T(8,128)(2,1)S(1)}, bf16[2,8,32,128]{3,2,1,0:T(8,128)(2,1)S(1)}, u32[]{:S(2)}, u32[]{:S(2)}) collective-permute-start(bf16[2,8,32,128]{3,2,1,0:T(8,128)(2,1)S(1)} %get-tuple-element.44), channel_id=1, source_target_pairs={{0,32},{16,48},{32,0},{48,16},{64,96},{80,112},{96,64},{112,80},{1... | collective-permute-start | bytes 393224 | tf_op jit(solution)/shard_map/ppermute | solution.py:181
  16.5 9.6 %copy-start = (bf16[512,256]{1,0:T(8,128)(2,1)S(1)}, bf16[512,256]{1,0:T(8,128)(2,1)}, u32[]{:S(2)}) copy-start(bf16[512,256]{1,0:T(8,128)(2,1)} %refs_5_.1) | copy-start | bytes 786436
  16.6 1.4 %collective-permute-start.4 = (bf16[4,4,32,128]{3,2,1,0:T(8,128)(2,1)S(1)}, bf16[4,4,32,128]{3,2,1,0:T(8,128)(2,1)S(1)}, u32[]{:S(2)}, u32[]{:S(2)}) collective-permute-start(bf16[4,4,32,128]{3,2,1,0:T(8,128)(2,1)S(1)} %get-tuple-element.51), channel_id=1, source_target_pairs={{0,16},{16,0},{32,48},{48,32},{64,80},{80,64},{96,112},{112,96},{1... | collective-permute-start | bytes 393224 | tf_op jit(solution)/shard_map/ppermute | solution.py:181
  18.0 5.8 %collective-permute-start.7 = (bf16[2,4,32,128]{3,2,1,0:T(8,128)(2,1)S(1)}, bf16[2,4,32,128]{3,2,1,0:T(8,128)(2,1)S(1)}, u32[]{:S(2)}, u32[]{:S(2)}) collective-permute-start(bf16[2,4,32,128]{3,2,1,0:T(8,128)(2,1)S(1)} %get-tuple-element.47), channel_id=1, source_target_pairs={{0,64},{16,80},{32,96},{48,112},{64,0},{80,16},{96,32},{112,48},{1... | collective-permute-start | bytes 196616 | tf_op jit(solution)/shard_map/ppermute | solution.py:181
  20.7 5.5 %collective-permute-start.5 = (bf16[2,4,32,128]{3,2,1,0:T(8,128)(2,1)S(1)}, bf16[2,4,32,128]{3,2,1,0:T(8,128)(2,1)S(1)}, u32[]{:S(2)}, u32[]{:S(2)}) collective-permute-start(bf16[2,4,32,128]{3,2,1,0:T(8,128)(2,1)S(1)} %get-tuple-element.49), channel_id=1, source_target_pairs={{0,96},{16,112},{32,64},{48,80},{64,32},{80,48},{96,0},{112,16},{1... | collective-permute-start | bytes 196616 | tf_op jit(solution)/shard_map/ppermute | solution.py:181
  21.8 4.3 %collective-permute-start.6 = (bf16[2,4,32,128]{3,2,1,0:T(8,128)(2,1)S(1)}, bf16[2,4,32,128]{3,2,1,0:T(8,128)(2,1)S(1)}, u32[]{:S(2)}, u32[]{:S(2)}) collective-permute-start(bf16[2,4,32,128]{3,2,1,0:T(8,128)(2,1)S(1)} %get-tuple-element.50), channel_id=1, source_target_pairs={{0,32},{16,48},{32,0},{48,16},{64,96},{80,112},{96,64},{112,80},{1... | collective-permute-start | bytes 196616 | tf_op jit(solution)/shard_map/ppermute | solution.py:181

commit v7 on v6

--- a/solution.py
+++ b/solution.py
@@ -9,7 +9,6 @@
 BF16 = jnp.bfloat16
 PARTS = 8
 CH = 32
-ORDER = (0, 3, 1, 2)
 AT_ONCE = 8
 BEHIND = 4
 SPREAD_AT_ONCE = 32
@@ -17,11 +16,8 @@
 VMEM = 24 * 1024 * 1024
 
 
-def pieces_of(refs):
-    def piece(j, low, high):
-        return refs[ORDER.index(j // 2)][j % 2, low:high]
-
-    return piece
+def slot_of(j):
+    return lax.select(j >= 6, j, lax.rem(j + 2, 6))
 
 
 def pack_kernel(p_ref, f_ref, o_s):
@@ -39,14 +35,19 @@
                     o_s[lax.bitwise_xor(me, 4 * half + t), at + q] = block[t]
 
 
-def spread_kernel(pair_ref, t_ref, w_ref, g_s, v_s):
+def both(refs):
+    return refs if len(refs) == 2 else (refs[0].at[0], refs[0].at[1])
+
+
+def spread_kernel(*refs):
+    pair, (t_ref, w_ref, g_s, v_s) = both(refs[:-4]), refs[-4:]
     odd = lax.rem(lax.axis_index("seq"), 2)
     lane = lax.broadcasted_iota(jnp.int32, (32, 128), 1)
     row = lax.broadcasted_iota(jnp.int32, (32, 128), 0)
     for j, at in ((0, odd), (1, 1 - odd)):
         at = pl.multiple_of(4 * CH * at, 4 * CH)
-        g_s[pl.ds(at, 4 * CH)] = pair_ref[j, 4:8].astype(F32).reshape(4 * CH, 128)
-    mine, other = pair_ref[0, 0:4].astype(F32), pair_ref[1, 0:4].astype(F32)
+        g_s[pl.ds(at, 4 * CH)] = pair[j][4:8].astype(F32).reshape(4 * CH, 128)
+    mine, other = pair[0][0:4].astype(F32), pair[1][0:4].astype(F32)
     firsts, seconds = jnp.where(odd == 1, mine, other), jnp.where(odd == 1, other, mine)
     for q in range(4):
         first, second = firsts[q], seconds[q]
@@ -96,7 +97,7 @@
     for s in range(PARTS):
         for q in range(4):
             at = PITCH * (4 * s + q)
-            y_ref[lax.bitwise_xor(me, s), q] = y_s[at : at + CH].astype(BF16)
+            y_ref[slot_of(lax.bitwise_xor(me, s)), q] = y_s[at : at + CH].astype(BF16)
 
 
 def convolve(ts, ws, o_s, y_s):
@@ -149,10 +150,10 @@
 
 def gate_kernel(*refs):
     y_refs, (d_ref, g_ref, o_ref, y_s, o_s, sem) = refs[:-6], refs[-6:]
-    piece = pieces_of(y_refs)
     me = lax.axis_index("seq")
+    pairs = [both(y_refs[i : i + n]) for i, n in ((0, 1), (1, 1), (2, 2), (4, 1))]
     for s in range(PARTS):
-        y_s[lax.bitwise_xor(me, s)] = piece(s, 0, 4)
+        y_s[lax.bitwise_xor(me, s)] = pairs[s // 2][s % 2][...]
     copies = []
     for q in range(4):
         pos = slice(128 * q, 128 * q + 128)
@@ -183,9 +184,21 @@
 
 def exchange(x):
     x = x.reshape(4, 2, *x.shape[1:])
-    other = swap(x[:, 1], 1)
-    pairs = jnp.stack([x[:, 0], other], 1)
-    return [swap(pairs[i], 2 * i) if i else pairs[i] for i in ORDER]
+    pairs = jnp.stack([x[:, 0], swap(x[:, 1], 1)], 1)
+    return [(pairs[0],)] + [(swap(pairs[i], 2 * i),) for i in range(1, 4)]
+
+
+def exchange_far_first(x):
+    x = x.reshape(4, 2, *x.shape[1:])
+    far = swap(x[0], 4)
+    other = swap(x[1:, 1], 1)
+    near = jnp.stack([x[1:, 0], other], 1)
+    return [
+        (near[0],),
+        (swap(near[1], 2),),
+        (far[0], swap(far[1], 1)),
+        (swap(near[2], 6),),
+    ]
 
 
 def on_device(key_branch, value_branch, gate_branch, conv_filter, skip_gain):
@@ -196,7 +209,7 @@
     sent = call(pack_kernel, jax.ShapeDtypeStruct((PARTS, 8, CH, 128), BF16))(
         product, conv_filter
     )
-    pairs = dict(zip(ORDER, exchange(sent)))
+    pairs = exchange(sent)
     tiles = [None] * 4
     for last, i in ((None, 0), (0, 2), (2, 3), (3, 1)):
         pair = pairs[i]
@@ -210,7 +223,7 @@
             ],
             [pltpu.VMEM((8 * CH, 128), F32)] * 2,
             cost_estimate=pl.CostEstimate(flops=10**9, bytes_accessed=10**7, transcendentals=0),
-        )(pair)
+        )(*pair)
     mixed = call(
         conv_kernel,
         jax.ShapeDtypeStruct((PARTS, 4, CH, 128), BF16),
@@ -219,7 +232,7 @@
             pltpu.VMEM((32 * PITCH, 128), F32),
         ],
     )(*[t for t, _ in tiles], *[w for _, w in tiles])
-    back = exchange(mixed)
+    back = exchange_far_first(mixed)
     return call(
         gate_kernel,
         jax.ShapeDtypeStruct((512, 256), BF16),
@@ -229,7 +242,7 @@
             pltpu.SemaphoreType.DMA((4,)),
         ],
         out_specs=pl.BlockSpec(memory_space=pl.ANY),
-    )(*back, direct, gate_branch)
+    )(*[y for pair in back for y in pair], direct, gate_branch)
 
 
 def solution(mesh):

time: 27.1 us -> 26.5 us (0.978)
  waiting for transfers between devices: 11.7 us -> 10.6 us
  starting transfers between devices: 9.31 us -> 9.73 us
    ppermute x8 -> x9, waiting for transfers between devices: 11.7 us -> 10.6 us  [swap(): return lax.ppermute(x, 'seq', [(i, i ^ j) for i in range(PARTS)])]
    ppermute x8 -> x9, starting transfers between devices: 9.31 us -> 9.73 us  [swap(): return lax.ppermute(x, 'seq', [(i, i ^ j) for i in range(PARTS)])]
  transfers between devices with their start and end apart: 8 -> 9, of which waited for: 7 -> 8; matrix products, arithmetic and copies ran while one was open for 0% -> 0% of each run, Pallas kernels for 6% -> 6%
where the time goes in v7:
time: 26.5 us; the launch traced here: 26.3 us
  waiting for transfers between devices  10.6 us (40%)
  starting transfers between devices  9.73 us (37%)
  Pallas kernels  4.6 us (17%)
  other arithmetic  1.24 us (5%)
    ppermute x9, waiting for transfers between devices, swap(): return lax.ppermute(x, 'seq', [(i, i ^ j) for i in range(PARTS)])  10.6 us
    ppermute x9, starting transfers between devices, swap(): return lax.ppermute(x, 'seq', [(i, i ^ j) for i in range(PARTS)])  9.73 us
    pallas_call x4, Pallas kernels, on_device(): call(spread_kernel, [jax.ShapeDtypeStruct((CH, 144, 128), BF16), jax.Shap...  2.05 us
    pallas_call x1, Pallas kernels, on_device(): call(conv_kernel, jax.ShapeDtypeStruct((PARTS, 4, CH, 128), BF16), [pltpu...  1.47 us
    mul x1, other arithmetic, on_device(): direct = skip_gain[None, :] * product  1.17 us
    pallas_call x1, Pallas kernels, on_device(): call(gate_kernel, jax.ShapeDtypeStruct((512, 256), BF16), [pltpu.VMEM((PA...  0.86 us
  transfers between devices with their start and end apart: 9, of which 8 were waited for; matrix products, arithmetic and copies ran while one was open for 0% of the time, Pallas kernels for 6%

profile of v7, /device:TPU:0, one launch (start us, length us, event | category | flops | bytes accessed | tf_op | source)
XLA Modules:
  0.0 26.3 jit_solution(10161109587333347217)
XLA Ops:
  0.0 0.0 copy-start.1
  0.0 1.2 %fusion = (f32[512,256]{1,0:T(8,128)S(1)}, bf16[512,256]{1,0:T(8,128)(2,1)S(1)}) fusion(bf16[512,256]{1,0:T(8,128)(2,1)} %param.6, bf16[512,256]{1,0:T(8,128)(2,1)} %param.5, f32[256]{0:T(256)} %param.9), kind=kLoop, calls=%fused_computation.7 | loop fusion | flops 786432 | bytes 1311744 | tf_op jit(solution)/shard_map/mul | solution.py:207
  1.2 0.0 copy-done.1
  1.2 0.2 shard_map.55
  1.5 0.1 collective-permute-start
  1.6 1.5 %collective-permute-done = bf16[4,8,32,128]{3,2,1,0:T(8,128)(2,1)S(1)} collective-permute-done((bf16[4,8,32,128]{3,2,1,0:T(8,128)(2,1)S(1)}, bf16[4,8,32,128]{3,2,1,0:T(8,128)(2,1)S(1)}, u32[]{:S(2)}, u32[]{:S(2)}) %collective-permute-start) | collective-permute-done | bytes 262176 | tf_op jit(solution)/shard_map/ppermute | solution.py:182
  3.1 4.0 %collective-permute-start.1 = (bf16[2,8,32,128]{3,2,1,0:T(8,128)(2,1)S(1)}, bf16[2,8,32,128]{3,2,1,0:T(8,128)(2,1)S(1)}, u32[]{:S(2)}, u32[]{:S(2)}) collective-permute-start(bf16[2,8,32,128]{3,2,1,0:T(8,128)(2,1)S(1)} %get-tuple-element.42), channel_id=1, source_target_pairs={{0,64},{16,80},{32,96},{48,112},{64,0},{80,16},{96,32},{112,48},{1... | collective-permute-start | bytes 393224 | tf_op jit(solution)/shard_map/ppermute | solution.py:182
  7.2 0.7 %collective-permute-start.3 = (bf16[2,8,32,128]{3,2,1,0:T(8,128)(2,1)S(1)}, bf16[2,8,32,128]{3,2,1,0:T(8,128)(2,1)S(1)}, u32[]{:S(2)}, u32[]{:S(2)}) collective-permute-start(bf16[2,8,32,128]{3,2,1,0:T(8,128)(2,1)S(1)} %get-tuple-element.41), channel_id=1, source_target_pairs={{0,96},{16,112},{32,64},{48,80},{64,32},{80,48},{96,0},{112,16},{1... | collective-permute-start | bytes 393224 | tf_op jit(solution)/shard_map/ppermute | solution.py:182
  7.9 0.3 %collective-permute-start.2 = (bf16[2,8,32,128]{3,2,1,0:T(8,128)(2,1)S(1)}, bf16[2,8,32,128]{3,2,1,0:T(8,128)(2,1)S(1)}, u32[]{:S(2)}, u32[]{:S(2)}) collective-permute-start(bf16[2,8,32,128]{3,2,1,0:T(8,128)(2,1)S(1)} %get-tuple-element.44), channel_id=1, source_target_pairs={{0,32},{16,48},{32,0},{48,16},{64,96},{80,112},{96,64},{112,80},{1... | collective-permute-start | bytes 393224 | tf_op jit(solution)/shard_map/ppermute | solution.py:182
  8.2 0.5 %shard_map.56 = (bf16[32,144,128]{2,1,0:T(8,128)(2,1)S(1)}, bf16[32,128,128]{2,1,0:T(8,128)(2,1)S(1)}) custom-call(bf16[2,8,32,128]{3,2,1,0:T(8,128)(2,1)S(1)} %get-tuple-element.43.refs_0_), custom_call_target="tpu_custom_call" | custom-call | flops 1000000000 | bytes 10000000 | tf_op jit(solution)/shard_map/pallas_call | solution.py:218
  8.7 2.4 %collective-permute-done.1.refs_0_ = bf16[2,8,32,128]{3,2,1,0:T(8,128)(2,1)S(1)} collective-permute-done((bf16[2,8,32,128]{3,2,1,0:T(8,128)(2,1)S(1)}, bf16[2,8,32,128]{3,2,1,0:T(8,128)(2,1)S(1)}, u32[]{:S(2)}, u32[]{:S(2)}) %collective-permute-start.1) | collective-permute-done | bytes 131104 | tf_op jit(solution)/shard_map/ppermute | solution.py:182
  11.1 0.5 %shard_map.57 = (bf16[32,144,128]{2,1,0:T(8,128)(2,1)S(1)}, bf16[32,128,128]{2,1,0:T(8,128)(2,1)S(1)}) custom-call(bf16[2,8,32,128]{3,2,1,0:T(8,128)(2,1)S(1)} %collective-permute-done.1.refs_0_), custom_call_target="tpu_custom_call" | custom-call | flops 1000000000 | bytes 10000000 | tf_op jit(solution)/shard_map/pallas_call | solution.py:218
  11.6 2.2 %collective-permute-done.3.refs_0_ = bf16[2,8,32,128]{3,2,1,0:T(8,128)(2,1)S(1)} collective-permute-done((bf16[2,8,32,128]{3,2,1,0:T(8,128)(2,1)S(1)}, bf16[2,8,32,128]{3,2,1,0:T(8,128)(2,1)S(1)}, u32[]{:S(2)}, u32[]{:S(2)}) %collective-permute-start.3) | collective-permute-done | bytes 131104 | tf_op jit(solution)/shard_map/ppermute | solution.py:182
  13.8 0.5 %shard_map.58 = (bf16[32,144,128]{2,1,0:T(8,128)(2,1)S(1)}, bf16[32,128,128]{2,1,0:T(8,128)(2,1)S(1)}) custom-call(bf16[2,8,32,128]{3,2,1,0:T(8,128)(2,1)S(1)} %collective-permute-done.3.refs_0_), custom_call_target="tpu_custom_call" | custom-call | flops 1000000000 | bytes 10000000 | tf_op jit(solution)/shard_map/pallas_call | solution.py:218
  14.3 0.3 collective-permute-done.2.refs_0_
  14.5 0.5 %shard_map.59 = (bf16[32,144,128]{2,1,0:T(8,128)(2,1)S(1)}, bf16[32,128,128]{2,1,0:T(8,128)(2,1)S(1)}) custom-call(bf16[2,8,32,128]{3,2,1,0:T(8,128)(2,1)S(1)} %collective-permute-done.2.refs_0_), custom_call_target="tpu_custom_call" | custom-call | flops 1000000000 | bytes 10000000 | tf_op jit(solution)/shard_map/pallas_call | solution.py:218
  15.1 1.5 %shard_map.60 = bf16[8,4,32,128]{3,2,1,0:T(8,128)(2,1)S(1)} custom-call(bf16[32,144,128]{2,1,0:T(8,128)(2,1)S(1)} %get-tuple-element.24.refs_0_, bf16[32,144,128]{2,1,0:T(8,128)(2,1)S(1)} %get-tuple-element.32.refs_1_, bf16[32,144,128]{2,1,0:T(8,128)(2,1)S(1)} %get-tuple-element.33.refs_2_, bf16[32,144,128]{2,1,0:T(8,128)(2,1)S(1)} %get-tuple-element.34.refs_3_, ...), custom_call_target="tpu_custom_call" | custom-call | tf_op jit(solution)/shard_map/pallas_call | solution.py:227
  16.6 0.0 copy-start
  16.6 0.1 collective-permute-start.4
  16.7 2.6 %collective-permute-start.6 = (bf16[2,4,32,128]{3,2,1,0:T(8,128)(2,1)S(1)}, bf16[2,4,32,128]{3,2,1,0:T(8,128)(2,1)S(1)}, u32[]{:S(2)}, u32[]{:S(2)}) collective-permute-start(bf16[2,4,32,128]{3,2,1,0:T(8,128)(2,1)S(1)} %slice.71), channel_id=1, source_target_pairs={{0,64},{16,80},{32,96},{48,112},{64,0},{80,16},{96,32},{112,48},{1... | collective-permute-start | bytes 196616 | tf_op jit(solution)/shard_map/ppermute | solution.py:182
  19.3 0.0 collective-permute-done.4
  19.4 1.9 %collective-permute-start.8 = (bf16[2,4,32,128]{3,2,1,0:T(8,128)(2,1)S(1)}, bf16[2,4,32,128]{3,2,1,0:T(8,128)(2,1)S(1)}, u32[]{:S(2)}, u32[]{:S(2)}) collective-permute-start(bf16[2,4,32,128]{3,2,1,0:T(8,128)(2,1)S(1)} %get-tuple-element.49), channel_id=1, source_target_pairs={{0,96},{16,112},{32,64},{48,80},{64,32},{80,48},{96,0},{112,16},{1... | collective-permute-start | bytes 196616 | tf_op jit(solution)/shard_map/ppermute | solution.py:182
  21.2 0.0 collective-permute-start.5
  21.2 1.5 %collective-permute-done.6 = bf16[2,4,32,128]{3,2,1,0:T(8,128)(2,1)S(1)} collective-permute-done((bf16[2,4,32,128]{3,2,1,0:T(8,128)(2,1)S(1)}, bf16[2,4,32,128]{3,2,1,0:T(8,128)(2,1)S(1)}, u32[]{:S(2)}, u32[]{:S(2)}) %collective-permute-start.6) | collective-permute-done | bytes 65568 | tf_op jit(solution)/shard_map/ppermute | solution.py:182
  22.7 0.0 collective-permute-start.7
  22.7 1.2 %collective-permute-done.7.refs_3_ = bf16[4,32,128]{2,1,0:T(8,128)(2,1)S(1)} collective-permute-done((bf16[4,32,128]{2,1,0:T(8,128)(2,1)S(1)}, bf16[4,32,128]{2,1,0:T(8,128)(2,1)S(1)}, u32[]{:S(2)}, u32[]{:S(2)}) %collective-permute-start.7) | collective-permute-done | bytes 32800 | tf_op jit(solution)/shard_map/ppermute | solution.py:182
  23.9 1.0 %collective-permute-done.8.refs_4_ = bf16[2,4,32,128]{3,2,1,0:T(8,128)(2,1)S(1)} collective-permute-done((bf16[2,4,32,128]{3,2,1,0:T(8,128)(2,1)S(1)}, bf16[2,4,32,128]{3,2,1,0:T(8,128)(2,1)S(1)}, u32[]{:S(2)}, u32[]{:S(2)}) %collective-permute-start.8) | collective-permute-done | bytes 65568 | tf_op jit(solution)/shard_map/ppermute | solution.py:182
  24.9 0.6 %collective-permute-done.5.refs_1_ = bf16[2,4,32,128]{3,2,1,0:T(8,128)(2,1)S(1)} collective-permute-done((bf16[2,4,32,128]{3,2,1,0:T(8,128)(2,1)S(1)}, bf16[2,4,32,128]{3,2,1,0:T(8,128)(2,1)S(1)}, u32[]{:S(2)}, u32[]{:S(2)}) %collective-permute-start.5) | collective-permute-done | bytes 65568 | tf_op jit(solution)/shard_map/ppermute | solution.py:182
  25.5 0.0 copy-done
  25.5 0.9 %shard_map.61 = bf16[512,256]{1,0:T(8,128)(2,1)} custom-call(bf16[2,4,32,128]{3,2,1,0:T(8,128)(2,1)S(1)} %get-tuple-element.50.refs_0_, bf16[2,4,32,128]{3,2,1,0:T(8,128)(2,1)S(1)} %collective-permute-done.5.refs_1_, bf16[4,32,128]{2,1,0:T(8,128)(2,1)S(1)} %get-tuple-element.53.refs_2_, bf16[4,32,128]{2,1,0:T(8,128)(2,1)S(1)} %collective-permute-done.7.refs_3_, ...), custom_call_target="tpu_custom_call" | custom-call | tf_op jit(solution)/shard_map/pallas_call | solution.py:236
  (6 shorter events, 0.1 us)
Async XLA Ops:
  0.0 1.2 %copy-start.1 = (bf16[512,256]{1,0:T(8,128)(2,1)S(1)}, bf16[512,256]{1,0:T(8,128)(2,1)}, u32[]{:S(2)}) copy-start(bf16[512,256]{1,0:T(8,128)(2,1)} %f_ref.1) | copy-start | bytes 786436
  1.5 1.6 %collective-permute-start = (bf16[4,8,32,128]{3,2,1,0:T(8,128)(2,1)S(1)}, bf16[4,8,32,128]{3,2,1,0:T(8,128)(2,1)S(1)}, u32[]{:S(2)}, u32[]{:S(2)}) collective-permute-start(bf16[4,8,32,128]{3,2,1,0:T(8,128)(2,1)S(1)} %get-tuple-element.45), channel_id=1, source_target_pairs={{0,16},{16,0},{32,48},{48,32},{64,80},{80,64},{96,112},{112,96},{1... | collective-permute-start | bytes 786440 | tf_op jit(solution)/shard_map/ppermute | solution.py:182
  3.1 7.9 %collective-permute-start.1 = (bf16[2,8,32,128]{3,2,1,0:T(8,128)(2,1)S(1)}, bf16[2,8,32,128]{3,2,1,0:T(8,128)(2,1)S(1)}, u32[]{:S(2)}, u32[]{:S(2)}) collective-permute-start(bf16[2,8,32,128]{3,2,1,0:T(8,128)(2,1)S(1)} %get-tuple-element.42), channel_id=1, source_target_pairs={{0,64},{16,80},{32,96},{48,112},{64,0},{80,16},{96,32},{112,48},{1... | collective-permute-start | bytes 393224 | tf_op jit(solution)/shard_map/ppermute | solution.py:182
  7.2 6.6 %collective-permute-start.3 = (bf16[2,8,32,128]{3,2,1,0:T(8,128)(2,1)S(1)}, bf16[2,8,32,128]{3,2,1,0:T(8,128)(2,1)S(1)}, u32[]{:S(2)}, u32[]{:S(2)}) collective-permute-start(bf16[2,8,32,128]{3,2,1,0:T(8,128)(2,1)S(1)} %get-tuple-element.41), channel_id=1, source_target_pairs={{0,96},{16,112},{32,64},{48,80},{64,32},{80,48},{96,0},{112,16},{1... | collective-permute-start | bytes 393224 | tf_op jit(solution)/shard_map/ppermute | solution.py:182
  7.9 6.7 %collective-permute-start.2 = (bf16[2,8,32,128]{3,2,1,0:T(8,128)(2,1)S(1)}, bf16[2,8,32,128]{3,2,1,0:T(8,128)(2,1)S(1)}, u32[]{:S(2)}, u32[]{:S(2)}) collective-permute-start(bf16[2,8,32,128]{3,2,1,0:T(8,128)(2,1)S(1)} %get-tuple-element.44), channel_id=1, source_target_pairs={{0,32},{16,48},{32,0},{48,16},{64,96},{80,112},{96,64},{112,80},{1... | collective-permute-start | bytes 393224 | tf_op jit(solution)/shard_map/ppermute | solution.py:182
  16.6 8.9 %copy-start = (bf16[512,256]{1,0:T(8,128)(2,1)S(1)}, bf16[512,256]{1,0:T(8,128)(2,1)}, u32[]{:S(2)}) copy-start(bf16[512,256]{1,0:T(8,128)(2,1)} %refs_6_.1) | copy-start | bytes 786436
  16.6 2.7 %collective-permute-start.4 = (bf16[3,4,32,128]{3,2,1,0:T(8,128)(2,1)S(1)}, bf16[3,4,32,128]{3,2,1,0:T(8,128)(2,1)S(1)}, u32[]{:S(2)}, u32[]{:S(2)}) collective-permute-start(bf16[3,4,32,128]{3,2,1,0:T(8,128)(2,1)S(1)} %get-tuple-element.47), channel_id=1, source_target_pairs={{0,16},{16,0},{32,48},{48,32},{64,80},{80,64},{96,112},{112,96},{1... | collective-permute-start | bytes 294920 | tf_op jit(solution)/shard_map/ppermute | solution.py:182
  16.7 6.0 %collective-permute-start.6 = (bf16[2,4,32,128]{3,2,1,0:T(8,128)(2,1)S(1)}, bf16[2,4,32,128]{3,2,1,0:T(8,128)(2,1)S(1)}, u32[]{:S(2)}, u32[]{:S(2)}) collective-permute-start(bf16[2,4,32,128]{3,2,1,0:T(8,128)(2,1)S(1)} %slice.71), channel_id=1, source_target_pairs={{0,64},{16,80},{32,96},{48,112},{64,0},{80,16},{96,32},{112,48},{1... | collective-permute-start | bytes 196616 | tf_op jit(solution)/shard_map/ppermute | solution.py:182
  19.4 5.6 %collective-permute-start.8 = (bf16[2,4,32,128]{3,2,1,0:T(8,128)(2,1)S(1)}, bf16[2,4,32,128]{3,2,1,0:T(8,128)(2,1)S(1)}, u32[]{:S(2)}, u32[]{:S(2)}) collective-permute-start(bf16[2,4,32,128]{3,2,1,0:T(8,128)(2,1)S(1)} %get-tuple-element.49), channel_id=1, source_target_pairs={{0,96},{16,112},{32,64},{48,80},{64,32},{80,48},{96,0},{112,16},{1... | collective-permute-start | bytes 196616 | tf_op jit(solution)/shard_map/ppermute | solution.py:182
  21.2 4.3 %collective-permute-start.5 = (bf16[2,4,32,128]{3,2,1,0:T(8,128)(2,1)S(1)}, bf16[2,4,32,128]{3,2,1,0:T(8,128)(2,1)S(1)}, u32[]{:S(2)}, u32[]{:S(2)}) collective-permute-start(bf16[2,4,32,128]{3,2,1,0:T(8,128)(2,1)S(1)} %get-tuple-element.51), channel_id=1, source_target_pairs={{0,32},{16,48},{32,0},{48,16},{64,96},{80,112},{96,64},{112,80},{1... | collective-permute-start | bytes 196616 | tf_op jit(solution)/shard_map/ppermute | solution.py:182
  22.7 1.2 %collective-permute-start.7 = (bf16[4,32,128]{2,1,0:T(8,128)(2,1)S(1)}, bf16[4,32,128]{2,1,0:T(8,128)(2,1)S(1)}, u32[]{:S(2)}, u32[]{:S(2)}) collective-permute-start(bf16[4,32,128]{2,1,0:T(8,128)(2,1)S(1)} %get-tuple-element.52), channel_id=1, source_target_pairs={{0,16},{16,0},{32,48},{48,32},{64,80},{80,64},{96,112},{112,96},{1... | collective-permute-start | bytes 98312 | tf_op jit(solution)/shard_map/ppermute | solution.py:182

commit v8 on v7

--- a/solution.py
+++ b/solution.py
@@ -32,7 +32,7 @@
                 block = x[128 * q : 128 * q + 128, 128 * half : 128 * half + 128]
                 block = block.T.astype(BF16).reshape(4, CH, 128)
                 for t in range(4):
-                    o_s[lax.bitwise_xor(me, 4 * half + t), at + q] = block[t]
+                    o_s[slot_of(lax.bitwise_xor(me, 4 * half + t)), at + q] = block[t]
 
 
 def both(refs):
@@ -184,12 +184,6 @@
 
 def exchange(x):
     x = x.reshape(4, 2, *x.shape[1:])
-    pairs = jnp.stack([x[:, 0], swap(x[:, 1], 1)], 1)
-    return [(pairs[0],)] + [(swap(pairs[i], 2 * i),) for i in range(1, 4)]
-
-
-def exchange_far_first(x):
-    x = x.reshape(4, 2, *x.shape[1:])
     far = swap(x[0], 4)
     other = swap(x[1:, 1], 1)
     near = jnp.stack([x[1:, 0], other], 1)
@@ -211,7 +205,7 @@
     )
     pairs = exchange(sent)
     tiles = [None] * 4
-    for last, i in ((None, 0), (0, 2), (2, 3), (3, 1)):
+    for last, i in ((None, 0), (0, 3), (3, 1), (1, 2)):
         pair = pairs[i]
         if last is not None:
             pair, tiles[last] = lax.optimization_barrier((pair, tiles[last]))
@@ -222,7 +216,7 @@
                 jax.ShapeDtypeStruct((CH, 128, 128), BF16),
             ],
             [pltpu.VMEM((8 * CH, 128), F32)] * 2,
-            cost_estimate=pl.CostEstimate(flops=10**9, bytes_accessed=10**7, transcendentals=0),
+            cost_estimate=pl.CostEstimate(flops=10**8, bytes_accessed=3 * 10**6, transcendentals=0),
         )(*pair)
     mixed = call(
         conv_kernel,
@@ -232,7 +226,7 @@
             pltpu.VMEM((32 * PITCH, 128), F32),
         ],
     )(*[t for t, _ in tiles], *[w for _, w in tiles])
-    back = exchange_far_first(mixed)
+    back = exchange(mixed)
     return call(
         gate_kernel,
         jax.ShapeDtypeStruct((512, 256), BF16),

time: 26.5 us -> 25.8 us (0.974)
  waiting for transfers between devices: 10.6 us -> 9.29 us
  starting transfers between devices: 9.73 us -> 10.3 us
    ppermute x9 -> x10, waiting for transfers between devices: 10.6 us -> 9.29 us  [swap(): return lax.ppermute(x, 'seq', [(i, i ^ j) for i in range(PARTS)])]
    ppermute x9 -> x10, starting transfers between devices: 9.73 us -> 10.3 us  [swap(): return lax.ppermute(x, 'seq', [(i, i ^ j) for i in range(PARTS)])]
  transfers between devices with their start and end apart: 9 -> 10, of which waited for: 8 -> 6; matrix products, arithmetic and copies ran while one was open for 0% -> 0% of each run, Pallas kernels for 6% -> 6%
where the time goes in v8:
time: 25.8 us; the launch traced here: 25.7 us
  starting transfers between devices  10.3 us (40%)
  waiting for transfers between devices  9.29 us (36%)
  Pallas kernels  4.62 us (18%)
  other arithmetic  1.22 us (5%)
    ppermute x10, starting transfers between devices, swap(): return lax.ppermute(x, 'seq', [(i, i ^ j) for i in range(PARTS)])  10.3 us
    ppermute x10, waiting for transfers between devices, swap(): return lax.ppermute(x, 'seq', [(i, i ^ j) for i in range(PARTS)])  9.29 us
    pallas_call x4, Pallas kernels, on_device(): call(spread_kernel, [jax.ShapeDtypeStruct((CH, 144, 128), BF16), jax.Shap...  2.07 us
    pallas_call x1, Pallas kernels, on_device(): call(conv_kernel, jax.ShapeDtypeStruct((PARTS, 4, CH, 128), BF16), [pltpu...  1.47 us
    mul x1, other arithmetic, on_device(): direct = skip_gain[None, :] * product  1.17 us
    pallas_call x1, Pallas kernels, on_device(): call(gate_kernel, jax.ShapeDtypeStruct((512, 256), BF16), [pltpu.VMEM((PA...  0.86 us
  transfers between devices with their start and end apart: 10, of which 6 were waited for; matrix products, arithmetic and copies ran while one was open for 0% of the time, Pallas kernels for 6%

profile of v8, /device:TPU:0, one launch (start us, length us, event | category | flops | bytes accessed | tf_op | source)
XLA Modules:
  0.0 25.7 jit_solution(3967508532059885963)
XLA Ops:
  0.0 0.0 copy-start.1
  0.0 1.2 %fusion = (f32[512,256]{1,0:T(8,128)S(1)}, bf16[512,256]{1,0:T(8,128)(2,1)S(1)}) fusion(bf16[512,256]{1,0:T(8,128)(2,1)} %param.6, bf16[512,256]{1,0:T(8,128)(2,1)} %param.5, f32[256]{0:T(256)} %param.9), kind=kLoop, calls=%fused_computation.1 | loop fusion | flops 786432 | bytes 1311744 | tf_op jit(solution)/shard_map/mul | solution.py:201
  1.2 0.0 copy-done.1
  1.2 0.2 shard_map.55
  1.4 0.1 collective-permute-start
  1.6 4.0 %collective-permute-start.2 = (bf16[2,8,32,128]{3,2,1,0:T(8,128)(2,1)S(1)}, bf16[2,8,32,128]{3,2,1,0:T(8,128)(2,1)S(1)}, u32[]{:S(2)}, u32[]{:S(2)}) collective-permute-start(bf16[2,8,32,128]{3,2,1,0:T(8,128)(2,1)S(1)} %slice.72), channel_id=1, source_target_pairs={{0,64},{16,80},{32,96},{48,112},{64,0},{80,16},{96,32},{112,48},{1... | collective-permute-start | bytes 393224 | tf_op jit(solution)/shard_map/ppermute | solution.py:182
  5.6 0.0 collective-permute-done
  5.6 1.1 %collective-permute-start.4 = (bf16[2,8,32,128]{3,2,1,0:T(8,128)(2,1)S(1)}, bf16[2,8,32,128]{3,2,1,0:T(8,128)(2,1)S(1)}, u32[]{:S(2)}, u32[]{:S(2)}) collective-permute-start(bf16[2,8,32,128]{3,2,1,0:T(8,128)(2,1)S(1)} %get-tuple-element.45), channel_id=1, source_target_pairs={{0,32},{16,48},{32,0},{48,16},{64,96},{80,112},{96,64},{112,80},{1... | collective-permute-start | bytes 393224 | tf_op jit(solution)/shard_map/ppermute | solution.py:182
  6.7 0.9 %collective-permute-start.1 = (bf16[2,8,32,128]{3,2,1,0:T(8,128)(2,1)S(1)}, bf16[2,8,32,128]{3,2,1,0:T(8,128)(2,1)S(1)}, u32[]{:S(2)}, u32[]{:S(2)}) collective-permute-start(bf16[2,8,32,128]{3,2,1,0:T(8,128)(2,1)S(1)} %get-tuple-element.46), channel_id=1, source_target_pairs={{0,96},{16,112},{32,64},{48,80},{64,32},{80,48},{96,0},{112,16},{1... | collective-permute-start | bytes 393224 | tf_op jit(solution)/shard_map/ppermute | solution.py:182
  7.6 2.3 %collective-permute-done.2 = bf16[2,8,32,128]{3,2,1,0:T(8,128)(2,1)S(1)} collective-permute-done((bf16[2,8,32,128]{3,2,1,0:T(8,128)(2,1)S(1)}, bf16[2,8,32,128]{3,2,1,0:T(8,128)(2,1)S(1)}, u32[]{:S(2)}, u32[]{:S(2)}) %collective-permute-start.2) | collective-permute-done | bytes 131104 | tf_op jit(solution)/shard_map/ppermute | solution.py:182
  10.0 0.1 collective-permute-start.3
  10.1 0.5 %shard_map.56 = (bf16[32,144,128]{2,1,0:T(8,128)(2,1)S(1)}, bf16[32,128,128]{2,1,0:T(8,128)(2,1)S(1)}) custom-call(bf16[2,8,32,128]{3,2,1,0:T(8,128)(2,1)S(1)} %get-tuple-element.47.refs_0_), custom_call_target="tpu_custom_call" | custom-call | flops 100000000 | bytes 3000000 | tf_op jit(solution)/shard_map/pallas_call | solution.py:212
  10.6 2.7 %collective-permute-done.1.refs_0_ = bf16[2,8,32,128]{3,2,1,0:T(8,128)(2,1)S(1)} collective-permute-done((bf16[2,8,32,128]{3,2,1,0:T(8,128)(2,1)S(1)}, bf16[2,8,32,128]{3,2,1,0:T(8,128)(2,1)S(1)}, u32[]{:S(2)}, u32[]{:S(2)}) %collective-permute-start.1) | collective-permute-done | bytes 131104 | tf_op jit(solution)/shard_map/ppermute | solution.py:182
  13.3 0.5 %shard_map.57 = (bf16[32,144,128]{2,1,0:T(8,128)(2,1)S(1)}, bf16[32,128,128]{2,1,0:T(8,128)(2,1)S(1)}) custom-call(bf16[2,8,32,128]{3,2,1,0:T(8,128)(2,1)S(1)} %collective-permute-done.1.refs_0_), custom_call_target="tpu_custom_call" | custom-call | flops 100000000 | bytes 3000000 | tf_op jit(solution)/shard_map/pallas_call | solution.py:212
  13.8 0.0 collective-permute-done.4.refs_0_
  13.8 0.5 %shard_map.58 = (bf16[32,144,128]{2,1,0:T(8,128)(2,1)S(1)}, bf16[32,128,128]{2,1,0:T(8,128)(2,1)S(1)}) custom-call(bf16[2,8,32,128]{3,2,1,0:T(8,128)(2,1)S(1)} %collective-permute-done.4.refs_0_), custom_call_target="tpu_custom_call" | custom-call | flops 100000000 | bytes 3000000 | tf_op jit(solution)/shard_map/pallas_call | solution.py:212
  14.3 0.0 collective-permute-done.3.refs_1_
  14.4 0.5 %shard_map.59 = (bf16[32,144,128]{2,1,0:T(8,128)(2,1)S(1)}, bf16[32,128,128]{2,1,0:T(8,128)(2,1)S(1)}) custom-call(bf16[8,32,128]{2,1,0:T(8,128)(2,1)S(1)} %get-tuple-element.33.refs_0_, bf16[8,32,128]{2,1,0:T(8,128)(2,1)S(1)} %collective-permute-done.3.refs_1_), custom_call_target="tpu_custom_call" | custom-call | flops 100000000 | bytes 3000000 | tf_op jit(solution)/shard_map/pallas_call | solution.py:212
  14.9 1.5 %shard_map.60 = bf16[8,4,32,128]{3,2,1,0:T(8,128)(2,1)S(1)} custom-call(bf16[32,144,128]{2,1,0:T(8,128)(2,1)S(1)} %get-tuple-element.25.refs_0_, bf16[32,144,128]{2,1,0:T(8,128)(2,1)S(1)} %get-tuple-element.32.refs_1_, bf16[32,144,128]{2,1,0:T(8,128)(2,1)S(1)} %get-tuple-element.35.refs_2_, bf16[32,144,128]{2,1,0:T(8,128)(2,1)S(1)} %get-tuple-element.36.refs_3_, ...), custom_call_target="tpu_custom_call" | custom-call | tf_op jit(solution)/shard_map/pallas_call | solution.py:221
  16.4 0.0 copy-start
  16.4 0.1 collective-permute-start.5
  16.5 2.6 %collective-permute-start.7 = (bf16[2,4,32,128]{3,2,1,0:T(8,128)(2,1)S(1)}, bf16[2,4,32,128]{3,2,1,0:T(8,128)(2,1)S(1)}, u32[]{:S(2)}, u32[]{:S(2)}) collective-permute-start(bf16[2,4,32,128]{3,2,1,0:T(8,128)(2,1)S(1)} %slice.81), channel_id=1, source_target_pairs={{0,64},{16,80},{32,96},{48,112},{64,0},{80,16},{96,32},{112,48},{1... | collective-permute-start | bytes 196616 | tf_op jit(solution)/shard_map/ppermute | solution.py:182
  19.1 0.0 collective-permute-done.5
  19.1 1.4 %collective-permute-start.9 = (bf16[2,4,32,128]{3,2,1,0:T(8,128)(2,1)S(1)}, bf16[2,4,32,128]{3,2,1,0:T(8,128)(2,1)S(1)}, u32[]{:S(2)}, u32[]{:S(2)}) collective-permute-start(bf16[2,4,32,128]{3,2,1,0:T(8,128)(2,1)S(1)} %get-tuple-element.50), channel_id=1, source_target_pairs={{0,96},{16,112},{32,64},{48,80},{64,32},{80,48},{96,0},{112,16},{1... | collective-permute-start | bytes 196616 | tf_op jit(solution)/shard_map/ppermute | solution.py:182
  20.6 0.0 collective-permute-start.6
  20.6 1.9 %collective-permute-done.7 = bf16[2,4,32,128]{3,2,1,0:T(8,128)(2,1)S(1)} collective-permute-done((bf16[2,4,32,128]{3,2,1,0:T(8,128)(2,1)S(1)}, bf16[2,4,32,128]{3,2,1,0:T(8,128)(2,1)S(1)}, u32[]{:S(2)}, u32[]{:S(2)}) %collective-permute-start.7) | collective-permute-done | bytes 65568 | tf_op jit(solution)/shard_map/ppermute | solution.py:182
  22.5 0.0 collective-permute-start.8
  22.5 1.2 %collective-permute-done.8.refs_3_ = bf16[4,32,128]{2,1,0:T(8,128)(2,1)S(1)} collective-permute-done((bf16[4,32,128]{2,1,0:T(8,128)(2,1)S(1)}, bf16[4,32,128]{2,1,0:T(8,128)(2,1)S(1)}, u32[]{:S(2)}, u32[]{:S(2)}) %collective-permute-start.8) | collective-permute-done | bytes 32800 | tf_op jit(solution)/shard_map/ppermute | solution.py:182
  23.7 1.0 %collective-permute-done.9.refs_4_ = bf16[2,4,32,128]{3,2,1,0:T(8,128)(2,1)S(1)} collective-permute-done((bf16[2,4,32,128]{3,2,1,0:T(8,128)(2,1)S(1)}, bf16[2,4,32,128]{3,2,1,0:T(8,128)(2,1)S(1)}, u32[]{:S(2)}, u32[]{:S(2)}) %collective-permute-start.9) | collective-permute-done | bytes 65568 | tf_op jit(solution)/shard_map/ppermute | solution.py:182
  24.7 0.1 collective-permute-done.6.refs_1_
  24.8 0.0 copy-done
  24.8 0.9 %shard_map.61 = bf16[512,256]{1,0:T(8,128)(2,1)} custom-call(bf16[2,4,32,128]{3,2,1,0:T(8,128)(2,1)S(1)} %get-tuple-element.51.refs_0_, bf16[2,4,32,128]{3,2,1,0:T(8,128)(2,1)S(1)} %collective-permute-done.6.refs_1_, bf16[4,32,128]{2,1,0:T(8,128)(2,1)S(1)} %get-tuple-element.56.refs_2_, bf16[4,32,128]{2,1,0:T(8,128)(2,1)S(1)} %collective-permute-done.8.refs_3_, ...), custom_call_target="tpu_custom_call" | custom-call | tf_op jit(solution)/shard_map/pallas_call | solution.py:230
  (8 shorter events, 0.1 us)
Async XLA Ops:
  0.0 1.2 %copy-start.1 = (bf16[512,256]{1,0:T(8,128)(2,1)S(1)}, bf16[512,256]{1,0:T(8,128)(2,1)}, u32[]{:S(2)}) copy-start(bf16[512,256]{1,0:T(8,128)(2,1)} %f_ref.1) | copy-start | bytes 786436
  1.4 4.2 %collective-permute-start = (bf16[3,8,32,128]{3,2,1,0:T(8,128)(2,1)S(1)}, bf16[3,8,32,128]{3,2,1,0:T(8,128)(2,1)S(1)}, u32[]{:S(2)}, u32[]{:S(2)}) collective-permute-start(bf16[3,8,32,128]{3,2,1,0:T(8,128)(2,1)S(1)} %get-tuple-element.43), channel_id=1, source_target_pairs={{0,16},{16,0},{32,48},{48,32},{64,80},{80,64},{96,112},{112,96},{1... | collective-permute-start | bytes 589832 | tf_op jit(solution)/shard_map/ppermute | solution.py:182
  1.6 8.4 %collective-permute-start.2 = (bf16[2,8,32,128]{3,2,1,0:T(8,128)(2,1)S(1)}, bf16[2,8,32,128]{3,2,1,0:T(8,128)(2,1)S(1)}, u32[]{:S(2)}, u32[]{:S(2)}) collective-permute-start(bf16[2,8,32,128]{3,2,1,0:T(8,128)(2,1)S(1)} %slice.72), channel_id=1, source_target_pairs={{0,64},{16,80},{32,96},{48,112},{64,0},{80,16},{96,32},{112,48},{1... | collective-permute-start | bytes 393224 | tf_op jit(solution)/shard_map/ppermute | solution.py:182
  5.6 8.2 %collective-permute-start.4 = (bf16[2,8,32,128]{3,2,1,0:T(8,128)(2,1)S(1)}, bf16[2,8,32,128]{3,2,1,0:T(8,128)(2,1)S(1)}, u32[]{:S(2)}, u32[]{:S(2)}) collective-permute-start(bf16[2,8,32,128]{3,2,1,0:T(8,128)(2,1)S(1)} %get-tuple-element.45), channel_id=1, source_target_pairs={{0,32},{16,48},{32,0},{48,16},{64,96},{80,112},{96,64},{112,80},{1... | collective-permute-start | bytes 393224 | tf_op jit(solution)/shard_map/ppermute | solution.py:182
  6.7 6.5 %collective-permute-start.1 = (bf16[2,8,32,128]{3,2,1,0:T(8,128)(2,1)S(1)}, bf16[2,8,32,128]{3,2,1,0:T(8,128)(2,1)S(1)}, u32[]{:S(2)}, u32[]{:S(2)}) collective-permute-start(bf16[2,8,32,128]{3,2,1,0:T(8,128)(2,1)S(1)} %get-tuple-element.46), channel_id=1, source_target_pairs={{0,96},{16,112},{32,64},{48,80},{64,32},{80,48},{96,0},{112,16},{1... | collective-permute-start | bytes 393224 | tf_op jit(solution)/shard_map/ppermute | solution.py:182
  10.0 4.4 %collective-permute-start.3 = (bf16[8,32,128]{2,1,0:T(8,128)(2,1)S(1)}, bf16[8,32,128]{2,1,0:T(8,128)(2,1)S(1)}, u32[]{:S(2)}, u32[]{:S(2)}) collective-permute-start(bf16[8,32,128]{2,1,0:T(8,128)(2,1)S(1)} %get-tuple-element.53), channel_id=1, source_target_pairs={{0,16},{16,0},{32,48},{48,32},{64,80},{80,64},{96,112},{112,96},{1... | collective-permute-start | bytes 196616 | tf_op jit(solution)/shard_map/ppermute | solution.py:182
  16.4 8.5 %copy-start = (bf16[512,256]{1,0:T(8,128)(2,1)S(1)}, bf16[512,256]{1,0:T(8,128)(2,1)}, u32[]{:S(2)}) copy-start(bf16[512,256]{1,0:T(8,128)(2,1)} %refs_6_.1) | copy-start | bytes 786436
  16.4 2.7 %collective-permute-start.5 = (bf16[3,4,32,128]{3,2,1,0:T(8,128)(2,1)S(1)}, bf16[3,4,32,128]{3,2,1,0:T(8,128)(2,1)S(1)}, u32[]{:S(2)}, u32[]{:S(2)}) collective-permute-start(bf16[3,4,32,128]{3,2,1,0:T(8,128)(2,1)S(1)} %get-tuple-element.48), channel_id=1, source_target_pairs={{0,16},{16,0},{32,48},{48,32},{64,80},{80,64},{96,112},{112,96},{1... | collective-permute-start | bytes 294920 | tf_op jit(solution)/shard_map/ppermute | solution.py:182
  16.5 6.0 %collective-permute-start.7 = (bf16[2,4,32,128]{3,2,1,0:T(8,128)(2,1)S(1)}, bf16[2,4,32,128]{3,2,1,0:T(8,128)(2,1)S(1)}, u32[]{:S(2)}, u32[]{:S(2)}) collective-permute-start(bf16[2,4,32,128]{3,2,1,0:T(8,128)(2,1)S(1)} %slice.81), channel_id=1, source_target_pairs={{0,64},{16,80},{32,96},{48,112},{64,0},{80,16},{96,32},{112,48},{1... | collective-permute-start | bytes 196616 | tf_op jit(solution)/shard_map/ppermute | solution.py:182
  19.1 5.6 %collective-permute-start.9 = (bf16[2,4,32,128]{3,2,1,0:T(8,128)(2,1)S(1)}, bf16[2,4,32,128]{3,2,1,0:T(8,128)(2,1)S(1)}, u32[]{:S(2)}, u32[]{:S(2)}) collective-permute-start(bf16[2,4,32,128]{3,2,1,0:T(8,128)(2,1)S(1)} %get-tuple-element.50), channel_id=1, source_target_pairs={{0,96},{16,112},{32,64},{48,80},{64,32},{80,48},{96,0},{112,16},{1... | collective-permute-start | bytes 196616 | tf_op jit(solution)/shard_map/ppermute | solution.py:182
  20.6 4.3 %collective-permute-start.6 = (bf16[2,4,32,128]{3,2,1,0:T(8,128)(2,1)S(1)}, bf16[2,4,32,128]{3,2,1,0:T(8,128)(2,1)S(1)}, u32[]{:S(2)}, u32[]{:S(2)}) collective-permute-start(bf16[2,4,32,128]{3,2,1,0:T(8,128)(2,1)S(1)} %get-tuple-element.52), channel_id=1, source_target_pairs={{0,32},{16,48},{32,0},{48,16},{64,96},{80,112},{96,64},{112,80},{1... | collective-permute-start | bytes 196616 | tf_op jit(solution)/shard_map/ppermute | solution.py:182
  22.5 1.2 %collective-permute-start.8 = (bf16[4,32,128]{2,1,0:T(8,128)(2,1)S(1)}, bf16[4,32,128]{2,1,0:T(8,128)(2,1)S(1)}, u32[]{:S(2)}, u32[]{:S(2)}) collective-permute-start(bf16[4,32,128]{2,1,0:T(8,128)(2,1)S(1)} %get-tuple-element.55), channel_id=1, source_target_pairs={{0,16},{16,0},{32,48},{48,32},{64,80},{80,64},{96,112},{112,96},{1... | collective-permute-start | bytes 98312 | tf_op jit(solution)/shard_map/ppermute | solution.py:182

commit v9 on v8

--- a/solution.py
+++ b/solution.py
@@ -205,7 +205,7 @@
     )
     pairs = exchange(sent)
     tiles = [None] * 4
-    for last, i in ((None, 0), (0, 3), (3, 1), (1, 2)):
+    for last, i in ((None, 0), (0, 2), (2, 3), (3, 1)):
         pair = pairs[i]
         if last is not None:
             pair, tiles[last] = lax.optimization_barrier((pair, tiles[last]))

time: 25.8 us -> 25.3 us (0.981)
  waiting for transfers between devices: 9.29 us -> 8.67 us
    ppermute x10, waiting for transfers between devices: 9.29 us -> 8.67 us  [swap(): return lax.ppermute(x, 'seq', [(i, i ^ j) for i in range(PARTS)])]
  transfers between devices with their start and end apart: 10 -> 10, of which waited for: 6 -> 8; matrix products, arithmetic and copies ran while one was open for 0% -> 0% of each run, Pallas kernels for 6% -> 6%
where the time goes in v9:
time: 25.3 us; the launch traced here: 25.2 us
  starting transfers between devices  10.4 us (41%)
  waiting for transfers between devices  8.67 us (34%)
  Pallas kernels  4.61 us (18%)
  other arithmetic  1.22 us (5%)
    ppermute x10, starting transfers between devices, swap(): return lax.ppermute(x, 'seq', [(i, i ^ j) for i in range(PARTS)])  10.4 us
    ppermute x10, waiting for transfers between devices, swap(): return lax.ppermute(x, 'seq', [(i, i ^ j) for i in range(PARTS)])  8.67 us
    pallas_call x4, Pallas kernels, on_device(): call(spread_kernel, [jax.ShapeDtypeStruct((CH, 144, 128), BF16), jax.Shap...  2.06 us
    pallas_call x1, Pallas kernels, on_device(): call(conv_kernel, jax.ShapeDtypeStruct((PARTS, 4, CH, 128), BF16), [pltpu...  1.47 us
    mul x1, other arithmetic, on_device(): direct = skip_gain[None, :] * product  1.17 us
    pallas_call x1, Pallas kernels, on_device(): call(gate_kernel, jax.ShapeDtypeStruct((512, 256), BF16), [pltpu.VMEM((PA...  0.86 us
  transfers between devices with their start and end apart: 10, of which 8 were waited for; matrix products, arithmetic and copies ran while one was open for 0% of the time, Pallas kernels for 6%

profile of v9, /device:TPU:0, one launch (start us, length us, event | category | flops | bytes accessed | tf_op | source)
XLA Modules:
  0.0 25.2 jit_solution(3341532775308653285)
XLA Ops:
  0.0 0.0 copy-start.1
  0.0 1.2 %fusion = (f32[512,256]{1,0:T(8,128)S(1)}, bf16[512,256]{1,0:T(8,128)(2,1)S(1)}) fusion(bf16[512,256]{1,0:T(8,128)(2,1)} %param.6, bf16[512,256]{1,0:T(8,128)(2,1)} %param.5, f32[256]{0:T(256)} %param.9), kind=kLoop, calls=%fused_computation.1 | loop fusion | flops 786432 | bytes 1311744 | tf_op jit(solution)/shard_map/mul | solution.py:201
  1.2 0.0 copy-done.1
  1.2 0.2 shard_map.55
  1.4 0.1 collective-permute-start.2
  1.6 4.0 %collective-permute-start = (bf16[2,8,32,128]{3,2,1,0:T(8,128)(2,1)S(1)}, bf16[2,8,32,128]{3,2,1,0:T(8,128)(2,1)S(1)}, u32[]{:S(2)}, u32[]{:S(2)}) collective-permute-start(bf16[2,8,32,128]{3,2,1,0:T(8,128)(2,1)S(1)} %slice.66), channel_id=1, source_target_pairs={{0,64},{16,80},{32,96},{48,112},{64,0},{80,16},{96,32},{112,48},{1... | collective-permute-start | bytes 393224 | tf_op jit(solution)/shard_map/ppermute | solution.py:182
  5.6 0.0 collective-permute-done.2
  5.6 1.6 %collective-permute-start.4 = (bf16[2,8,32,128]{3,2,1,0:T(8,128)(2,1)S(1)}, bf16[2,8,32,128]{3,2,1,0:T(8,128)(2,1)S(1)}, u32[]{:S(2)}, u32[]{:S(2)}) collective-permute-start(bf16[2,8,32,128]{3,2,1,0:T(8,128)(2,1)S(1)} %get-tuple-element.45), channel_id=1, source_target_pairs={{0,96},{16,112},{32,64},{48,80},{64,32},{80,48},{96,0},{112,16},{1... | collective-permute-start | bytes 393224 | tf_op jit(solution)/shard_map/ppermute | solution.py:182
  7.2 0.0 collective-permute-start.3
  7.2 2.5 %collective-permute-done = bf16[2,8,32,128]{3,2,1,0:T(8,128)(2,1)S(1)} collective-permute-done((bf16[2,8,32,128]{3,2,1,0:T(8,128)(2,1)S(1)}, bf16[2,8,32,128]{3,2,1,0:T(8,128)(2,1)S(1)}, u32[]{:S(2)}, u32[]{:S(2)}) %collective-permute-start) | collective-permute-done | bytes 131104 | tf_op jit(solution)/shard_map/ppermute | solution.py:182
  9.8 0.1 collective-permute-start.1
  9.9 0.5 %shard_map.56 = (bf16[32,144,128]{2,1,0:T(8,128)(2,1)S(1)}, bf16[32,128,128]{2,1,0:T(8,128)(2,1)S(1)}) custom-call(bf16[2,8,32,128]{3,2,1,0:T(8,128)(2,1)S(1)} %get-tuple-element.46.refs_0_), custom_call_target="tpu_custom_call" | custom-call | flops 100000000 | bytes 3000000 | tf_op jit(solution)/shard_map/pallas_call | solution.py:212
  10.4 0.7 %collective-permute-done.1.refs_1_ = bf16[8,32,128]{2,1,0:T(8,128)(2,1)S(1)} collective-permute-done((bf16[8,32,128]{2,1,0:T(8,128)(2,1)S(1)}, bf16[8,32,128]{2,1,0:T(8,128)(2,1)S(1)}, u32[]{:S(2)}, u32[]{:S(2)}) %collective-permute-start.1) | collective-permute-done | bytes 65568 | tf_op jit(solution)/shard_map/ppermute | solution.py:182
  11.1 0.5 %shard_map.57 = (bf16[32,144,128]{2,1,0:T(8,128)(2,1)S(1)}, bf16[32,128,128]{2,1,0:T(8,128)(2,1)S(1)}) custom-call(bf16[8,32,128]{2,1,0:T(8,128)(2,1)S(1)} %get-tuple-element.26.refs_0_, bf16[8,32,128]{2,1,0:T(8,128)(2,1)S(1)} %collective-permute-done.1.refs_1_), custom_call_target="tpu_custom_call" | custom-call | flops 100000000 | bytes 3000000 | tf_op jit(solution)/shard_map/pallas_call | solution.py:212
  11.6 0.9 %collective-permute-done.4.refs_0_ = bf16[2,8,32,128]{3,2,1,0:T(8,128)(2,1)S(1)} collective-permute-done((bf16[2,8,32,128]{3,2,1,0:T(8,128)(2,1)S(1)}, bf16[2,8,32,128]{3,2,1,0:T(8,128)(2,1)S(1)}, u32[]{:S(2)}, u32[]{:S(2)}) %collective-permute-start.4) | collective-permute-done | bytes 131104 | tf_op jit(solution)/shard_map/ppermute | solution.py:182
  12.6 0.5 %shard_map.58 = (bf16[32,144,128]{2,1,0:T(8,128)(2,1)S(1)}, bf16[32,128,128]{2,1,0:T(8,128)(2,1)S(1)}) custom-call(bf16[2,8,32,128]{3,2,1,0:T(8,128)(2,1)S(1)} %collective-permute-done.4.refs_0_), custom_call_target="tpu_custom_call" | custom-call | flops 100000000 | bytes 3000000 | tf_op jit(solution)/shard_map/pallas_call | solution.py:212
  13.1 0.2 collective-permute-done.3.refs_0_
  13.3 0.5 %shard_map.59 = (bf16[32,144,128]{2,1,0:T(8,128)(2,1)S(1)}, bf16[32,128,128]{2,1,0:T(8,128)(2,1)S(1)}) custom-call(bf16[2,8,32,128]{3,2,1,0:T(8,128)(2,1)S(1)} %collective-permute-done.3.refs_0_), custom_call_target="tpu_custom_call" | custom-call | flops 100000000 | bytes 3000000 | tf_op jit(solution)/shard_map/pallas_call | solution.py:212
  13.8 1.5 %shard_map.60 = bf16[8,4,32,128]{3,2,1,0:T(8,128)(2,1)S(1)} custom-call(bf16[32,144,128]{2,1,0:T(8,128)(2,1)S(1)} %get-tuple-element.25.refs_0_, bf16[32,144,128]{2,1,0:T(8,128)(2,1)S(1)} %get-tuple-element.34.refs_1_, bf16[32,144,128]{2,1,0:T(8,128)(2,1)S(1)} %get-tuple-element.35.refs_2_, bf16[32,144,128]{2,1,0:T(8,128)(2,1)S(1)} %get-tuple-element.36.refs_3_, ...), custom_call_target="tpu_custom_call" | custom-call | tf_op jit(solution)/shard_map/pallas_call | solution.py:221
  15.3 0.0 copy-start
  15.3 0.1 collective-permute-start.5
  15.4 2.8 %collective-permute-start.7 = (bf16[2,4,32,128]{3,2,1,0:T(8,128)(2,1)S(1)}, bf16[2,4,32,128]{3,2,1,0:T(8,128)(2,1)S(1)}, u32[]{:S(2)}, u32[]{:S(2)}) collective-permute-start(bf16[2,4,32,128]{3,2,1,0:T(8,128)(2,1)S(1)} %slice.81), channel_id=1, source_target_pairs={{0,64},{16,80},{32,96},{48,112},{64,0},{80,16},{96,32},{112,48},{1... | collective-permute-start | bytes 196616 | tf_op jit(solution)/shard_map/ppermute | solution.py:182
  18.2 0.0 collective-permute-done.5
  18.3 1.7 %collective-permute-start.9 = (bf16[2,4,32,128]{3,2,1,0:T(8,128)(2,1)S(1)}, bf16[2,4,32,128]{3,2,1,0:T(8,128)(2,1)S(1)}, u32[]{:S(2)}, u32[]{:S(2)}) collective-permute-start(bf16[2,4,32,128]{3,2,1,0:T(8,128)(2,1)S(1)} %get-tuple-element.50), channel_id=1, source_target_pairs={{0,96},{16,112},{32,64},{48,80},{64,32},{80,48},{96,0},{112,16},{1... | collective-permute-start | bytes 196616 | tf_op jit(solution)/shard_map/ppermute | solution.py:182
  20.0 0.0 collective-permute-start.6
  20.0 1.4 %collective-permute-done.7 = bf16[2,4,32,128]{3,2,1,0:T(8,128)(2,1)S(1)} collective-permute-done((bf16[2,4,32,128]{3,2,1,0:T(8,128)(2,1)S(1)}, bf16[2,4,32,128]{3,2,1,0:T(8,128)(2,1)S(1)}, u32[]{:S(2)}, u32[]{:S(2)}) %collective-permute-start.7) | collective-permute-done | bytes 65568 | tf_op jit(solution)/shard_map/ppermute | solution.py:182
  21.5 0.0 collective-permute-start.8
  21.5 1.2 %collective-permute-done.8.refs_3_ = bf16[4,32,128]{2,1,0:T(8,128)(2,1)S(1)} collective-permute-done((bf16[4,32,128]{2,1,0:T(8,128)(2,1)S(1)}, bf16[4,32,128]{2,1,0:T(8,128)(2,1)S(1)}, u32[]{:S(2)}, u32[]{:S(2)}) %collective-permute-start.8) | collective-permute-done | bytes 32800 | tf_op jit(solution)/shard_map/ppermute | solution.py:182
  22.7 1.2 %collective-permute-done.9.refs_4_ = bf16[2,4,32,128]{3,2,1,0:T(8,128)(2,1)S(1)} collective-permute-done((bf16[2,4,32,128]{3,2,1,0:T(8,128)(2,1)S(1)}, bf16[2,4,32,128]{3,2,1,0:T(8,128)(2,1)S(1)}, u32[]{:S(2)}, u32[]{:S(2)}) %collective-permute-start.9) | collective-permute-done | bytes 65568 | tf_op jit(solution)/shard_map/ppermute | solution.py:182
  23.8 0.5 %collective-permute-done.6.refs_1_ = bf16[2,4,32,128]{3,2,1,0:T(8,128)(2,1)S(1)} collective-permute-done((bf16[2,4,32,128]{3,2,1,0:T(8,128)(2,1)S(1)}, bf16[2,4,32,128]{3,2,1,0:T(8,128)(2,1)S(1)}, u32[]{:S(2)}, u32[]{:S(2)}) %collective-permute-start.6) | collective-permute-done | bytes 65568 | tf_op jit(solution)/shard_map/ppermute | solution.py:182
  24.3 0.0 copy-done
  24.3 0.9 %shard_map.61 = bf16[512,256]{1,0:T(8,128)(2,1)} custom-call(bf16[2,4,32,128]{3,2,1,0:T(8,128)(2,1)S(1)} %get-tuple-element.51.refs_0_, bf16[2,4,32,128]{3,2,1,0:T(8,128)(2,1)S(1)} %collective-permute-done.6.refs_1_, bf16[4,32,128]{2,1,0:T(8,128)(2,1)S(1)} %get-tuple-element.56.refs_2_, bf16[4,32,128]{2,1,0:T(8,128)(2,1)S(1)} %collective-permute-done.8.refs_3_, ...), custom_call_target="tpu_custom_call" | custom-call | tf_op jit(solution)/shard_map/pallas_call | solution.py:230
  (8 shorter events, 0.1 us)
Async XLA Ops:
  0.0 1.2 %copy-start.1 = (bf16[512,256]{1,0:T(8,128)(2,1)S(1)}, bf16[512,256]{1,0:T(8,128)(2,1)}, u32[]{:S(2)}) copy-start(bf16[512,256]{1,0:T(8,128)(2,1)} %f_ref.1) | copy-start | bytes 786436
  1.4 4.2 %collective-permute-start.2 = (bf16[3,8,32,128]{3,2,1,0:T(8,128)(2,1)S(1)}, bf16[3,8,32,128]{3,2,1,0:T(8,128)(2,1)S(1)}, u32[]{:S(2)}, u32[]{:S(2)}) collective-permute-start(bf16[3,8,32,128]{3,2,1,0:T(8,128)(2,1)S(1)} %get-tuple-element.43), channel_id=1, source_target_pairs={{0,16},{16,0},{32,48},{48,32},{64,80},{80,64},{96,112},{112,96},{1... | collective-permute-start | bytes 589832 | tf_op jit(solution)/shard_map/ppermute | solution.py:182
  1.6 8.2 %collective-permute-start = (bf16[2,8,32,128]{3,2,1,0:T(8,128)(2,1)S(1)}, bf16[2,8,32,128]{3,2,1,0:T(8,128)(2,1)S(1)}, u32[]{:S(2)}, u32[]{:S(2)}) collective-permute-start(bf16[2,8,32,128]{3,2,1,0:T(8,128)(2,1)S(1)} %slice.66), channel_id=1, source_target_pairs={{0,64},{16,80},{32,96},{48,112},{64,0},{80,16},{96,32},{112,48},{1... | collective-permute-start | bytes 393224 | tf_op jit(solution)/shard_map/ppermute | solution.py:182
  5.6 6.9 %collective-permute-start.4 = (bf16[2,8,32,128]{3,2,1,0:T(8,128)(2,1)S(1)}, bf16[2,8,32,128]{3,2,1,0:T(8,128)(2,1)S(1)}, u32[]{:S(2)}, u32[]{:S(2)}) collective-permute-start(bf16[2,8,32,128]{3,2,1,0:T(8,128)(2,1)S(1)} %get-tuple-element.45), channel_id=1, source_target_pairs={{0,96},{16,112},{32,64},{48,80},{64,32},{80,48},{96,0},{112,16},{1... | collective-permute-start | bytes 393224 | tf_op jit(solution)/shard_map/ppermute | solution.py:182
  7.2 6.1 %collective-permute-start.3 = (bf16[2,8,32,128]{3,2,1,0:T(8,128)(2,1)S(1)}, bf16[2,8,32,128]{3,2,1,0:T(8,128)(2,1)S(1)}, u32[]{:S(2)}, u32[]{:S(2)}) collective-permute-start(bf16[2,8,32,128]{3,2,1,0:T(8,128)(2,1)S(1)} %get-tuple-element.47), channel_id=1, source_target_pairs={{0,32},{16,48},{32,0},{48,16},{64,96},{80,112},{96,64},{112,80},{1... | collective-permute-start | bytes 393224 | tf_op jit(solution)/shard_map/ppermute | solution.py:182
  9.8 1.3 %collective-permute-start.1 = (bf16[8,32,128]{2,1,0:T(8,128)(2,1)S(1)}, bf16[8,32,128]{2,1,0:T(8,128)(2,1)S(1)}, u32[]{:S(2)}, u32[]{:S(2)}) collective-permute-start(bf16[8,32,128]{2,1,0:T(8,128)(2,1)S(1)} %get-tuple-element.53), channel_id=1, source_target_pairs={{0,16},{16,0},{32,48},{48,32},{64,80},{80,64},{96,112},{112,96},{1... | collective-permute-start | bytes 196616 | tf_op jit(solution)/shard_map/ppermute | solution.py:182
  15.3 9.0 %copy-start = (bf16[512,256]{1,0:T(8,128)(2,1)S(1)}, bf16[512,256]{1,0:T(8,128)(2,1)}, u32[]{:S(2)}) copy-start(bf16[512,256]{1,0:T(8,128)(2,1)} %refs_6_.1) | copy-start | bytes 786436
  15.3 2.9 %collective-permute-start.5 = (bf16[3,4,32,128]{3,2,1,0:T(8,128)(2,1)S(1)}, bf16[3,4,32,128]{3,2,1,0:T(8,128)(2,1)S(1)}, u32[]{:S(2)}, u32[]{:S(2)}) collective-permute-start(bf16[3,4,32,128]{3,2,1,0:T(8,128)(2,1)S(1)} %get-tuple-element.48), channel_id=1, source_target_pairs={{0,16},{16,0},{32,48},{48,32},{64,80},{80,64},{96,112},{112,96},{1... | collective-permute-start | bytes 294920 | tf_op jit(solution)/shard_map/ppermute | solution.py:182
  15.4 6.0 %collective-permute-start.7 = (bf16[2,4,32,128]{3,2,1,0:T(8,128)(2,1)S(1)}, bf16[2,4,32,128]{3,2,1,0:T(8,128)(2,1)S(1)}, u32[]{:S(2)}, u32[]{:S(2)}) collective-permute-start(bf16[2,4,32,128]{3,2,1,0:T(8,128)(2,1)S(1)} %slice.81), channel_id=1, source_target_pairs={{0,64},{16,80},{32,96},{48,112},{64,0},{80,16},{96,32},{112,48},{1... | collective-permute-start | bytes 196616 | tf_op jit(solution)/shard_map/ppermute | solution.py:182
  18.3 5.6 %collective-permute-start.9 = (bf16[2,4,32,128]{3,2,1,0:T(8,128)(2,1)S(1)}, bf16[2,4,32,128]{3,2,1,0:T(8,128)(2,1)S(1)}, u32[]{:S(2)}, u32[]{:S(2)}) collective-permute-start(bf16[2,4,32,128]{3,2,1,0:T(8,128)(2,1)S(1)} %get-tuple-element.50), channel_id=1, source_target_pairs={{0,96},{16,112},{32,64},{48,80},{64,32},{80,48},{96,0},{112,16},{1... | collective-permute-start | bytes 196616 | tf_op jit(solution)/shard_map/ppermute | solution.py:182
  20.0 4.3 %collective-permute-start.6 = (bf16[2,4,32,128]{3,2,1,0:T(8,128)(2,1)S(1)}, bf16[2,4,32,128]{3,2,1,0:T(8,128)(2,1)S(1)}, u32[]{:S(2)}, u32[]{:S(2)}) collective-permute-start(bf16[2,4,32,128]{3,2,1,0:T(8,128)(2,1)S(1)} %get-tuple-element.52), channel_id=1, source_target_pairs={{0,32},{16,48},{32,0},{48,16},{64,96},{80,112},{96,64},{112,80},{1... | collective-permute-start | bytes 196616 | tf_op jit(solution)/shard_map/ppermute | solution.py:182
  21.5 1.2 %collective-permute-start.8 = (bf16[4,32,128]{2,1,0:T(8,128)(2,1)S(1)}, bf16[4,32,128]{2,1,0:T(8,128)(2,1)S(1)}, u32[]{:S(2)}, u32[]{:S(2)}) collective-permute-start(bf16[4,32,128]{2,1,0:T(8,128)(2,1)S(1)} %get-tuple-element.55), channel_id=1, source_target_pairs={{0,16},{16,0},{32,48},{48,32},{64,80},{80,64},{96,112},{112,96},{1... | collective-permute-start | bytes 98312 | tf_op jit(solution)/shard_map/ppermute | solution.py:182

commit v10 on v9

--- a/solution.py
+++ b/solution.py
@@ -205,7 +205,7 @@
     )
     pairs = exchange(sent)
     tiles = [None] * 4
-    for last, i in ((None, 0), (0, 2), (2, 3), (3, 1)):
+    for last, i in ((None, 0), (0, 2), (2, 1), (1, 3)):
         pair = pairs[i]
         if last is not None:
             pair, tiles[last] = lax.optimization_barrier((pair, tiles[last]))

time: 25.3 us -> 25.3 us (level)
  starting transfers between devices: 10.4 us -> 10.1 us
    ppermute x10, starting transfers between devices: 10.4 us -> 10.1 us  [swap(): return lax.ppermute(x, 'seq', [(i, i ^ j) for i in range(PARTS)])]
  transfers between devices with their start and end apart: 10 -> 10, of which waited for: 8 -> 7; matrix products, arithmetic and copies ran while one was open for 0% -> 0% of each run, Pallas kernels for 6% -> 6%
where the time goes in v10:
time: 25.3 us; the launch traced here: 25 us
  starting transfers between devices  10.1 us (40%)
  waiting for transfers between devices  8.78 us (35%)
  Pallas kernels  4.62 us (18%)
  other arithmetic  1.22 us (5%)
    ppermute x10, starting transfers between devices, swap(): return lax.ppermute(x, 'seq', [(i, i ^ j) for i in range(PARTS)])  10.1 us
    ppermute x10, waiting for transfers between devices, swap(): return lax.ppermute(x, 'seq', [(i, i ^ j) for i in range(PARTS)])  8.78 us
    pallas_call x4, Pallas kernels, on_device(): call(spread_kernel, [jax.ShapeDtypeStruct((CH, 144, 128), BF16), jax.Shap...  2.06 us
    pallas_call x1, Pallas kernels, on_device(): call(conv_kernel, jax.ShapeDtypeStruct((PARTS, 4, CH, 128), BF16), [pltpu...  1.48 us
    mul x1, other arithmetic, on_device(): direct = skip_gain[None, :] * product  1.17 us
    pallas_call x1, Pallas kernels, on_device(): call(gate_kernel, jax.ShapeDtypeStruct((512, 256), BF16), [pltpu.VMEM((PA...  0.86 us
  transfers between devices with their start and end apart: 10, of which 7 were waited for; matrix products, arithmetic and copies ran while one was open for 0% of the time, Pallas kernels for 6%

profile of v10, /device:TPU:0, one launch (start us, length us, event | category | flops | bytes accessed | tf_op | source)
XLA Modules:
  0.0 25.0 jit_solution(16861165604627199104)
XLA Ops:
  0.0 0.0 copy-start.1
  0.0 1.2 %fusion = (f32[512,256]{1,0:T(8,128)S(1)}, bf16[512,256]{1,0:T(8,128)(2,1)S(1)}) fusion(bf16[512,256]{1,0:T(8,128)(2,1)} %param.6, bf16[512,256]{1,0:T(8,128)(2,1)} %param.5, f32[256]{0:T(256)} %param.9), kind=kLoop, calls=%fused_computation.1 | loop fusion | flops 786432 | bytes 1311744 | tf_op jit(solution)/shard_map/mul | solution.py:201
  1.2 0.0 copy-done.1
  1.2 0.2 shard_map.55
  1.4 0.1 collective-permute-start.2
  1.6 4.0 %collective-permute-start = (bf16[2,8,32,128]{3,2,1,0:T(8,128)(2,1)S(1)}, bf16[2,8,32,128]{3,2,1,0:T(8,128)(2,1)S(1)}, u32[]{:S(2)}, u32[]{:S(2)}) collective-permute-start(bf16[2,8,32,128]{3,2,1,0:T(8,128)(2,1)S(1)} %slice.66), channel_id=1, source_target_pairs={{0,64},{16,80},{32,96},{48,112},{64,0},{80,16},{96,32},{112,48},{1... | collective-permute-start | bytes 393224 | tf_op jit(solution)/shard_map/ppermute | solution.py:182
  5.6 0.0 collective-permute-done.2
  5.6 1.1 %collective-permute-start.4 = (bf16[2,8,32,128]{3,2,1,0:T(8,128)(2,1)S(1)}, bf16[2,8,32,128]{3,2,1,0:T(8,128)(2,1)S(1)}, u32[]{:S(2)}, u32[]{:S(2)}) collective-permute-start(bf16[2,8,32,128]{3,2,1,0:T(8,128)(2,1)S(1)} %get-tuple-element.45), channel_id=1, source_target_pairs={{0,32},{16,48},{32,0},{48,16},{64,96},{80,112},{96,64},{112,80},{1... | collective-permute-start | bytes 393224 | tf_op jit(solution)/shard_map/ppermute | solution.py:182
  6.7 0.9 %collective-permute-start.3 = (bf16[2,8,32,128]{3,2,1,0:T(8,128)(2,1)S(1)}, bf16[2,8,32,128]{3,2,1,0:T(8,128)(2,1)S(1)}, u32[]{:S(2)}, u32[]{:S(2)}) collective-permute-start(bf16[2,8,32,128]{3,2,1,0:T(8,128)(2,1)S(1)} %get-tuple-element.47), channel_id=1, source_target_pairs={{0,96},{16,112},{32,64},{48,80},{64,32},{80,48},{96,0},{112,16},{1... | collective-permute-start | bytes 393224 | tf_op jit(solution)/shard_map/ppermute | solution.py:182
  7.6 2.3 %collective-permute-done = bf16[2,8,32,128]{3,2,1,0:T(8,128)(2,1)S(1)} collective-permute-done((bf16[2,8,32,128]{3,2,1,0:T(8,128)(2,1)S(1)}, bf16[2,8,32,128]{3,2,1,0:T(8,128)(2,1)S(1)}, u32[]{:S(2)}, u32[]{:S(2)}) %collective-permute-start) | collective-permute-done | bytes 131104 | tf_op jit(solution)/shard_map/ppermute | solution.py:182
  10.0 0.1 collective-permute-start.1
  10.1 0.5 %shard_map.56 = (bf16[32,144,128]{2,1,0:T(8,128)(2,1)S(1)}, bf16[32,128,128]{2,1,0:T(8,128)(2,1)S(1)}) custom-call(bf16[2,8,32,128]{3,2,1,0:T(8,128)(2,1)S(1)} %get-tuple-element.46.refs_0_), custom_call_target="tpu_custom_call" | custom-call | flops 100000000 | bytes 3000000 | tf_op jit(solution)/shard_map/pallas_call | solution.py:212
  10.6 0.7 %collective-permute-done.1.refs_1_ = bf16[8,32,128]{2,1,0:T(8,128)(2,1)S(1)} collective-permute-done((bf16[8,32,128]{2,1,0:T(8,128)(2,1)S(1)}, bf16[8,32,128]{2,1,0:T(8,128)(2,1)S(1)}, u32[]{:S(2)}, u32[]{:S(2)}) %collective-permute-start.1) | collective-permute-done | bytes 65568 | tf_op jit(solution)/shard_map/ppermute | solution.py:182
  11.3 0.5 %shard_map.57 = (bf16[32,144,128]{2,1,0:T(8,128)(2,1)S(1)}, bf16[32,128,128]{2,1,0:T(8,128)(2,1)S(1)}) custom-call(bf16[8,32,128]{2,1,0:T(8,128)(2,1)S(1)} %get-tuple-element.26.refs_0_, bf16[8,32,128]{2,1,0:T(8,128)(2,1)S(1)} %collective-permute-done.1.refs_1_), custom_call_target="tpu_custom_call" | custom-call | flops 100000000 | bytes 3000000 | tf_op jit(solution)/shard_map/pallas_call | solution.py:212
  11.8 1.5 %collective-permute-done.4.refs_0_ = bf16[2,8,32,128]{3,2,1,0:T(8,128)(2,1)S(1)} collective-permute-done((bf16[2,8,32,128]{3,2,1,0:T(8,128)(2,1)S(1)}, bf16[2,8,32,128]{3,2,1,0:T(8,128)(2,1)S(1)}, u32[]{:S(2)}, u32[]{:S(2)}) %collective-permute-start.4) | collective-permute-done | bytes 131104 | tf_op jit(solution)/shard_map/ppermute | solution.py:182
  13.3 0.5 %shard_map.58 = (bf16[32,144,128]{2,1,0:T(8,128)(2,1)S(1)}, bf16[32,128,128]{2,1,0:T(8,128)(2,1)S(1)}) custom-call(bf16[2,8,32,128]{3,2,1,0:T(8,128)(2,1)S(1)} %collective-permute-done.4.refs_0_), custom_call_target="tpu_custom_call" | custom-call | flops 100000000 | bytes 3000000 | tf_op jit(solution)/shard_map/pallas_call | solution.py:212
  13.8 0.0 collective-permute-done.3.refs_0_
  13.8 0.5 %shard_map.59 = (bf16[32,144,128]{2,1,0:T(8,128)(2,1)S(1)}, bf16[32,128,128]{2,1,0:T(8,128)(2,1)S(1)}) custom-call(bf16[2,8,32,128]{3,2,1,0:T(8,128)(2,1)S(1)} %collective-permute-done.3.refs_0_), custom_call_target="tpu_custom_call" | custom-call | flops 100000000 | bytes 3000000 | tf_op jit(solution)/shard_map/pallas_call | solution.py:212
  14.4 1.5 %shard_map.60 = bf16[8,4,32,128]{3,2,1,0:T(8,128)(2,1)S(1)} custom-call(bf16[32,144,128]{2,1,0:T(8,128)(2,1)S(1)} %get-tuple-element.25.refs_0_, bf16[32,144,128]{2,1,0:T(8,128)(2,1)S(1)} %get-tuple-element.33.refs_1_, bf16[32,144,128]{2,1,0:T(8,128)(2,1)S(1)} %get-tuple-element.34.refs_2_, bf16[32,144,128]{2,1,0:T(8,128)(2,1)S(1)} %get-tuple-element.36.refs_3_, ...), custom_call_target="tpu_custom_call" | custom-call | tf_op jit(solution)/shard_map/pallas_call | solution.py:221
  15.8 0.0 copy-start
  15.9 0.1 collective-permute-start.5
  16.0 2.1 %collective-permute-start.7 = (bf16[2,4,32,128]{3,2,1,0:T(8,128)(2,1)S(1)}, bf16[2,4,32,128]{3,2,1,0:T(8,128)(2,1)S(1)}, u32[]{:S(2)}, u32[]{:S(2)}) collective-permute-start(bf16[2,4,32,128]{3,2,1,0:T(8,128)(2,1)S(1)} %slice.81), channel_id=1, source_target_pairs={{0,64},{16,80},{32,96},{48,112},{64,0},{80,16},{96,32},{112,48},{1... | collective-permute-start | bytes 196616 | tf_op jit(solution)/shard_map/ppermute | solution.py:182
  18.1 0.0 collective-permute-done.5
  18.1 1.7 %collective-permute-start.9 = (bf16[2,4,32,128]{3,2,1,0:T(8,128)(2,1)S(1)}, bf16[2,4,32,128]{3,2,1,0:T(8,128)(2,1)S(1)}, u32[]{:S(2)}, u32[]{:S(2)}) collective-permute-start(bf16[2,4,32,128]{3,2,1,0:T(8,128)(2,1)S(1)} %get-tuple-element.50), channel_id=1, source_target_pairs={{0,96},{16,112},{32,64},{48,80},{64,32},{80,48},{96,0},{112,16},{1... | collective-permute-start | bytes 196616 | tf_op jit(solution)/shard_map/ppermute | solution.py:182
  19.8 0.0 collective-permute-start.6
  19.8 2.2 %collective-permute-done.7 = bf16[2,4,32,128]{3,2,1,0:T(8,128)(2,1)S(1)} collective-permute-done((bf16[2,4,32,128]{3,2,1,0:T(8,128)(2,1)S(1)}, bf16[2,4,32,128]{3,2,1,0:T(8,128)(2,1)S(1)}, u32[]{:S(2)}, u32[]{:S(2)}) %collective-permute-start.7) | collective-permute-done | bytes 65568 | tf_op jit(solution)/shard_map/ppermute | solution.py:182
  22.0 0.0 collective-permute-start.8
  22.0 1.2 %collective-permute-done.8.refs_3_ = bf16[4,32,128]{2,1,0:T(8,128)(2,1)S(1)} collective-permute-done((bf16[4,32,128]{2,1,0:T(8,128)(2,1)S(1)}, bf16[4,32,128]{2,1,0:T(8,128)(2,1)S(1)}, u32[]{:S(2)}, u32[]{:S(2)}) %collective-permute-start.8) | collective-permute-done | bytes 32800 | tf_op jit(solution)/shard_map/ppermute | solution.py:182
  23.2 0.5 %collective-permute-done.9.refs_4_ = bf16[2,4,32,128]{3,2,1,0:T(8,128)(2,1)S(1)} collective-permute-done((bf16[2,4,32,128]{3,2,1,0:T(8,128)(2,1)S(1)}, bf16[2,4,32,128]{3,2,1,0:T(8,128)(2,1)S(1)}, u32[]{:S(2)}, u32[]{:S(2)}) %collective-permute-start.9) | collective-permute-done | bytes 65568 | tf_op jit(solution)/shard_map/ppermute | solution.py:182
  23.7 0.4 %collective-permute-done.6.refs_1_ = bf16[2,4,32,128]{3,2,1,0:T(8,128)(2,1)S(1)} collective-permute-done((bf16[2,4,32,128]{3,2,1,0:T(8,128)(2,1)S(1)}, bf16[2,4,32,128]{3,2,1,0:T(8,128)(2,1)S(1)}, u32[]{:S(2)}, u32[]{:S(2)}) %collective-permute-start.6) | collective-permute-done | bytes 65568 | tf_op jit(solution)/shard_map/ppermute | solution.py:182
  24.1 0.0 copy-done
  24.1 0.9 %shard_map.61 = bf16[512,256]{1,0:T(8,128)(2,1)} custom-call(bf16[2,4,32,128]{3,2,1,0:T(8,128)(2,1)S(1)} %get-tuple-element.51.refs_0_, bf16[2,4,32,128]{3,2,1,0:T(8,128)(2,1)S(1)} %collective-permute-done.6.refs_1_, bf16[4,32,128]{2,1,0:T(8,128)(2,1)S(1)} %get-tuple-element.56.refs_2_, bf16[4,32,128]{2,1,0:T(8,128)(2,1)S(1)} %collective-permute-done.8.refs_3_, ...), custom_call_target="tpu_custom_call" | custom-call | tf_op jit(solution)/shard_map/pallas_call | solution.py:230
  (8 shorter events, 0.1 us)
Async XLA Ops:
  0.0 1.2 %copy-start.1 = (bf16[512,256]{1,0:T(8,128)(2,1)S(1)}, bf16[512,256]{1,0:T(8,128)(2,1)}, u32[]{:S(2)}) copy-start(bf16[512,256]{1,0:T(8,128)(2,1)} %f_ref.1) | copy-start | bytes 786436
  1.4 4.2 %collective-permute-start.2 = (bf16[3,8,32,128]{3,2,1,0:T(8,128)(2,1)S(1)}, bf16[3,8,32,128]{3,2,1,0:T(8,128)(2,1)S(1)}, u32[]{:S(2)}, u32[]{:S(2)}) collective-permute-start(bf16[3,8,32,128]{3,2,1,0:T(8,128)(2,1)S(1)} %get-tuple-element.43), channel_id=1, source_target_pairs={{0,16},{16,0},{32,48},{48,32},{64,80},{80,64},{96,112},{112,96},{1... | collective-permute-start | bytes 589832 | tf_op jit(solution)/shard_map/ppermute | solution.py:182
  1.6 8.4 %collective-permute-start = (bf16[2,8,32,128]{3,2,1,0:T(8,128)(2,1)S(1)}, bf16[2,8,32,128]{3,2,1,0:T(8,128)(2,1)S(1)}, u32[]{:S(2)}, u32[]{:S(2)}) collective-permute-start(bf16[2,8,32,128]{3,2,1,0:T(8,128)(2,1)S(1)} %slice.66), channel_id=1, source_target_pairs={{0,64},{16,80},{32,96},{48,112},{64,0},{80,16},{96,32},{112,48},{1... | collective-permute-start | bytes 393224 | tf_op jit(solution)/shard_map/ppermute | solution.py:182
  5.6 7.7 %collective-permute-start.4 = (bf16[2,8,32,128]{3,2,1,0:T(8,128)(2,1)S(1)}, bf16[2,8,32,128]{3,2,1,0:T(8,128)(2,1)S(1)}, u32[]{:S(2)}, u32[]{:S(2)}) collective-permute-start(bf16[2,8,32,128]{3,2,1,0:T(8,128)(2,1)S(1)} %get-tuple-element.45), channel_id=1, source_target_pairs={{0,32},{16,48},{32,0},{48,16},{64,96},{80,112},{96,64},{112,80},{1... | collective-permute-start | bytes 393224 | tf_op jit(solution)/shard_map/ppermute | solution.py:182
  6.7 7.1 %collective-permute-start.3 = (bf16[2,8,32,128]{3,2,1,0:T(8,128)(2,1)S(1)}, bf16[2,8,32,128]{3,2,1,0:T(8,128)(2,1)S(1)}, u32[]{:S(2)}, u32[]{:S(2)}) collective-permute-start(bf16[2,8,32,128]{3,2,1,0:T(8,128)(2,1)S(1)} %get-tuple-element.47), channel_id=1, source_target_pairs={{0,96},{16,112},{32,64},{48,80},{64,32},{80,48},{96,0},{112,16},{1... | collective-permute-start | bytes 393224 | tf_op jit(solution)/shard_map/ppermute | solution.py:182
  10.0 1.3 %collective-permute-start.1 = (bf16[8,32,128]{2,1,0:T(8,128)(2,1)S(1)}, bf16[8,32,128]{2,1,0:T(8,128)(2,1)S(1)}, u32[]{:S(2)}, u32[]{:S(2)}) collective-permute-start(bf16[8,32,128]{2,1,0:T(8,128)(2,1)S(1)} %get-tuple-element.53), channel_id=1, source_target_pairs={{0,16},{16,0},{32,48},{48,32},{64,80},{80,64},{96,112},{112,96},{1... | collective-permute-start | bytes 196616 | tf_op jit(solution)/shard_map/ppermute | solution.py:182
  15.8 8.3 %copy-start = (bf16[512,256]{1,0:T(8,128)(2,1)S(1)}, bf16[512,256]{1,0:T(8,128)(2,1)}, u32[]{:S(2)}) copy-start(bf16[512,256]{1,0:T(8,128)(2,1)} %refs_6_.1) | copy-start | bytes 786436
  15.9 2.2 %collective-permute-start.5 = (bf16[3,4,32,128]{3,2,1,0:T(8,128)(2,1)S(1)}, bf16[3,4,32,128]{3,2,1,0:T(8,128)(2,1)S(1)}, u32[]{:S(2)}, u32[]{:S(2)}) collective-permute-start(bf16[3,4,32,128]{3,2,1,0:T(8,128)(2,1)S(1)} %get-tuple-element.48), channel_id=1, source_target_pairs={{0,16},{16,0},{32,48},{48,32},{64,80},{80,64},{96,112},{112,96},{1... | collective-permute-start | bytes 294920 | tf_op jit(solution)/shard_map/ppermute | solution.py:182
  16.0 6.0 %collective-permute-start.7 = (bf16[2,4,32,128]{3,2,1,0:T(8,128)(2,1)S(1)}, bf16[2,4,32,128]{3,2,1,0:T(8,128)(2,1)S(1)}, u32[]{:S(2)}, u32[]{:S(2)}) collective-permute-start(bf16[2,4,32,128]{3,2,1,0:T(8,128)(2,1)S(1)} %slice.81), channel_id=1, source_target_pairs={{0,64},{16,80},{32,96},{48,112},{64,0},{80,16},{96,32},{112,48},{1... | collective-permute-start | bytes 196616 | tf_op jit(solution)/shard_map/ppermute | solution.py:182
  18.1 5.6 %collective-permute-start.9 = (bf16[2,4,32,128]{3,2,1,0:T(8,128)(2,1)S(1)}, bf16[2,4,32,128]{3,2,1,0:T(8,128)(2,1)S(1)}, u32[]{:S(2)}, u32[]{:S(2)}) collective-permute-start(bf16[2,4,32,128]{3,2,1,0:T(8,128)(2,1)S(1)} %get-tuple-element.50), channel_id=1, source_target_pairs={{0,96},{16,112},{32,64},{48,80},{64,32},{80,48},{96,0},{112,16},{1... | collective-permute-start | bytes 196616 | tf_op jit(solution)/shard_map/ppermute | solution.py:182
  19.8 4.3 %collective-permute-start.6 = (bf16[2,4,32,128]{3,2,1,0:T(8,128)(2,1)S(1)}, bf16[2,4,32,128]{3,2,1,0:T(8,128)(2,1)S(1)}, u32[]{:S(2)}, u32[]{:S(2)}) collective-permute-start(bf16[2,4,32,128]{3,2,1,0:T(8,128)(2,1)S(1)} %get-tuple-element.52), channel_id=1, source_target_pairs={{0,32},{16,48},{32,0},{48,16},{64,96},{80,112},{96,64},{112,80},{1... | collective-permute-start | bytes 196616 | tf_op jit(solution)/shard_map/ppermute | solution.py:182
  22.0 1.2 %collective-permute-start.8 = (bf16[4,32,128]{2,1,0:T(8,128)(2,1)S(1)}, bf16[4,32,128]{2,1,0:T(8,128)(2,1)S(1)}, u32[]{:S(2)}, u32[]{:S(2)}) collective-permute-start(bf16[4,32,128]{2,1,0:T(8,128)(2,1)S(1)} %get-tuple-element.55), channel_id=1, source_target_pairs={{0,16},{16,0},{32,48},{48,32},{64,80},{80,64},{96,112},{112,96},{1... | collective-permute-start | bytes 98312 | tf_op jit(solution)/shard_map/ppermute | solution.py:182
